TPU v7x, 512 devices: a whole 4x4x16 slice. The times are simulated.
512 devices in a mesh: tm: 32 (over z, core), row: 16 (over y, x).
Axes of the slice: x: 4, y: 4, z: 16, core: 2. Of those that a mesh axis runs over, the one named last changes fastest.
Arguments:
- lower_factor: bfloat16 [64, 1024, 1024], P('tm', 'row'), may hold values from -0.1875 to 0.1875
- arrow_factor: bfloat16 [64, 1024, 512], P('tm', 'row'), may hold values from -0.25 to 0.25
- block_inverse: bfloat16 [64, 1024, 1024], P('tm', 'row'), as said below
- boundary_sigma: bfloat16 [32, 1024, 1024], P('tm', 'row'), as said below
- boundary_tip: bfloat16 [32, 1024, 512], P('tm', 'row'), may hold values from -3 to 3
- tip_inverse: bfloat16 [512, 512], replicated, as said below
- slope_weights: float32 [64, 1024], P('tm', 'row'), may hold values from 0.1 to 1
Outputs:
- sigma_diag: float32 [64, 1024, 1024], P('tm', 'row')
- sigma_lower: float32 [64, 1024, 1024], P('tm', 'row')
- sigma_tip: float32 [64, 1024, 512], P('tm', 'row')
- logdet_slope: float32 [], replicated
Inputs may be any that keep to these rules, and one draw needn't show every extreme that they name: `block_inverse`: each block is symmetric with a diagonal part of order one. `boundary_sigma`: each block is symmetric with a diagonal part of order one. `tip_inverse`: symmetric with a diagonal part of order one.
All inputs are finite; a program needn't handle non-finite values.
Results may differ from a plain program's by a relative error of at most 0.0041.
Values may be sent and summed in bfloat16 or wider, within the bound.
No kernel may reach another device: no remote copies, remote signals or barrier semaphores. Data moves between devices by JAX's collectives and lax.ppermute only.
A program may use at most 64 MiB of HBM per device.

v0:
```python
import jax
import jax.numpy as jnp
from jax import lax
from jax.sharding import PartitionSpec as P


def from_behind(value, axis, steps):
    count = lax.axis_size(axis)
    initial, last = (max(0, -steps), min(count, count - steps))
    return lax.ppermute(value, axis, [(source, source + steps) for source in range(initial, last)])


def contract_first(left, right):
    return lax.dot_general(
        left, right, (((0,), (0,)), ((), ())), preferred_element_type=jnp.float32
    )


def contract_last(left, right):
    return lax.dot_general(
        left, right, (((1,), (1,)), ((), ())), preferred_element_type=jnp.float32
    )


def on_device(
    lower_factor,
    arrow_factor,
    block_inverse,
    boundary_sigma,
    boundary_tip,
    tip_inverse,
    slope_weights,
):
    blocks = lower_factor.shape[0]
    rows = lower_factor.shape[1]
    offset = lax.axis_index("row") * rows
    sigma_state, tip_state = from_behind((boundary_sigma[0], boundary_tip[0]), "tm", -1)
    diag_list = [None] * blocks
    lower_list = [None] * blocks
    tip_list = [None] * blocks
    slope_local = jnp.float32(0.0)
    for j in reversed(range(blocks)):
        low = lower_factor[j]
        arr = arrow_factor[j]
        full_low, full_arr, full_tip = (
            lax.all_gather(low, "row", axis=0, tiled=True),
            lax.all_gather(arr, "row", axis=0, tiled=True),
            lax.all_gather(tip_state, "row", axis=0, tiled=True),
        )
        lower_c = -(
            jnp.dot(sigma_state, full_low, preferred_element_type=jnp.float32)
            + contract_last(tip_state, full_arr)
        )
        low_cols = lax.dynamic_slice_in_dim(full_low, offset, rows, 1)
        tip_n = -(
            contract_first(low_cols, full_tip)
            + jnp.dot(arr, tip_inverse, preferred_element_type=jnp.float32)
        )
        lower_b = lower_c.astype(jnp.bfloat16)
        tip_b = tip_n.astype(jnp.bfloat16)
        full_c, full_r = (
            lax.all_gather(lower_b, "row", axis=0, tiled=True),
            lax.all_gather(tip_b, "row", axis=0, tiled=True),
        )
        lower_sum = contract_first(low_cols, full_c)
        tip_sum = contract_last(arr, full_r)
        new_sigma = block_inverse[j].astype(jnp.float32) - lower_sum - tip_sum
        own_square = lax.dynamic_slice_in_dim(new_sigma, offset, rows, 1)
        slope_local = slope_local + jnp.sum(slope_weights[j] * jnp.diagonal(own_square))
        diag_list[j] = new_sigma
        lower_list[j] = lower_c
        tip_list[j] = tip_n
        sigma_state = new_sigma.astype(jnp.bfloat16)
        tip_state = tip_b
    slope = lax.psum(slope_local, ("tm", "row"))
    return (jnp.stack(diag_list), jnp.stack(lower_list), jnp.stack(tip_list), slope)


def solution(mesh):
    return jax.shard_map(
        on_device,
        mesh=mesh,
        in_specs=(
            P("tm", "row", None),
            P("tm", "row", None),
            P("tm", "row", None),
            P("tm", "row", None),
            P("tm", "row", None),
            P(),
            P("tm", "row"),
        ),
        out_specs=(P("tm", "row", None), P("tm", "row", None), P("tm", "row", None), P()),
        check_vma=False,
    )
```

profile of v0, /device:TPU:1, one launch (start us, length us, event | category | flops | bytes accessed | tf_op | source)
XLA Modules:
  0.0 688.5 jit_solution(175449894543334442)
XLA Ops:
  7.2 8.9 %collective-permute-start.1 = (bf16[64,512]{1,0:T(8,128)(2,1)}, bf16[64,512]{1,0:T(8,128)(2,1)S(1)}, u32[]{:S(2)}, u32[]{:S(2)}) collective-permute-start(bf16[64,512]{1,0:T(8,128)(2,1)} %bitcast.94), channel_id=1, source_target_pairs={{16,0},{32,16},{48,32},{64,48},{80,64},{96,80},{112,96},{128,112},... | collective-permute-start | bytes 196616 | tf_op jit(solution)/shard_map/ppermute | solution.py:10
  18.0 1.7 fusion.49
  19.7 1.5 fusion.50
  23.0 52.4 %all-gather.16.cloned.1.call-done = bf16[1024,512]{1,0:T(8,128)(2,1)} async-done(((bf16[64,512]{1,0:T(8,128)(2,1)}), bf16[1024,512]{1,0:T(8,128)(2,1)}) %all-gather.16.cloned.1.call-update) | async-done | bytes 1048592 | tf_op jit(solution)/shard_map/all_gather | solution.py:48
  75.3 63.8 %all-gather.26.cloned.1.call-done = bf16[1,1024,1024]{2,1,0:T(8,128)(2,1)} async-done(((bf16[1,64,1024]{2,1,0:T(8,128)(2,1)}), bf16[1,1024,1024]{2,1,0:T(8,128)(2,1)}) %all-gather.26.cloned.1.call-update) | async-done | bytes 2097168 | tf_op jit(solution)/shard_map/all_gather | solution.py:46
  139.1 2.5 fusion.51
  142.3 3.4 collective-permute-start
  145.7 53.3 %all-gather.28.cloned.1.call-done = bf16[1,1024,512]{2,1,0:T(8,128)(2,1)} async-done(((bf16[1,64,512]{2,1,0:T(8,128)(2,1)}), bf16[1,1024,512]{2,1,0:T(8,128)(2,1)}) %all-gather.28.cloned.1.call-update) | async-done | bytes 1048592 | tf_op jit(solution)/shard_map/all_gather | solution.py:47
  199.1 1.7 fusion.22
  200.8 1.2 fusion.52
  202.1 60.6 %all-gather.24.cloned.1.call-done = bf16[1,1024,1024]{2,1,0:T(8,128)(2,1)} async-done(((bf16[1,64,1024]{2,1,0:T(8,128)(2,1)}), bf16[1,1024,1024]{2,1,0:T(8,128)(2,1)}) %all-gather.24.cloned.1.call-update) | async-done | bytes 2097168 | tf_op jit(solution)/shard_map/all_gather | solution.py:46
  262.7 59.8 %all-gather.18.cloned.1.call-done = bf16[1024,512]{1,0:T(8,128)(2,1)} async-done(((bf16[64,512]{1,0:T(8,128)(2,1)}), bf16[1024,512]{1,0:T(8,128)(2,1)}) %all-gather.18.cloned.1.call-update) | async-done | bytes 1048592 | tf_op jit(solution)/shard_map/all_gather | solution.py:63
  322.5 1.8 fusion.26
  325.3 57.5 %all-gather.30.cloned.1.call-done = bf16[1,1024,512]{2,1,0:T(8,128)(2,1)} async-done(((bf16[1,64,512]{2,1,0:T(8,128)(2,1)}), bf16[1,1024,512]{2,1,0:T(8,128)(2,1)}) %all-gather.30.cloned.1.call-update) | async-done | bytes 1048592 | tf_op jit(solution)/shard_map/all_gather | solution.py:47
  382.8 2.4 fusion.20
  385.6 61.0 %all-gather.14.cloned.1.call-done = bf16[1024,1024]{1,0:T(8,128)(2,1)} async-done(((bf16[64,1024]{1,0:T(8,128)(2,1)}), bf16[1024,1024]{1,0:T(8,128)(2,1)}) %all-gather.14.cloned.1.call-update) | async-done | bytes 2097168 | tf_op jit(solution)/shard_map/all_gather | solution.py:62
  446.6 2.3 fusion.17
  450.1 1.6 pad_maximum_fusion.2
  452.6 53.9 %all-gather.22.cloned.1.call-done = bf16[1024,512]{1,0:T(8,128)(2,1)} async-done(((bf16[64,512]{1,0:T(8,128)(2,1)}), bf16[1024,512]{1,0:T(8,128)(2,1)}) %all-gather.22.cloned.1.call-update) | async-done | bytes 1048592 | tf_op jit(solution)/shard_map/all_gather | solution.py:63
  506.5 2.4 convolution_bitcast_fusion
  508.9 60.9 %all-gather.20.cloned.1.call-done = bf16[1024,1024]{1,0:T(8,128)(2,1)} async-done(((bf16[64,1024]{1,0:T(8,128)(2,1)}), bf16[1024,1024]{1,0:T(8,128)(2,1)}) %all-gather.20.cloned.1.call-update) | async-done | bytes 2097168 | tf_op jit(solution)/shard_map/all_gather | solution.py:62
  569.8 2.3 fusion.16
  574.9 1.8 pad_maximum_fusion.1
  576.7 104.5 %psum.7 = f32[]{:T(128)} all-reduce(f32[]{:T(128)S(6)} %add.34), channel_id=1, replica_groups=mesh['tm'=32,'row'=16] {'tm','row'}, use_global_device_ids=true, to_apply=%region_2.3 | all-reduce | flops 1 | bytes 8 | tf_op jit(solution)/shard_map/psum | solution.py:75
  (53 shorter events, 10.0 us)
Async XLA Ops:
  7.2 14.7 %copy-start = (bf16[512,512]{1,0:T(8,128)(2,1)S(1)}, bf16[512,512]{1,0:T(8,128)(2,1)}, u32[]{:S(2)}) copy-start(bf16[512,512]{1,0:T(8,128)(2,1)} %param.12) | copy-start | bytes 1572868
  7.2 135.1 %copy-start.10 = (bf16[1,64,1024]{2,1,0:T(8,128)(2,1)S(1)}, bf16[1,64,1024]{2,1,0:T(8,128)(2,1)}, u32[]{:S(2)}) copy-start(bf16[1,64,1024]{2,1,0:T(8,128)(2,1)} %param.10) | copy-start | bytes 393220
  7.2 68.2 %all-gather.16.cloned.1.call-start = ((), (), s32[]{:S(2)}) async-start(), calls=%async_computation.1 | async-start | bytes 1114112 | tf_op jit(solution)/shard_map/all_gather | solution.py:48
  7.2 10.0 %collective-permute-start.1 = (bf16[64,512]{1,0:T(8,128)(2,1)}, bf16[64,512]{1,0:T(8,128)(2,1)S(1)}, u32[]{:S(2)}, u32[]{:S(2)}) collective-permute-start(bf16[64,512]{1,0:T(8,128)(2,1)} %bitcast.94), channel_id=1, source_target_pairs={{16,0},{32,16},{48,32},{64,48},{80,64},{96,80},{112,96},{128,112},... | collective-permute-start | bytes 196616 | tf_op jit(solution)/shard_map/ppermute | solution.py:10
  17.3 0.6 copy-start.7
  17.9 181.2 %copy-start.8 = (bf16[64,512]{1,0:T(8,128)(2,1)S(1)}, bf16[64,512]{1,0:T(8,128)(2,1)}, u32[]{:S(2)}) copy-start(bf16[64,512]{1,0:T(8,128)(2,1)} %copy-done.7) | copy-start | bytes 196612
  17.9 121.2 %all-gather.26.cloned.1.call-start = ((), (), s32[]{:S(2)}) async-start(), calls=%async_computation.6 | async-start | bytes 2228224 | tf_op jit(solution)/shard_map/all_gather | solution.py:46
  19.7 179.4 %all-gather.28.cloned.1.call-start = ((), (), s32[]{:S(2)}) async-start(), calls=%async_computation.7 | async-start | bytes 1114112 | tf_op jit(solution)/shard_map/all_gather | solution.py:47
  21.3 241.5 %all-gather.24.cloned.1.call-start = ((), (), s32[]{:S(2)}) async-start(), calls=%async_computation.5 | async-start | bytes 2228224 | tf_op jit(solution)/shard_map/all_gather | solution.py:46
  21.9 300.7 %all-gather.18.cloned.1.call-start = ((), (), s32[]{:S(2)}) async-start(), calls=%async_computation.2 | async-start | bytes 1114112 | tf_op jit(solution)/shard_map/all_gather | solution.py:63
  139.1 61.6 %copy-start.3 = (bf16[1,1024,1024]{2,1,0:T(8,128)(2,1)S(1)}, bf16[1,1024,1024]{2,1,0:T(8,128)(2,1)}, u32[]{:S(2)}) copy-start(bf16[1,1024,1024]{2,1,0:T(8,128)(2,1)} %all-gather.26.cloned.1.call-done) | copy-start | bytes 6291460
  141.7 241.1 %all-gather.30.cloned.1.call-start = ((), (), s32[]{:S(2)}) async-start(), calls=%async_computation.8 | async-start | bytes 1114112 | tf_op jit(solution)/shard_map/all_gather | solution.py:47
  142.3 304.3 %all-gather.14.cloned.1.call-start = ((), (), s32[]{:S(2)}) async-start(), calls=%async_computation | async-start | bytes 2228224 | tf_op jit(solution)/shard_map/all_gather | solution.py:62
  142.3 58.4 %collective-permute-start = (bf16[64,1024]{1,0:T(8,128)(2,1)S(1)}, bf16[64,1024]{1,0:T(8,128)(2,1)S(1)}, u32[]{:S(2)}, u32[]{:S(2)}) collective-permute-start(bf16[64,1024]{1,0:T(8,128)(2,1)S(1)} %bitcast.93), channel_id=1, source_target_pairs={{16,0},{32,16},{48,32},{64,48},{80,64},{96,80},{112,96},{128,112},... | collective-permute-start | bytes 393224 | tf_op jit(solution)/shard_map/ppermute | solution.py:10
  200.7 123.6 %copy-start.4 = (bf16[2,64,512]{2,1,0:T(8,128)(2,1)S(1)}, bf16[2,64,512]{2,1,0:T(8,128)(2,1)}, u32[]{:S(2)}) copy-start(bf16[2,64,512]{2,1,0:T(8,128)(2,1)} %param.8) | copy-start | bytes 393220
  200.8 182.0 %copy-start.6 = (bf16[64,512]{1,0:T(8,128)(2,1)S(1)}, bf16[64,512]{1,0:T(8,128)(2,1)}, u32[]{:S(2)}) copy-start(bf16[64,512]{1,0:T(8,128)(2,1)} %get-tuple-element.10) | copy-start | bytes 196612
  202.0 304.5 %all-gather.22.cloned.1.call-start = ((), (), s32[]{:S(2)}) async-start(), calls=%async_computation.4 | async-start | bytes 1114112 | tf_op jit(solution)/shard_map/all_gather | solution.py:63
  322.5 62.6 %copy-start.1 = (bf16[1024,512]{1,0:T(8,128)(2,1)S(1)}, bf16[1024,512]{1,0:T(8,128)(2,1)}, u32[]{:S(2)}) copy-start(bf16[1024,512]{1,0:T(8,128)(2,1)} %all-gather.18.cloned.1.call-done) | copy-start | bytes 3145732
  325.3 244.5 %all-gather.20.cloned.1.call-start = ((), (), s32[]{:S(2)}) async-start(), calls=%async_computation.3 | async-start | bytes 2228224 | tf_op jit(solution)/shard_map/all_gather | solution.py:62
  385.6 63.3 %copy-start.2 = (bf16[1,1024,1024]{2,1,0:T(8,128)(2,1)S(1)}, bf16[1,1024,1024]{2,1,0:T(8,128)(2,1)}, u32[]{:S(2)}) copy-start(bf16[1,1024,1024]{2,1,0:T(8,128)(2,1)} %all-gather.24.cloned.1.call-done) | copy-start | bytes 6291460
  446.6 2.3 copy-start.5
  508.9 64.1 %copy-start.9 = (f32[2,64]{1,0:T(2,128)S(1)}, f32[2,64]{1,0:T(2,128)}, u32[]{:S(2)}) copy-start(f32[2,64]{1,0:T(2,128)} %param.13) | copy-start | bytes 1540
Sparse Core Ops, SparseCore 0:
  18.0 57.2 all-gather.15
  78.9 60.1 all-gather.25
  142.2 56.8 all-gather.27
  202.5 60.1 all-gather.23
  265.6 56.8 all-gather.17
  325.4 57.3 all-gather.29
  386.4 60.1 all-gather.13
  449.6 56.8 all-gather.21
  509.5 60.1 all-gather.19
where the time goes:
time: 689 us
  waiting for transfers between devices  525 us (76%)
  blocking collectives  105 us (15%)
  matrix products  20.1 us (3%)
  between operations  15.3 us (2%)
  starting transfers between devices  12.7 us (2%)
    all_gather x2, waiting for transfers between devices, on_device(): lax.all_gather(low, 'row', axis=0, tiled=True)  124 us
    all_gather x2, waiting for transfers between devices, on_device(): lax.all_gather(lower_b, 'row', axis=0, tiled=True)  122 us
    all_gather x2, waiting for transfers between devices, on_device(): lax.all_gather(tip_b, 'row', axis=0, tiled=True)  114 us
    all_gather x2, waiting for transfers between devices, on_device(): lax.all_gather(arr, 'row', axis=0, tiled=True)  111 us
    psum x1, blocking collectives, on_device(): slope = lax.psum(slope_local, ('tm', 'row'))  105 us
    all_gather x1, waiting for transfers between devices, on_device(): lax.all_gather(tip_state, 'row', axis=0, tiled=True)  52.4 us
  transfers between devices with their start and end apart: 11, of which 10 were waited for; matrix products, arithmetic and copies ran while one was open for 3% of the time, Pallas kernels for 0%

commit v1 on v0

v1 whole, which is shorter than its diff:
```python
import jax
import jax.numpy as jnp
from jax import lax
from jax.experimental import pallas as pl
from jax.experimental.pallas import tpu as pltpu
from jax.sharding import Mesh, PartitionSpec as P

SIDE = 4
ROWS = 64
HALF = 512
BLOCK = 1024
BF = jnp.bfloat16
F32 = jnp.float32
EVERY = ("tm", "y", "x")

S, R, L1, M1, L0, M0, X1 = 0, 2, 3, 5, 6, 8, 9
KEPT = 9 * ROWS
SENT = 11 * ROWS
PANEL = SIDE * KEPT
SHARE = 2 * ROWS
VMEM_BYTES = 48 * 1024 * 1024


def line_groups(partitions, phase):
    groups = []
    for t in range(partitions):
        base = t * SIDE * SIDE
        for i in range(SIDE):
            if (t + phase) % 2 == 0:
                groups.append([base + SIDE * i + x for x in range(SIDE)])
            else:
                groups.append([base + SIDE * y + i for y in range(SIDE)])
    return groups


def height_groups(partitions):
    plane = SIDE * SIDE
    return [
        [t * plane + r for t in range(core, partitions, 2)]
        for core in range(2)
        for r in range(plane)
    ]


def exchange(value, groups):
    return lax.all_to_all(value, EVERY, 0, 0, tiled=True, axis_index_groups=groups)


def dot(left, right):
    return jnp.dot(left, right, preferred_element_type=F32)


def dot_t(left, right):
    return lax.dot_general(left, right, (((1,), (1,)), ((), ())), preferred_element_type=F32)


def split(value):
    high = value.astype(BF)
    return high, (value - high.astype(F32)).astype(BF)


def place():
    core = lax.rem(lax.axis_index("tm"), 2)
    y, x = lax.axis_index("y"), lax.axis_index("x")
    first = jnp.where(core == 0, x, y)
    return core, y * SIDE + x, first


def natural(core, second, first):
    return jnp.where(core == 0, SIDE * second + first, SIDE * first + second)


def columns_t(ref, piece, row):
    half = lax.div(row, 8)
    lane = lax.div(lax.rem(row, 8), 2)
    window = ref[
        :,
        pl.ds(pl.multiple_of((piece + half) * ROWS, ROWS), ROWS),
        pl.ds(pl.multiple_of(lane * 128, 128), 128),
    ]
    window = window.reshape(window.shape[0] * ROWS, 128)
    want = lax.broadcasted_iota(jnp.int32, (ROWS, 128), 0) + lax.rem(row, 2) * ROWS
    pick = jnp.where(lax.broadcasted_iota(jnp.int32, (ROWS, 128), 1) == want, 1.0, 0.0)
    return dot_t(pick.astype(BF), window).astype(BF)


def panel_kernel(got, out, panel, xs, share, sem_in, sem_x, sem_out, sem_share):
    core, _, first = place()
    loads = [
        pltpu.make_async_copy(got.at[j, pl.ds(0, KEPT)], panel.at[j], sem_in.at[j])
        for j in range(SIDE)
    ]
    loads_x = [
        pltpu.make_async_copy(got.at[j, pl.ds(KEPT, SHARE)], xs.at[j], sem_x.at[j])
        for j in range(SIDE)
    ]
    for copy in loads + loads_x:
        copy.start()
    for copy in loads:
        copy.wait()
    stores = [
        pltpu.make_async_copy(
            panel.at[j], out.at[d, pl.ds(j * KEPT, KEPT)], sem_out.at[d * SIDE + j]
        )
        for d in range(SIDE)
        for j in range(SIDE)
    ]
    for copy in stores:
        copy.start()
    cols = [columns_t(panel, L0, natural(core, d, first)) for d in range(SIDE)]
    cols = jnp.concatenate(cols, axis=0)
    for copy in loads_x:
        copy.wait()
    for h in range(2):
        part = dot(cols, xs[:, h * ROWS : (h + 1) * ROWS, :].reshape(SIDE * ROWS, HALF))
        for d in range(SIDE):
            share[d, h * ROWS : (h + 1) * ROWS, :] = part[d * ROWS : (d + 1) * ROWS].astype(BF)
    stores_share = [
        pltpu.make_async_copy(share.at[d], out.at[d, pl.ds(PANEL, SHARE)], sem_share.at[d])
        for d in range(SIDE)
    ]
    for copy in stores_share:
        copy.start()
    for copy in stores + stores_share:
        copy.wait()


def block_kernel(
    got, x_ref, q_ref, weight_ref, diag, lower, tip, slope, mat, shares, sem_in, sem_share
):
    core, row, _ = place()
    loads = []
    for d in range(SIDE):
        for j in range(SIDE):
            loads.append(
                pltpu.make_async_copy(
                    got.at[d, pl.ds(j * KEPT, KEPT)],
                    mat.at[natural(core, d, j)],
                    sem_in.at[d * SIDE + j],
                )
            )
    loads_share = [
        pltpu.make_async_copy(got.at[d, pl.ds(PANEL, SHARE)], shares.at[d], sem_share.at[d])
        for d in range(SIDE)
    ]
    for copy in loads + loads_share:
        copy.start()
    for copy in loads + loads_share:
        copy.wait()

    def piece(k, q):
        return mat[SIDE * q : SIDE * (q + 1), k * ROWS : (k + 1) * ROWS, :].reshape(
            SIDE * ROWS, HALF
        )

    def part(value, q):
        return value[:, q * 256 : (q + 1) * 256]

    def own(k):
        return mat[row, k * ROWS : (k + 1) * ROWS, :]

    def over_rows(left, k):
        total = dot(part(left, 0), piece(k, 0))
        for q in range(1, SIDE):
            total += dot(part(left, q), piece(k, q))
        return total

    def over_columns(left, k):
        return jnp.concatenate([dot_t(left, piece(k, q)) for q in range(SIDE)], axis=1)

    def times_factor(left_rows, left_tip, low, arr):
        both = jnp.concatenate([over_rows(left_rows, low + h) for h in range(2)], axis=1)
        return both + over_columns(left_tip, arr)

    z1 = columns_t(mat, L1, row)
    z0 = columns_t(mat, L0, row)
    z1_tip, z0_tip = own(M1), own(M0)
    u = over_columns(z0[:, :HALF], L1) + over_columns(z0[:, HALF:], L1 + 1)
    u_tip = over_rows(z0, M1) - z0_tip.astype(F32)
    uh, ul = split(u)
    uh_tip, ul_tip = split(u_tip)
    rows_in = jnp.concatenate([z1, uh, ul], axis=0)
    tip_in = jnp.concatenate([z1_tip, uh_tip, ul_tip], axis=0)
    top = jnp.concatenate([over_rows(rows_in, S + h) for h in range(2)], axis=1)
    top = top + over_columns(tip_in, R)
    bottom = over_rows(rows_in, R) + dot(tip_in, q_ref[...])
    p1, a = top[:64], top[64:128] + top[128:]
    p1_tip, a_tip = bottom[:64], bottom[64:128] + bottom[128:]
    tip[1] = -p1_tip
    tip[0] = a_tip
    own_rows = jnp.concatenate([own(S), own(S + 1)], axis=1)
    p1h, p1l = split(p1)
    ah, al = split(a)
    p1h_tip, p1l_tip = split(p1_tip)
    ah_tip, al_tip = split(a_tip)
    out = times_factor(
        jnp.concatenate([p1h, p1l, ah, al, own_rows], axis=0),
        jnp.concatenate([p1h_tip, p1l_tip, ah_tip, al_tip, own(R)], axis=0),
        L1,
        M1,
    )
    lower[1] = -out[256:]
    sigma1 = x_ref[1].astype(F32) + out[:64] + out[64:128]
    diag[1] = sigma1
    carried = shares[0].astype(F32)
    for d in range(1, SIDE):
        carried += shares[d].astype(F32)
    carried = jnp.concatenate([carried[:ROWS], carried[ROWS:]], axis=1)
    p0 = carried + out[128:192] + out[192:256]
    p0h, p0l = split(p0)
    out = times_factor(
        jnp.concatenate([p0h, p0l, sigma1.astype(BF)], axis=0),
        jnp.concatenate([-ah_tip, -al_tip, (-p1_tip).astype(BF)], axis=0),
        L0,
        M0,
    )
    lower[0] = -out[128:]
    sigma0 = x_ref[0].astype(F32) + out[:64] + out[64:128]
    diag[0] = sigma0
    at = lax.broadcasted_iota(jnp.int32, (ROWS, BLOCK), 0) + row * ROWS
    on_diagonal = lax.broadcasted_iota(jnp.int32, (ROWS, BLOCK), 1) == at
    traced = sigma0 * weight_ref[0] + sigma1 * weight_ref[1]
    traced = jnp.sum(jnp.where(on_diagonal, traced, 0.0))
    slope[...] = jnp.full(slope.shape, traced, F32)


def on_device(
    lower_factor,
    arrow_factor,
    block_inverse,
    boundary_sigma,
    boundary_tip,
    tip_inverse,
    slope_weights,
    partitions,
):
    start = jnp.concatenate([boundary_sigma[0], boundary_tip[0]], axis=1)
    start = lax.ppermute(start, "tm", [(p + 1, p) for p in range(partitions - 1)])
    wide = jnp.concatenate(
        [
            start,
            lower_factor[1],
            arrow_factor[1],
            lower_factor[0],
            arrow_factor[0],
            block_inverse[1],
        ],
        axis=1,
    )
    rows = jnp.concatenate([wide[:, HALF * k : HALF * (k + 1)] for k in range(11)], axis=0)
    rows = jnp.broadcast_to(rows[None], (SIDE, SENT, HALF))
    got = exchange(rows, line_groups(partitions, 0))
    anywhere = pl.BlockSpec(memory_space=pl.ANY)
    fast = pl.BlockSpec(memory_space=pltpu.VMEM)
    params = pltpu.CompilerParams(vmem_limit_bytes=VMEM_BYTES)
    sent = pl.pallas_call(
        panel_kernel,
        out_shape=jax.ShapeDtypeStruct((SIDE, PANEL + SHARE, HALF), BF),
        in_specs=[anywhere],
        out_specs=anywhere,
        scratch_shapes=[
            pltpu.VMEM((SIDE, KEPT, HALF), BF),
            pltpu.VMEM((SIDE, SHARE, HALF), BF),
            pltpu.VMEM((SIDE, SHARE, HALF), BF),
            pltpu.SemaphoreType.DMA((SIDE,)),
            pltpu.SemaphoreType.DMA((SIDE,)),
            pltpu.SemaphoreType.DMA((16,)),
            pltpu.SemaphoreType.DMA((SIDE,)),
        ],
        compiler_params=params,
    )(got)
    got = exchange(sent, line_groups(partitions, 1))
    weights = slope_weights[:, :, None]
    diag, lower, tip, slope = pl.pallas_call(
        block_kernel,
        out_shape=(
            jax.ShapeDtypeStruct((2, ROWS, BLOCK), F32),
            jax.ShapeDtypeStruct((2, ROWS, BLOCK), F32),
            jax.ShapeDtypeStruct((2, ROWS, HALF), F32),
            jax.ShapeDtypeStruct((16, 8, 128), F32),
        ),
        in_specs=[anywhere, fast, fast, fast],
        out_specs=(fast, fast, fast, fast),
        scratch_shapes=[
            pltpu.VMEM((16, KEPT, HALF), BF),
            pltpu.VMEM((SIDE, SHARE, HALF), BF),
            pltpu.SemaphoreType.DMA((16,)),
            pltpu.SemaphoreType.DMA((SIDE,)),
        ],
        compiler_params=params,
    )(got, block_inverse, tip_inverse, weights)
    total = jnp.sum(lax.all_to_all(slope, ("y", "x"), 0, 0, tiled=True), axis=0)
    total = jnp.broadcast_to(total[None], (partitions // 2, 8, 128))
    total = jnp.sum(exchange(total, height_groups(partitions)), axis=0)
    other = lax.ppermute(total, "tm", [(p, p ^ 1) for p in range(partitions)])
    return diag, lower, tip, (total + other)[0, 0]


def solution(mesh):
    partitions = mesh.shape["tm"]
    fine = Mesh(mesh.devices.reshape(partitions, SIDE, SIDE), EVERY)
    rows = P("tm", ("y", "x"), None)

    def program(*args):
        return on_device(*args, partitions=partitions)

    return jax.shard_map(
        program,
        mesh=fine,
        in_specs=(rows, rows, rows, rows, rows, P(), P("tm", ("y", "x"))),
        out_specs=(rows, rows, rows, P()),
        check_vma=False,
    )
```

time: 689 us -> 156 us (0.23)
  waiting for transfers between devices: 525 us -> 58.5 us
  blocking collectives: 105 us -> 56.2 us
  matrix products: 20.1 us -> 0 us
  between operations: 15.3 us -> 0.8 us
  Pallas kernels: 0 us -> 14.2 us
  starting transfers between devices: 12.7 us -> 20.6 us
    all_gather x9 -> x0, waiting for transfers between devices: 523 us -> none  [the longest x2 124 us: on_device(): lax.all_gather(low, 'row', axis=0, tiled=True)]
    psum x1 -> x0, blocking collectives: 105 us -> none  [on_device(): slope = lax.psum(slope_local, ('tm', 'row'))]
    all_to_all x0 -> x1, waiting for transfers between devices: none -> 57.7 us  [exchange(): lax.all_to_all(value, EVERY, 0, 0, tiled=True, axis_index_groups=groups)]
    all_to_all x0 -> x3, blocking collectives: none -> 56.2 us  [the longest x2 47.1 us: exchange(): lax.all_to_all(value, EVERY, 0, 0, tiled=True, axis_index_groups=groups)]
    dot_general x12 -> x0, matrix products: 20.1 us -> none  [the longest x4 8.93 us: contract_first(): lax.dot_general(left, right, (((0,), (0,)), ((), ())), preferred_element_...]
    pallas_call x0 -> x2, Pallas kernels: none -> 14.2 us  [the longest x1 8.99 us: on_device(): pl.pallas_call(block_kernel, out_shape=(jax.ShapeDtypeStruct((2, ROWS, BL...]
  transfers between devices with their start and end apart: 11 -> 3, of which waited for: 10 -> 2; matrix products, arithmetic and copies ran while one was open for 3% -> 1% of each run, Pallas kernels for 0% -> 0%
where the time goes in v1:
time: 156 us
  waiting for transfers between devices  58.5 us (38%)
  blocking collectives  56.2 us (36%)
  starting transfers between devices  20.6 us (13%)
  Pallas kernels  14.2 us (9%)
  local copies, waits for them, and re-layouts  4.52 us (3%)
    all_to_all x1, waiting for transfers between devices, exchange(): lax.all_to_all(value, EVERY, 0, 0, tiled=True, axis_index_groups=groups)  57.7 us
    all_to_all x2, blocking collectives, exchange(): lax.all_to_all(value, EVERY, 0, 0, tiled=True, axis_index_groups=groups)  47.1 us
    all_to_all x1, blocking collectives, on_device(): total = jnp.sum(lax.all_to_all(slope, ('y', 'x'), 0, 0, tiled=True), axis=0)  9.07 us
    pallas_call x1, Pallas kernels, on_device(): pl.pallas_call(block_kernel, out_shape=(jax.ShapeDtypeStruct((2, ROWS, BL...  8.99 us
    ppermute x1, starting transfers between devices, on_device(): lax.ppermute(start, 'tm', [(p + 1, p) for p in range(partitions - 1)])  8.79 us
    all_to_all x1, starting transfers between devices, exchange(): lax.all_to_all(value, EVERY, 0, 0, tiled=True, axis_index_groups=groups)  6.03 us
    ppermute x1, starting transfers between devices, on_device(): other = lax.ppermute(total, 'tm', [(p, p ^ 1) for p in range(partitions)])  5.74 us
    pallas_call x1, Pallas kernels, on_device(): pl.pallas_call(panel_kernel, out_shape=jax.ShapeDtypeStruct((SIDE, PANEL...  5.2 us
  transfers between devices with their start and end apart: 3, of which 2 were waited for; matrix products, arithmetic and copies ran while one was open for 1% of the time, Pallas kernels for 0%

profile of v1, /device:TPU:1, one launch (start us, length us, event | category | flops | bytes accessed | tf_op | source)
XLA Modules:
  0.0 155.8 jit_solution(3117667925495244509)
XLA Ops:
  0.6 1.0 pad_maximum_fusion
  1.6 8.8 %collective-permute-start = (bf16[64,1536]{1,0:T(8,128)(2,1)S(1)}, bf16[64,1536]{1,0:T(8,128)(2,1)S(1)}, u32[]{:S(2)}, u32[]{:S(2)}) collective-permute-start(bf16[64,1536]{1,0:T(8,128)(2,1)S(1)} %pad_maximum_fusion), channel_id=1, source_target_pairs={{16,0},{32,16},{48,32},{64,48},{80,64},{96,80},{112,96},{128,112},... | collective-permute-start | bytes 589832 | tf_op jit(solution)/shard_map/ppermute | solution.py:238
  10.4 1.0 slice_bitcast_fusion.1
  11.4 0.9 slice_bitcast_fusion
  12.3 0.0 collective-permute-done
  12.4 0.8 bitcast_dynamic-update-slice_fusion.1
  13.3 0.8 bitcast_dynamic-update-slice_fusion
  14.1 0.2 broadcast_in_dim.6
  14.4 22.3 %all_to_all.20.got = bf16[4,704,512]{2,1,0:T(8,128)(2,1)S(1)} all-to-all(bf16[4,704,512]{2,1,0:T(8,128)(2,1)S(1)} %broadcast_in_dim.6), channel_id=1, replica_groups={{0,1,2,3},{4,5,6,7},{8,9,10,11},{12,13,14,15},{16,20,24,28},{17,21,25,2..., dimensions={0} | all-to-all | bytes 5767168 | tf_op jit(solution)/shard_map/all_to_all | solution.py:46
  36.7 5.2 %shard_map.102 = bf16[4,2432,512]{2,1,0:T(8,128)(2,1)} custom-call(bf16[4,704,512]{2,1,0:T(8,128)(2,1)S(1)} %all_to_all.20.got), custom_call_target="tpu_custom_call" | custom-call | tf_op jit(solution)/shard_map/pallas_call | solution.py:256
  41.9 0.0 copy-start.2
  41.9 0.0 copy-start
  41.9 0.0 copy-start.1
  41.9 6.0 %all-to-all-start.1 = ((bf16[4,2432,512]{2,1,0:T(8,128)(2,1)}), bf16[4,2432,512]{2,1,0:T(8,128)(2,1)}, u32[]{:S(2)}, u32[]{:S(2)}) async-start(bf16[4,2432,512]{2,1,0:T(8,128)(2,1)} %shard_map.102), calls=%async_computation.1 | async-start | bytes 19922944 | tf_op jit(solution)/shard_map/all_to_all | solution.py:46
  48.0 0.0 copy-done.2
  48.0 0.1 copy.12.weight_ref
  48.1 57.7 %all-to-all-done.1.got = bf16[4,2432,512]{2,1,0:T(8,128)(2,1)} async-done(((bf16[4,2432,512]{2,1,0:T(8,128)(2,1)}), bf16[4,2432,512]{2,1,0:T(8,128)(2,1)}, u32[]{:S(2)}, u32[]{:S(2)}) %all-to-all-start.1) | async-done | bytes 9961504 | tf_op jit(solution)/shard_map/all_to_all | solution.py:46
  105.8 0.0 copy-done
  105.8 9.0 %shard_map.103 = (f32[2,64,1024]{2,1,0:T(8,128)}, f32[2,64,1024]{2,1,0:T(8,128)}, f32[2,64,512]{2,1,0:T(8,128)}, f32[16,8,128]{2,1,0:T(8,128)S(1)}) custom-call(bf16[4,2432,512]{2,1,0:T(8,128)(2,1)} %all-to-all-done.1.got, bf16[2,64,1024]{2,1,0:T(8,128)(2,1)S(1)} %copy-done, bf16[512,512]{1,0:T(8,128)(2,1)S(1)} %copy-done.1, f32[2,64,1]{2,1,0:T(8,128)S(1)} %copy.12.weight_ref), custom_call_target="tpu_custom_call" | custom-call | tf_op jit(solution)/shard_map/pallas_call | solution.py:274
  114.8 9.1 %all_to_all.21 = f32[16,8,128]{2,1,0:T(8,128)S(1)} all-to-all(f32[16,8,128]{2,1,0:T(8,128)S(1)} %get-tuple-element.11), channel_id=1, replica_groups=mesh['tm'=32,'y'=4,'x'=4] {'y','x'}, dimensions={0} | all-to-all | bytes 131072 | tf_op jit(solution)/shard_map/all_to_all | solution.py:292
  123.9 24.8 %all_to_all.22 = f32[16,8,128]{2,1,0:T(8,128)S(1)} all-to-all(f32[16,8,128]{2,1,0:T(8,128)S(1)} %broadcast_in_dim.8), channel_id=1, replica_groups={{0,32,64,96,128,160,192,224,256,288,320,352,384,416,448,480},{1,33,65,9..., dimensions={0} | all-to-all | bytes 131072 | tf_op jit(solution)/shard_map/all_to_all | solution.py:46
  148.7 5.7 %collective-permute-start.1 = (f32[8,128]{1,0:T(8,128)S(1)}, f32[8,128]{1,0:T(8,128)S(1)}, u32[]{:S(2)}, u32[]{:S(2)}) collective-permute-start(f32[8,128]{1,0:T(8,128)S(1)} %reduce_sum.19), channel_id=1, source_target_pairs={{0,16},{16,0},{32,48},{48,32},{64,80},{80,64},{96,112},{112,96},{1... | collective-permute-start | bytes 12296 | tf_op jit(solution)/shard_map/ppermute | solution.py:295
  154.5 0.8 collective-permute-done.1
  155.3 0.5 slice.59
  (14 shorter events, 0.1 us)
Async XLA Ops:
  1.6 10.7 %collective-permute-start = (bf16[64,1536]{1,0:T(8,128)(2,1)S(1)}, bf16[64,1536]{1,0:T(8,128)(2,1)S(1)}, u32[]{:S(2)}, u32[]{:S(2)}) collective-permute-start(bf16[64,1536]{1,0:T(8,128)(2,1)S(1)} %pad_maximum_fusion), channel_id=1, source_target_pairs={{16,0},{32,16},{48,32},{64,48},{80,64},{96,80},{112,96},{128,112},... | collective-permute-start | bytes 589832 | tf_op jit(solution)/shard_map/ppermute | solution.py:238
  41.9 6.1 %copy-start.2 = (f32[2,64]{1,0:T(2,128)S(1)}, f32[2,64]{1,0:T(2,128)}, u32[]{:S(2)}) copy-start(f32[2,64]{1,0:T(2,128)} %param.13) | copy-start | bytes 1540
  41.9 63.9 %copy-start = (bf16[2,64,1024]{2,1,0:T(8,128)(2,1)S(1)}, bf16[2,64,1024]{2,1,0:T(8,128)(2,1)}, u32[]{:S(2)}) copy-start(bf16[2,64,1024]{2,1,0:T(8,128)(2,1)} %x_ref.1) | copy-start | bytes 786436
  41.9 63.9 %copy-start.1 = (bf16[512,512]{1,0:T(8,128)(2,1)S(1)}, bf16[512,512]{1,0:T(8,128)(2,1)}, u32[]{:S(2)}) copy-start(bf16[512,512]{1,0:T(8,128)(2,1)} %q_ref.1) | copy-start | bytes 1572868
  41.9 63.9 %all-to-all-start.1 = ((bf16[4,2432,512]{2,1,0:T(8,128)(2,1)}), bf16[4,2432,512]{2,1,0:T(8,128)(2,1)}, u32[]{:S(2)}, u32[]{:S(2)}) async-start(bf16[4,2432,512]{2,1,0:T(8,128)(2,1)} %shard_map.102), calls=%async_computation.1 | async-start | bytes 19922944 | tf_op jit(solution)/shard_map/all_to_all | solution.py:46
  148.7 6.5 %collective-permute-start.1 = (f32[8,128]{1,0:T(8,128)S(1)}, f32[8,128]{1,0:T(8,128)S(1)}, u32[]{:S(2)}, u32[]{:S(2)}) collective-permute-start(f32[8,128]{1,0:T(8,128)S(1)} %reduce_sum.19), channel_id=1, source_target_pairs={{0,16},{16,0},{32,48},{48,32},{64,80},{80,64},{96,112},{112,96},{1... | collective-permute-start | bytes 12296 | tf_op jit(solution)/shard_map/ppermute | solution.py:295

commit v2 on v1

v2 whole, which is shorter than its diff:
```python
import jax
import jax.numpy as jnp
from jax import lax
from jax.experimental import pallas as pl
from jax.experimental.pallas import tpu as pltpu
from jax.sharding import Mesh, PartitionSpec as P

SIDE = 4
ROWS = 64
HALF = 512
BLOCK = 1024
BF = jnp.bfloat16
F32 = jnp.float32
EVERY = ("tm", "y", "x")

S, R, L1, M1, L0, M0, X1 = 0, 2, 3, 5, 6, 8, 9
EARLY = 6 * ROWS
PART = 3 * ROWS
SENT = 11 * ROWS
SHARE = 2 * ROWS
OWN = SHARE + 32
VMEM_BYTES = 60 * 1024 * 1024


def line_groups(partitions, phase):
    groups = []
    for t in range(partitions):
        base = t * SIDE * SIDE
        for i in range(SIDE):
            if (t + phase) % 2 == 0:
                groups.append([base + SIDE * i + x for x in range(SIDE)])
            else:
                groups.append([base + SIDE * y + i for y in range(SIDE)])
    return groups


def height_groups(partitions):
    plane = SIDE * SIDE
    return [
        [t * plane + r for t in range(core, partitions, 2)]
        for core in range(2)
        for r in range(plane)
    ]


def line_shift(partitions, steps):
    pairs = []
    for t in range(partitions):
        for y in range(SIDE):
            for x in range(SIDE):
                to = ((y + steps) % SIDE, x) if t % 2 == 0 else (y, (x + steps) % SIDE)
                base = t * SIDE * SIDE
                pairs.append((base + SIDE * y + x, base + SIDE * to[0] + to[1]))
    return pairs


def cost(megabytes):
    return pl.CostEstimate(flops=0, bytes_accessed=megabytes * 1_000_000, transcendentals=0)


def exchange(value, groups):
    return lax.all_to_all(value, EVERY, 0, 0, tiled=True, axis_index_groups=groups)


def dot(left, right):
    return jnp.dot(left, right, preferred_element_type=F32)


def dot_t(left, right):
    return lax.dot_general(left, right, (((1,), (1,)), ((), ())), preferred_element_type=F32)


def split(value):
    high = value.astype(BF)
    return high, (value - high.astype(F32)).astype(BF)


def place():
    core = lax.rem(lax.axis_index("tm"), 2)
    y, x = lax.axis_index("y"), lax.axis_index("x")
    first = jnp.where(core == 0, x, y)
    return core, y * SIDE + x, first


def natural(core, second, first):
    return jnp.where(core == 0, SIDE * second + first, SIDE * first + second)


def columns_t(ref, piece, row):
    half = lax.div(row, 8)
    lane = lax.div(lax.rem(row, 8), 2)
    window = ref[
        :,
        pl.ds(pl.multiple_of((piece + half) * ROWS, ROWS), ROWS),
        pl.ds(pl.multiple_of(lane * 128, 128), 128),
    ]
    window = window.reshape(window.shape[0] * ROWS, 128)
    want = lax.broadcasted_iota(jnp.int32, (ROWS, 128), 0) + lax.rem(row, 2) * ROWS
    pick = jnp.where(lax.broadcasted_iota(jnp.int32, (ROWS, 128), 1) == want, 1.0, 0.0)
    return dot_t(pick.astype(BF), window).astype(BF)


def panel_kernel(got, out, out_late, panel, mine, sem_in, sem_out, sem_late, sem_mine):
    core, _, first = place()
    loads = [pltpu.make_async_copy(got.at[j], panel.at[j], sem_in.at[j]) for j in range(SIDE)]
    for copy in loads:
        copy.start()
    stores = []
    for j in range(SIDE):
        loads[j].wait()
        here = [
            pltpu.make_async_copy(
                panel.at[j, pl.ds(0, EARLY)],
                out.at[d, pl.ds(j * EARLY, EARLY)],
                sem_out.at[d * SIDE + j],
            )
            for d in range(SIDE)
        ]
        here += [
            pltpu.make_async_copy(
                panel.at[j, pl.ds(EARLY, PART)],
                out_late.at[pl.ds(j * PART, PART)],
                sem_late.at[j],
            ),
        ]
        for copy in here:
            copy.start()
        stores += here
    cols = [columns_t(panel, L0, natural(core, d, first)) for d in range(SIDE)]
    for d in range(SIDE):
        mine[d, SHARE:, :] = jnp.concatenate([cols[d][:32], cols[d][32:]], axis=1)
    cols = jnp.concatenate(cols, axis=0)
    for h in range(2):
        at = (X1 + h) * ROWS
        part = dot(cols, panel[:, at : at + ROWS, :].reshape(SIDE * ROWS, HALF))
        for d in range(SIDE):
            mine[d, h * ROWS : (h + 1) * ROWS, :] = part[d * ROWS : (d + 1) * ROWS].astype(BF)
    stores_mine = [
        pltpu.make_async_copy(mine.at[d], out.at[d, pl.ds(SIDE * EARLY, OWN)], sem_mine.at[d])
        for d in range(SIDE)
    ]
    for copy in stores_mine:
        copy.start()
    for copy in stores + stores_mine:
        copy.wait()


class Gathered:
    def __init__(self, mat):
        self.mat = mat

    def piece(self, k, q):
        rows = self.mat[SIDE * q : SIDE * (q + 1), k * ROWS : (k + 1) * ROWS, :]
        return rows.reshape(SIDE * ROWS, HALF)

    def over_rows(self, left, k):
        total = dot(left[:, :256], self.piece(k, 0))
        for q in range(1, SIDE):
            total += dot(left[:, q * 256 : (q + 1) * 256], self.piece(k, q))
        return total

    def over_columns(self, left, k):
        return jnp.concatenate([dot_t(left, self.piece(k, q)) for q in range(SIDE)], axis=1)

    def times_factor(self, left_rows, left_tip, k):
        both = jnp.concatenate([self.over_rows(left_rows, k + h) for h in range(2)], axis=1)
        return both + self.over_columns(left_tip, k + 2)


def load_exchanged(got, mat, sem, piece):
    core, _, _ = place()
    return [
        pltpu.make_async_copy(
            got.at[d, pl.ds(j * EARLY + piece * ROWS, PART)],
            mat.at[natural(core, d, j)],
            sem.at[d * SIDE + j],
        )
        for d in range(SIDE)
        for j in range(SIDE)
    ]


def load_shifted(panels, mat, sem):
    core, _, _ = place()
    second = jnp.where(core == 0, lax.axis_index("y"), lax.axis_index("x"))
    return [
        pltpu.make_async_copy(
            panel.at[pl.ds(j * PART, PART)],
            mat.at[natural(core, lax.rem(second + SIDE - k, SIDE), j)],
            sem.at[k * SIDE + j],
        )
        for k, panel in enumerate(panels)
        for j in range(SIDE)
    ]


def trace_kernel(
    got,
    arrow_ref,
    x_ref,
    q_ref,
    weight_ref,
    tip,
    rows_out,
    tip_out,
    slope,
    factor,
    state,
    shares,
    sem_factor,
    sem_state,
    sem_share,
):
    core, row, _ = place()
    load_share = pltpu.make_async_copy(got.at[:, pl.ds(SIDE * EARLY, OWN)], shares, sem_share)
    load_factor = load_exchanged(got, factor, sem_factor, L1)
    load_state = load_exchanged(got, state, sem_state, S)
    for copy in [load_share] + load_factor + load_state:
        copy.start()
    for copy in [load_share] + load_factor:
        copy.wait()
    have = Gathered(factor)
    z1 = columns_t(factor, 0, row)
    z1_tip, z0_tip = arrow_ref[1], arrow_ref[0]
    parts = []
    for d in range(SIDE):
        held = shares[d, SHARE:, :]
        parts.append(jnp.concatenate([held[:, :256], held[:, 256:]], axis=0))
    even = jnp.concatenate(parts, axis=1)
    odd = [parts[d][:, j * 64 : (j + 1) * 64] for j in range(SIDE) for d in range(SIDE)]
    z0 = jnp.where(core == 0, even, jnp.concatenate(odd, axis=1))
    u = have.over_columns(z0[:, :HALF], 0) + have.over_columns(z0[:, HALF:], 1)
    u_tip = have.over_rows(z0, 2) - z0_tip.astype(F32)
    uh, ul = split(u)
    uh_tip, ul_tip = split(u_tip)
    rows_in = jnp.concatenate([z1, uh, ul], axis=0)
    tip_in = jnp.concatenate([z1_tip, uh_tip, ul_tip], axis=0)
    for copy in load_state:
        copy.wait()
    have = Gathered(state)
    top = have.times_factor(rows_in, tip_in, 0)
    bottom = have.over_rows(rows_in, 2) + dot(tip_in, q_ref[...])
    p1, a = top[:64], top[64:128] + top[128:]
    p1_tip, a_tip = bottom[:64], bottom[64:128] + bottom[128:]
    tip[1] = -p1_tip
    tip[0] = a_tip
    rows_out[...] = jnp.concatenate([p1, a], axis=0)
    tip_out[...] = jnp.concatenate([p1_tip, a_tip], axis=0)
    at = lax.broadcasted_iota(jnp.int32, (ROWS, BLOCK), 0) + row * ROWS
    on_diagonal = lax.broadcasted_iota(jnp.int32, (ROWS, BLOCK), 1) == at
    carried = sum_shares(shares)
    traced0 = jnp.where(on_diagonal, x_ref[0].astype(F32), 0.0)
    traced0 += z0.astype(F32) * carried + u * a
    traced1 = jnp.where(on_diagonal, x_ref[1].astype(F32), 0.0) + z1.astype(F32) * p1
    traced = traced0 * weight_ref[0] + traced1 * weight_ref[1]
    tip_traced = u_tip * a_tip * weight_ref[0] + z1_tip.astype(F32) * p1_tip * weight_ref[1]
    slope[...] = jnp.full(slope.shape, jnp.sum(traced) + jnp.sum(tip_traced), F32)


def sum_shares(shares):
    total = shares[0, :SHARE, :].astype(F32)
    for d in range(1, SIDE):
        total += shares[d, :SHARE, :].astype(F32)
    return jnp.concatenate([total[:ROWS], total[ROWS:]], axis=1)


def first_kernel(
    got,
    start_ref,
    x_ref,
    rows_ref,
    tip_ref,
    diag,
    lower,
    next_rows,
    next_tip,
    factor,
    shares,
    sem_factor,
    sem_share,
):
    load_share = pltpu.make_async_copy(
        got.at[:, pl.ds(SIDE * EARLY, SHARE)], shares, sem_share
    )
    loads = load_exchanged(got, factor, sem_factor, L1)
    for copy in loads + [load_share]:
        copy.start()
    p1h, p1l = split(rows_ref[:64])
    ah, al = split(rows_ref[64:])
    p1h_tip, p1l_tip = split(tip_ref[:64])
    ah_tip, al_tip = split(tip_ref[64:])
    own_rows, own_tip = start_ref[:, :BLOCK], start_ref[:, BLOCK:]
    for copy in loads + [load_share]:
        copy.wait()
    out = Gathered(factor).times_factor(
        jnp.concatenate([p1h, p1l, ah, al, own_rows], axis=0),
        jnp.concatenate([p1h_tip, p1l_tip, ah_tip, al_tip, own_tip], axis=0),
        0,
    )
    lower[...] = -out[256:]
    sigma1 = x_ref[1].astype(F32) + out[:64] + out[64:128]
    diag[...] = sigma1
    p0 = sum_shares(shares) + out[128:192] + out[192:256]
    p0h, p0l = split(p0)
    next_rows[...] = jnp.concatenate([p0h, p0l, sigma1.astype(BF)], axis=0)
    next_tip[...] = jnp.concatenate([-ah_tip, -al_tip, -p1h_tip], axis=0)


def last_kernel(
    late0,
    late1,
    late2,
    late3,
    x_ref,
    diag1,
    lower1,
    next_rows,
    next_tip,
    diag,
    lower,
    factor,
    sem,
):
    loads = load_shifted((late0, late1, late2, late3), factor, sem)
    for copy in loads:
        copy.start()
    diag[1] = diag1[...]
    lower[1] = lower1[...]
    for copy in loads:
        copy.wait()
    out = Gathered(factor).times_factor(next_rows[...], next_tip[...], 0)
    lower[0] = -out[128:]
    diag[0] = x_ref[0].astype(F32) + out[:64] + out[64:128]


def on_device(
    lower_factor,
    arrow_factor,
    block_inverse,
    boundary_sigma,
    boundary_tip,
    tip_inverse,
    slope_weights,
    partitions,
):
    start = jnp.concatenate([boundary_sigma[0], boundary_tip[0]], axis=1)
    start = lax.ppermute(start, "tm", [(p + 1, p) for p in range(partitions - 1)])
    wide = jnp.concatenate(
        [
            start,
            lower_factor[1],
            arrow_factor[1],
            lower_factor[0],
            arrow_factor[0],
            block_inverse[1],
        ],
        axis=1,
    )
    rows = jnp.concatenate([wide[:, HALF * k : HALF * (k + 1)] for k in range(11)], axis=0)
    rows = jnp.broadcast_to(rows[None], (SIDE, SENT, HALF))
    got = exchange(rows, line_groups(partitions, 0))
    anywhere = pl.BlockSpec(memory_space=pl.ANY)
    fast = pl.BlockSpec(memory_space=pltpu.VMEM)
    params = pltpu.CompilerParams(vmem_limit_bytes=VMEM_BYTES)
    sent, late = pl.pallas_call(
        panel_kernel,
        out_shape=(
            jax.ShapeDtypeStruct((SIDE, SIDE * EARLY + OWN, HALF), BF),
            jax.ShapeDtypeStruct((SIDE * PART, HALF), BF),
        ),
        in_specs=[anywhere],
        out_specs=(anywhere,) * 2,
        scratch_shapes=[
            pltpu.VMEM((SIDE, SENT, HALF), BF),
            pltpu.VMEM((SIDE, OWN, HALF), BF),
            pltpu.SemaphoreType.DMA((SIDE,)),
            pltpu.SemaphoreType.DMA((16,)),
            pltpu.SemaphoreType.DMA((SIDE,)),
            pltpu.SemaphoreType.DMA((SIDE,)),
        ],
        compiler_params=params,
        cost_estimate=cost(12),
    )(got)
    lates = [late] + [lax.ppermute(late, EVERY, line_shift(partitions, k)) for k in range(1, SIDE)]
    early = exchange(sent, line_groups(partitions, 1))
    weights = slope_weights[:, :, None]
    tip, rows_out, tip_out, slope = pl.pallas_call(
        trace_kernel,
        out_shape=(
            jax.ShapeDtypeStruct((2, ROWS, HALF), F32),
            jax.ShapeDtypeStruct((2 * ROWS, BLOCK), F32),
            jax.ShapeDtypeStruct((2 * ROWS, HALF), F32),
            jax.ShapeDtypeStruct((16, 8, 128), F32),
        ),
        in_specs=[anywhere] + [fast] * 4,
        out_specs=(fast,) * 4,
        scratch_shapes=[
            pltpu.VMEM((16, 3 * ROWS, HALF), BF),
            pltpu.VMEM((16, 3 * ROWS, HALF), BF),
            pltpu.VMEM((SIDE, OWN, HALF), BF),
            pltpu.SemaphoreType.DMA((16,)),
            pltpu.SemaphoreType.DMA((16,)),
            pltpu.SemaphoreType.DMA,
        ],
        compiler_params=params,
        cost_estimate=cost(20),
    )(early, arrow_factor, block_inverse, tip_inverse, weights)
    total = jnp.sum(lax.all_to_all(slope, ("y", "x"), 0, 0, tiled=True), axis=0)
    total = jnp.broadcast_to(total[None], (partitions // 2, 8, 128))
    total = jnp.sum(exchange(total, height_groups(partitions)), axis=0)
    other = lax.ppermute(total, "tm", [(p, p ^ 1) for p in range(partitions)])
    diag1, lower1, next_rows, next_tip = pl.pallas_call(
        first_kernel,
        out_shape=(
            jax.ShapeDtypeStruct((ROWS, BLOCK), F32),
            jax.ShapeDtypeStruct((ROWS, BLOCK), F32),
            jax.ShapeDtypeStruct((3 * ROWS, BLOCK), BF),
            jax.ShapeDtypeStruct((3 * ROWS, HALF), BF),
        ),
        in_specs=[anywhere] + [fast] * 4,
        out_specs=(fast,) * 4,
        scratch_shapes=[
            pltpu.VMEM((16, 3 * ROWS, HALF), BF),
            pltpu.VMEM((SIDE, SHARE, HALF), BF),
            pltpu.SemaphoreType.DMA((16,)),
            pltpu.SemaphoreType.DMA,
        ],
        compiler_params=params,
        cost_estimate=cost(15),
    )(early, start, block_inverse, rows_out, tip_out)
    diag, lower = pl.pallas_call(
        last_kernel,
        out_shape=(
            jax.ShapeDtypeStruct((2, ROWS, BLOCK), F32),
            jax.ShapeDtypeStruct((2, ROWS, BLOCK), F32),
        ),
        in_specs=[anywhere] * 4 + [fast] * 5,
        out_specs=(fast,) * 2,
        scratch_shapes=[
            pltpu.VMEM((16, PART, HALF), BF),
            pltpu.SemaphoreType.DMA((16,)),
        ],
        compiler_params=params,
        cost_estimate=cost(15),
    )(*lates, block_inverse, diag1, lower1, next_rows, next_tip)
    return diag, lower, tip, (total + other)[0, 0]


def solution(mesh):
    partitions = mesh.shape["tm"]
    fine = Mesh(mesh.devices.reshape(partitions, SIDE, SIDE), EVERY)
    rows = P("tm", ("y", "x"), None)

    def program(*args):
        return on_device(*args, partitions=partitions)

    return jax.shard_map(
        program,
        mesh=fine,
        in_specs=(rows, rows, rows, rows, rows, P(), P("tm", ("y", "x"))),
        out_specs=(rows, rows, rows, P()),
        check_vma=False,
    )
```

time: 156 us -> 150 us (0.962)
  waiting for transfers between devices: 58.5 us -> 30.3 us
  starting transfers between devices: 20.6 us -> 30.4 us
  Pallas kernels: 14.2 us -> 23 us
  local copies, waits for them, and re-layouts: 4.52 us -> 6.53 us
    all_to_all x1, waiting for transfers between devices: 57.7 us -> 30.3 us  [exchange(): lax.all_to_all(value, EVERY, 0, 0, tiled=True, axis_index_groups=groups)]
    ppermute x0 -> x3, starting transfers between devices: none -> 10.7 us  [on_device(): lax.ppermute(late, EVERY, line_shift(partitions, k))]
    pallas_call x2 -> x4, Pallas kernels: 14.2 us -> 23 us  [the longest x1 7.63 us: on_device(): pl.pallas_call(trace_kernel, out_shape=(jax.ShapeDtypeStruct((2, ROWS, HA...]
    unnamed x16 -> x22, local copies, waits for them, and re-layouts: 1.76 us -> 3.14 us
  transfers between devices with their start and end apart: 3 -> 6, of which waited for: 2 -> 1; matrix products, arithmetic and copies ran while one was open for 1% -> 2% of each run, Pallas kernels for 0% -> 12%
where the time goes in v2:
time: 150 us; the launch traced here: 149 us
  blocking collectives  57.1 us (38%)
  starting transfers between devices  30.4 us (20%)
  waiting for transfers between devices  30.3 us (20%)
  Pallas kernels  23 us (15%)
  local copies, waits for them, and re-layouts  6.53 us (4%)
    all_to_all x2, blocking collectives, exchange(): lax.all_to_all(value, EVERY, 0, 0, tiled=True, axis_index_groups=groups)  47 us
    all_to_all x1, waiting for transfers between devices, exchange(): lax.all_to_all(value, EVERY, 0, 0, tiled=True, axis_index_groups=groups)  30.3 us
    ppermute x3, starting transfers between devices, on_device(): lax.ppermute(late, EVERY, line_shift(partitions, k))  10.7 us
    all_to_all x1, blocking collectives, on_device(): total = jnp.sum(lax.all_to_all(slope, ('y', 'x'), 0, 0, tiled=True), axis=0)  10 us
    ppermute x1, starting transfers between devices, on_device(): lax.ppermute(start, 'tm', [(p + 1, p) for p in range(partitions - 1)])  8.79 us
    pallas_call x1, Pallas kernels, on_device(): pl.pallas_call(trace_kernel, out_shape=(jax.ShapeDtypeStruct((2, ROWS, HA...  7.63 us
    pallas_call x1, Pallas kernels, on_device(): pl.pallas_call(first_kernel, out_shape=(jax.ShapeDtypeStruct((ROWS, BLOCK...  5.69 us
    all_to_all x1, starting transfers between devices, exchange(): lax.all_to_all(value, EVERY, 0, 0, tiled=True, axis_index_groups=groups)  5.51 us
  transfers between devices with their start and end apart: 6, of which 1 were waited for; matrix products, arithmetic and copies ran while one was open for 2% of the time, Pallas kernels for 12%

profile of v2, /device:TPU:1, one launch (start us, length us, event | category | flops | bytes accessed | tf_op | source)
XLA Modules:
  0.0 149.2 jit_solution(3500446352528200242)
XLA Ops:
  0.6 1.0 pad_maximum_fusion
  1.6 8.8 %collective-permute-start = (bf16[64,1536]{1,0:T(8,128)(2,1)S(1)}, bf16[64,1536]{1,0:T(8,128)(2,1)S(1)}, u32[]{:S(2)}, u32[]{:S(2)}) collective-permute-start(bf16[64,1536]{1,0:T(8,128)(2,1)S(1)} %pad_maximum_fusion), channel_id=1, source_target_pairs={{16,0},{32,16},{48,32},{64,48},{80,64},{96,80},{112,96},{128,112},... | collective-permute-start | bytes 589832 | tf_op jit(solution)/shard_map/ppermute | solution.py:347
  10.4 1.0 slice_bitcast_fusion.1
  11.4 0.9 slice_bitcast_fusion
  12.4 0.8 bitcast_dynamic-update-slice_fusion.1
  13.3 0.8 bitcast_dynamic-update-slice_fusion
  14.4 23.1 %all_to_all.20.got = bf16[4,704,512]{2,1,0:T(8,128)(2,1)} all-to-all(bf16[4,704,512]{2,1,0:T(8,128)(2,1)S(1)} %broadcast_in_dim.6), channel_id=1, replica_groups={{0,1,2,3},{4,5,6,7},{8,9,10,11},{12,13,14,15},{16,20,24,28},{17,21,25,2..., dimensions={0} | all-to-all | bytes 5767168 | tf_op jit(solution)/shard_map/all_to_all | solution.py:62
  37.5 4.5 %shard_map.102 = (bf16[4,1696,512]{2,1,0:T(8,128)(2,1)}, bf16[768,512]{1,0:T(8,128)(2,1)}) custom-call(bf16[4,704,512]{2,1,0:T(8,128)(2,1)} %all_to_all.20.got), custom_call_target="tpu_custom_call" | custom-call | bytes 12000000 | tf_op jit(solution)/shard_map/pallas_call | solution.py:365
  42.0 5.5 %all-to-all-start.1 = ((bf16[4,1696,512]{2,1,0:T(8,128)(2,1)}), bf16[4,1696,512]{2,1,0:T(8,128)(2,1)}, u32[]{:S(2)}, u32[]{:S(2)}) async-start(bf16[4,1696,512]{2,1,0:T(8,128)(2,1)} %get-tuple-element.17), calls=%async_computation.1 | async-start | bytes 13893632 | tf_op jit(solution)/shard_map/all_to_all | solution.py:62
  47.5 3.3 %collective-permute-start.1 = (bf16[768,512]{1,0:T(8,128)(2,1)S(1)}, bf16[768,512]{1,0:T(8,128)(2,1)S(1)}, u32[]{:S(2)}, u32[]{:S(2)}) collective-permute-start(bf16[768,512]{1,0:T(8,128)(2,1)S(1)} %copy-done), channel_id=1, source_target_pairs={{0,4},{1,5},{2,6},{3,7},{4,8},{5,9},{6,10},{7,11},{8,12},{9,13},{1... | collective-permute-start | bytes 2359304 | tf_op jit(solution)/shard_map/ppermute | solution.py:384
  50.8 4.3 %collective-permute-start.2 = (bf16[768,512]{1,0:T(8,128)(2,1)S(1)}, bf16[768,512]{1,0:T(8,128)(2,1)S(1)}, u32[]{:S(2)}, u32[]{:S(2)}) collective-permute-start(bf16[768,512]{1,0:T(8,128)(2,1)S(1)} %copy-done), channel_id=1, source_target_pairs={{0,8},{1,9},{2,10},{3,11},{4,12},{5,13},{6,14},{7,15},{8,0},{9,1},... | collective-permute-start | bytes 2359304 | tf_op jit(solution)/shard_map/ppermute | solution.py:384
  55.1 3.1 %collective-permute-start.3 = (bf16[768,512]{1,0:T(8,128)(2,1)S(1)}, bf16[768,512]{1,0:T(8,128)(2,1)S(1)}, u32[]{:S(2)}, u32[]{:S(2)}) collective-permute-start(bf16[768,512]{1,0:T(8,128)(2,1)S(1)} %copy-done), channel_id=1, source_target_pairs={{0,12},{1,13},{2,14},{3,15},{4,0},{5,1},{6,2},{7,3},{8,4},{9,5},{1... | collective-permute-start | bytes 2359304 | tf_op jit(solution)/shard_map/ppermute | solution.py:384
  58.2 0.7 copy.12.weight_ref
  59.0 30.3 %all-to-all-done.1.got = bf16[4,1696,512]{2,1,0:T(8,128)(2,1)} async-done(((bf16[4,1696,512]{2,1,0:T(8,128)(2,1)}), bf16[4,1696,512]{2,1,0:T(8,128)(2,1)}, u32[]{:S(2)}, u32[]{:S(2)}) %all-to-all-start.1) | async-done | bytes 6946848 | tf_op jit(solution)/shard_map/all_to_all | solution.py:62
  89.3 7.6 %shard_map.103 = (f32[2,64,512]{2,1,0:T(8,128)}, f32[128,1024]{1,0:T(8,128)}, f32[128,512]{1,0:T(8,128)}, f32[16,8,128]{2,1,0:T(8,128)}) custom-call(bf16[4,1696,512]{2,1,0:T(8,128)(2,1)} %all-to-all-done.1.got, bf16[2,64,512]{2,1,0:T(8,128)(2,1)} %arrow_ref.1, bf16[2,64,1024]{2,1,0:T(8,128)(2,1)} %x_ref.5, bf16[512,512]{1,0:T(8,128)(2,1)} %q_ref.1, ...), custom_call_target="tpu_custom_call" | custom-call | bytes 20000000 | tf_op jit(solution)/shard_map/pallas_call | solution.py:387
  96.9 10.0 %all_to_all.21 = f32[16,8,128]{2,1,0:T(8,128)S(1)} all-to-all(f32[16,8,128]{2,1,0:T(8,128)} %get-tuple-element.27), channel_id=1, replica_groups=mesh['tm'=32,'y'=4,'x'=4] {'y','x'}, dimensions={0} | all-to-all | bytes 131072 | tf_op jit(solution)/shard_map/all_to_all | solution.py:408
  106.9 23.9 %all_to_all.22 = f32[16,8,128]{2,1,0:T(8,128)S(1)} all-to-all(f32[16,8,128]{2,1,0:T(8,128)S(1)} %broadcast_in_dim.8), channel_id=1, replica_groups={{0,32,64,96,128,160,192,224,256,288,320,352,384,416,448,480},{1,33,65,9..., dimensions={0} | all-to-all | bytes 131072 | tf_op jit(solution)/shard_map/all_to_all | solution.py:62
  130.9 5.5 %collective-permute-start.4 = (f32[8,128]{1,0:T(8,128)S(1)}, f32[8,128]{1,0:T(8,128)S(1)}, u32[]{:S(2)}, u32[]{:S(2)}) collective-permute-start(f32[8,128]{1,0:T(8,128)S(1)} %reduce_sum.19), channel_id=1, source_target_pairs={{0,16},{16,0},{32,48},{48,32},{64,80},{80,64},{96,112},{112,96},{1... | collective-permute-start | bytes 12296 | tf_op jit(solution)/shard_map/ppermute | solution.py:411
  136.3 5.7 %shard_map.104 = (f32[64,1024]{1,0:T(8,128)}, f32[64,1024]{1,0:T(8,128)}, bf16[192,1024]{1,0:T(8,128)(2,1)}, bf16[192,512]{1,0:T(8,128)(2,1)}) custom-call(bf16[4,1696,512]{2,1,0:T(8,128)(2,1)} %all-to-all-done.1.got, bf16[64,1536]{1,0:T(8,128)(2,1)} %copy-done.4, bf16[2,64,1024]{2,1,0:T(8,128)(2,1)} %x_ref.5, f32[128,1024]{1,0:T(8,128)} %get-tuple-element.18.rows_ref, ...), custom_call_target="tpu_custom_call" | custom-call | bytes 15000000 | tf_op jit(solution)/shard_map/pallas_call | solution.py:412
  142.1 0.8 copy-done.1
  142.9 0.3 copy-done.2
  143.2 0.3 copy-done.3
  143.5 5.2 %shard_map.105 = (f32[2,64,1024]{2,1,0:T(8,128)}, f32[2,64,1024]{2,1,0:T(8,128)}) custom-call(bf16[768,512]{1,0:T(8,128)(2,1)} %get-tuple-element.16.late0, bf16[768,512]{1,0:T(8,128)(2,1)} %copy-done.1, bf16[768,512]{1,0:T(8,128)(2,1)} %copy-done.2, bf16[768,512]{1,0:T(8,128)(2,1)} %copy-done.3, bf16[2,64,1024]{2,1,0:T(8,128)(2,1)} %x_ref.5, ...), custom_call_target="tpu_custom_call" | custom-call | bytes 15000000 | tf_op jit(solution)/shard_map/pallas_call | solution.py:431
  148.7 0.5 slice.59
  (28 shorter events, 0.4 us)
Async XLA Ops:
  1.6 10.7 %collective-permute-start = (bf16[64,1536]{1,0:T(8,128)(2,1)S(1)}, bf16[64,1536]{1,0:T(8,128)(2,1)S(1)}, u32[]{:S(2)}, u32[]{:S(2)}) collective-permute-start(bf16[64,1536]{1,0:T(8,128)(2,1)S(1)} %pad_maximum_fusion), channel_id=1, source_target_pairs={{16,0},{32,16},{48,32},{64,48},{80,64},{96,80},{112,96},{128,112},... | collective-permute-start | bytes 589832 | tf_op jit(solution)/shard_map/ppermute | solution.py:347
  12.3 29.7 %copy-start.4 = (bf16[64,1536]{1,0:T(8,128)(2,1)}, bf16[64,1536]{1,0:T(8,128)(2,1)S(1)}, u32[]{:S(2)}) copy-start(bf16[64,1536]{1,0:T(8,128)(2,1)S(1)} %collective-permute-done.start_ref) | copy-start | bytes 589828
  42.0 5.6 %copy-start = (bf16[768,512]{1,0:T(8,128)(2,1)S(1)}, bf16[768,512]{1,0:T(8,128)(2,1)}, u32[]{:S(2)}) copy-start(bf16[768,512]{1,0:T(8,128)(2,1)} %get-tuple-element.16.late0) | copy-start | bytes 2359300
  42.0 16.3 %copy-start.5 = (f32[2,64]{1,0:T(2,128)S(1)}, f32[2,64]{1,0:T(2,128)}, u32[]{:S(2)}) copy-start(f32[2,64]{1,0:T(2,128)} %param.13) | copy-start | bytes 1540
  42.0 47.3 %all-to-all-start.1 = ((bf16[4,1696,512]{2,1,0:T(8,128)(2,1)}), bf16[4,1696,512]{2,1,0:T(8,128)(2,1)}, u32[]{:S(2)}, u32[]{:S(2)}) async-start(bf16[4,1696,512]{2,1,0:T(8,128)(2,1)} %get-tuple-element.17), calls=%async_computation.1 | async-start | bytes 13893632 | tf_op jit(solution)/shard_map/all_to_all | solution.py:62
  47.5 94.5 %collective-permute-start.1 = (bf16[768,512]{1,0:T(8,128)(2,1)S(1)}, bf16[768,512]{1,0:T(8,128)(2,1)S(1)}, u32[]{:S(2)}, u32[]{:S(2)}) collective-permute-start(bf16[768,512]{1,0:T(8,128)(2,1)S(1)} %copy-done), channel_id=1, source_target_pairs={{0,4},{1,5},{2,6},{3,7},{4,8},{5,9},{6,10},{7,11},{8,12},{9,13},{1... | collective-permute-start | bytes 2359304 | tf_op jit(solution)/shard_map/ppermute | solution.py:384
  50.8 91.2 %collective-permute-start.2 = (bf16[768,512]{1,0:T(8,128)(2,1)S(1)}, bf16[768,512]{1,0:T(8,128)(2,1)S(1)}, u32[]{:S(2)}, u32[]{:S(2)}) collective-permute-start(bf16[768,512]{1,0:T(8,128)(2,1)S(1)} %copy-done), channel_id=1, source_target_pairs={{0,8},{1,9},{2,10},{3,11},{4,12},{5,13},{6,14},{7,15},{8,0},{9,1},... | collective-permute-start | bytes 2359304 | tf_op jit(solution)/shard_map/ppermute | solution.py:384
  55.1 86.9 %collective-permute-start.3 = (bf16[768,512]{1,0:T(8,128)(2,1)S(1)}, bf16[768,512]{1,0:T(8,128)(2,1)S(1)}, u32[]{:S(2)}, u32[]{:S(2)}) collective-permute-start(bf16[768,512]{1,0:T(8,128)(2,1)S(1)} %copy-done), channel_id=1, source_target_pairs={{0,12},{1,13},{2,14},{3,15},{4,0},{5,1},{6,2},{7,3},{8,4},{9,5},{1... | collective-permute-start | bytes 2359304 | tf_op jit(solution)/shard_map/ppermute | solution.py:384
  130.9 17.8 %collective-permute-start.4 = (f32[8,128]{1,0:T(8,128)S(1)}, f32[8,128]{1,0:T(8,128)S(1)}, u32[]{:S(2)}, u32[]{:S(2)}) collective-permute-start(f32[8,128]{1,0:T(8,128)S(1)} %reduce_sum.19), channel_id=1, source_target_pairs={{0,16},{16,0},{32,48},{48,32},{64,80},{80,64},{96,112},{112,96},{1... | collective-permute-start | bytes 12296 | tf_op jit(solution)/shard_map/ppermute | solution.py:411
  142.0 0.9 copy-start.1
  142.1 1.1 copy-start.2
  142.1 1.4 copy-start.3

commit v3 on v2

v3 whole, which is shorter than its diff:
```python
import functools

import jax
import jax.numpy as jnp
from jax import lax
from jax.experimental import pallas as pl
from jax.experimental.pallas import tpu as pltpu
from jax.sharding import Mesh, PartitionSpec as P

SIDE = 4
ROWS = 64
HALF = 512
BLOCK = 1024
BF = jnp.bfloat16
F32 = jnp.float32
EVERY = ("tm", "y", "x")

L1, M1, L0, M0, X1 = 0, 2, 3, 5, 6
PART = 3 * ROWS
EARLY = 2 * PART
SENT = 8 * ROWS
SHARE = 2 * ROWS
OWN = SHARE + 32
VMEM_BYTES = 127 * 512 * 1024


def line_groups(partitions, phase):
    groups = []
    for t in range(partitions):
        base = t * SIDE * SIDE
        for i in range(SIDE):
            if (t + phase) % 2 == 0:
                groups.append([base + SIDE * i + x for x in range(SIDE)])
            else:
                groups.append([base + SIDE * y + i for y in range(SIDE)])
    return groups


def plane_groups(partitions):
    plane = 2 * SIDE * SIDE
    return [[z * plane + r for r in range(plane)] for z in range(partitions // 2)]


def height_groups(partitions):
    plane = SIDE * SIDE
    return [
        [t * plane + r for t in range(core, partitions, 2)]
        for core in range(2)
        for r in range(plane)
    ]


def state_shift(partitions, steps):
    pairs = []
    for t in range(partitions - 1):
        for y in range(SIDE):
            for x in range(SIDE):
                to = (y, (x + steps) % SIDE) if t % 2 == 0 else ((y + steps) % SIDE, x)
                source = (t + 1) * SIDE * SIDE + SIDE * y + x
                pairs.append((source, t * SIDE * SIDE + SIDE * to[0] + to[1]))
    return pairs


def line_shift(partitions, steps):
    pairs = []
    for t in range(partitions):
        for y in range(SIDE):
            for x in range(SIDE):
                to = ((y + steps) % SIDE, x) if t % 2 == 0 else (y, (x + steps) % SIDE)
                base = t * SIDE * SIDE
                pairs.append((base + SIDE * y + x, base + SIDE * to[0] + to[1]))
    return pairs


def cost(megabytes):
    return pl.CostEstimate(flops=0, bytes_accessed=megabytes * 1_000_000, transcendentals=0)


def exchange(value, groups):
    return lax.all_to_all(value, EVERY, 0, 0, tiled=True, axis_index_groups=groups)


def dot(left, right):
    return jnp.dot(left, right, preferred_element_type=F32)


def dot_t(left, right):
    return lax.dot_general(left, right, (((1,), (1,)), ((), ())), preferred_element_type=F32)


def split(value):
    high = value.astype(BF)
    return high, (value - high.astype(F32)).astype(BF)


def place():
    core = lax.rem(lax.axis_index("tm"), 2)
    y, x = lax.axis_index("y"), lax.axis_index("x")
    first = jnp.where(core == 0, x, y)
    return core, y * SIDE + x, first


def natural(core, second, first):
    return jnp.where(core == 0, SIDE * second + first, SIDE * first + second)


def columns_t(ref, piece, row):
    half = lax.div(row, 8)
    lane = lax.div(lax.rem(row, 8), 2)
    window = ref[
        :,
        pl.ds(pl.multiple_of((piece + half) * ROWS, ROWS), ROWS),
        pl.ds(pl.multiple_of(lane * 128, 128), 128),
    ]
    window = window.reshape(window.shape[0] * ROWS, 128)
    want = lax.broadcasted_iota(jnp.int32, (ROWS, 128), 0) + lax.rem(row, 2) * ROWS
    pick = jnp.where(lax.broadcasted_iota(jnp.int32, (ROWS, 128), 1) == want, 1.0, 0.0)
    return dot_t(pick.astype(BF), window).astype(BF)


def pack_kernel(low, arrow, inverse, sigma, tip, out, start, held, own, sem_in, sem_own, sem_out):
    loads = []
    for k, (ref, j, h) in enumerate(
        [(low, 1, 0), (low, 1, 1), (arrow, 1, 0), (low, 0, 0), (low, 0, 1), (arrow, 0, 0)]
        + [(inverse, 1, 0), (inverse, 1, 1)]
    ):
        loads.append(
            pltpu.make_async_copy(
                ref.at[j, :, pl.ds(h * HALF, HALF)],
                held.at[pl.ds(k * ROWS, ROWS)],
                sem_in.at[k],
            )
        )
    loads_own = [
        pltpu.make_async_copy(sigma.at[0], own.at[:, pl.ds(0, BLOCK)], sem_own.at[0]),
        pltpu.make_async_copy(tip.at[0], own.at[:, pl.ds(BLOCK, HALF)], sem_own.at[1]),
    ]
    for copy in loads + loads_own:
        copy.start()
    for copy in loads + loads_own:
        copy.wait()
    stores = [pltpu.make_async_copy(held, out.at[d], sem_out.at[d]) for d in range(SIDE)]
    stores.append(pltpu.make_async_copy(own, start, sem_out.at[SIDE]))
    for copy in stores:
        copy.start()
    for copy in stores:
        copy.wait()


def state_kernel(steps, *refs):
    count = len(steps)
    owns = refs[:count]
    out, held, sem_in, sem_out = refs[-4:]
    _, _, first = place()
    loads = [pltpu.make_async_copy(owns[i], held.at[i], sem_in.at[i]) for i in range(count)]
    for copy in loads:
        copy.start()
    stores = []
    for i, k in enumerate(steps):
        loads[i].wait()
        j = lax.rem(first + SIDE - k, SIDE)
        here = []
        for d in range(SIDE):
            for h in range(3):
                at = pl.multiple_of(j * EARLY + h * ROWS, ROWS)
                here.append(
                    pltpu.make_async_copy(
                        held.at[i, :, pl.ds(h * HALF, HALF)],
                        out.at[d, pl.ds(at, ROWS)],
                        sem_out.at[(i * SIDE + d) * 3 + h],
                    )
                )
        for copy in here:
            copy.start()
        stores += here
    for copy in stores:
        copy.wait()


def panel_kernel(got, begun, out, out_late, panel, mine, sem_in, sem_out, sem_late, sem_mine):
    del begun
    core, _, first = place()
    loads = [pltpu.make_async_copy(got.at[j], panel.at[j], sem_in.at[j]) for j in range(SIDE)]
    for copy in loads:
        copy.start()
    stores = []
    for j in range(SIDE):
        loads[j].wait()
        here = [
            pltpu.make_async_copy(
                panel.at[j, pl.ds(0, PART)],
                out.at[d, pl.ds(j * EARLY + PART, PART)],
                sem_out.at[d * SIDE + j],
            )
            for d in range(SIDE)
        ]
        here.append(
            pltpu.make_async_copy(
                panel.at[j, pl.ds(PART, PART)],
                out_late.at[pl.ds(j * PART, PART)],
                sem_late.at[j],
            )
        )
        for copy in here:
            copy.start()
        stores += here
    cols = [columns_t(panel, L0, natural(core, d, first)) for d in range(SIDE)]
    for d in range(SIDE):
        mine[d, SHARE:, :] = jnp.concatenate([cols[d][:32], cols[d][32:]], axis=1)
    cols = jnp.concatenate(cols, axis=0)
    for h in range(2):
        at = (X1 + h) * ROWS
        part = dot(cols, panel[:, at : at + ROWS, :].reshape(SIDE * ROWS, HALF))
        for d in range(SIDE):
            mine[d, h * ROWS : (h + 1) * ROWS, :] = part[d * ROWS : (d + 1) * ROWS].astype(BF)
    stores_mine = [
        pltpu.make_async_copy(mine.at[d], out.at[d, pl.ds(SIDE * EARLY, OWN)], sem_mine.at[d])
        for d in range(SIDE)
    ]
    for copy in stores_mine:
        copy.start()
    for copy in stores + stores_mine:
        copy.wait()


class Gathered:
    def __init__(self, mat):
        self.mat = mat

    def piece(self, k):
        return self.mat[:, k * ROWS : (k + 1) * ROWS, :].reshape(BLOCK, HALF)

    def over_rows(self, left, k):
        return dot(left, self.piece(k))

    def over_columns(self, left, k):
        return dot_t(left, self.piece(k))

    def times_factor(self, left_rows, left_tip, k):
        both = jnp.concatenate([self.over_rows(left_rows, k + h) for h in range(2)], axis=1)
        return both + self.over_columns(left_tip, k + 2)


def load_exchanged(got, mat, sem, piece):
    core, _, _ = place()
    return [
        pltpu.make_async_copy(
            got.at[d, pl.ds(j * EARLY + piece * ROWS, PART)],
            mat.at[natural(core, d, j)],
            sem.at[d * SIDE + j],
        )
        for d in range(SIDE)
        for j in range(SIDE)
    ]


def load_shifted(panels, mat, sem):
    core, _, _ = place()
    second = jnp.where(core == 0, lax.axis_index("y"), lax.axis_index("x"))
    return [
        pltpu.make_async_copy(
            panel.at[pl.ds(j * PART, PART)],
            mat.at[natural(core, lax.rem(second + SIDE - k, SIDE), j)],
            sem.at[k * SIDE + j],
        )
        for k, panel in enumerate(panels)
        for j in range(SIDE)
    ]


def sum_shares(shares):
    total = shares[0, :SHARE, :].astype(F32)
    for d in range(1, SIDE):
        total += shares[d, :SHARE, :].astype(F32)
    return jnp.concatenate([total[:ROWS], total[ROWS:]], axis=1)


def trace_kernel(
    got,
    arrow_ref,
    x_ref,
    q_ref,
    weight_ref,
    tip_ref,
    rows_ref,
    rows_tip_ref,
    slope_ref,
    factor,
    state,
    shares,
    arrow,
    x,
    q,
    weight,
    tip,
    rows,
    rows_tip,
    slope,
    sem_factor,
    sem_state,
    sem_in,
    sem_out,
):
    core, row, _ = place()
    load_share = pltpu.make_async_copy(got.at[:, pl.ds(SIDE * EARLY, OWN)], shares, sem_in.at[0])
    load_arrow = pltpu.make_async_copy(arrow_ref, arrow, sem_in.at[1])
    load_x = pltpu.make_async_copy(x_ref, x, sem_in.at[2])
    load_q = pltpu.make_async_copy(q_ref, q, sem_in.at[3])
    load_weight = pltpu.make_async_copy(weight_ref, weight, sem_in.at[4])
    load_factor = load_exchanged(got, factor, sem_factor, 3)
    load_state = load_exchanged(got, state, sem_state, 0)
    at_once = [load_share, load_arrow] + load_factor
    for copy in at_once + load_state + [load_q, load_x, load_weight]:
        copy.start()
    for copy in at_once:
        copy.wait()
    have = Gathered(factor)
    z1 = columns_t(factor, 0, row)
    z1_tip, z0_tip = arrow[1], arrow[0]
    parts = []
    for d in range(SIDE):
        held = shares[d, SHARE:, :]
        parts.append(jnp.concatenate([held[:, :256], held[:, 256:]], axis=0))
    even = jnp.concatenate(parts, axis=1)
    odd = [parts[d][:, j * 64 : (j + 1) * 64] for j in range(SIDE) for d in range(SIDE)]
    z0 = jnp.where(core == 0, even, jnp.concatenate(odd, axis=1))
    u = have.over_columns(z0[:, :HALF], 0) + have.over_columns(z0[:, HALF:], 1)
    u_tip = have.over_rows(z0, 2) - z0_tip.astype(F32)
    uh, ul = split(u)
    uh_tip, ul_tip = split(u_tip)
    rows_in = jnp.concatenate([z1, uh, ul], axis=0)
    tip_in = jnp.concatenate([z1_tip, uh_tip, ul_tip], axis=0)
    for copy in load_state + [load_q]:
        copy.wait()
    have = Gathered(state)
    top = have.times_factor(rows_in, tip_in, 0)
    bottom = have.over_rows(rows_in, 2) + dot(tip_in, q[...])
    p1, a = top[:64], top[64:128] + top[128:]
    p1_tip, a_tip = bottom[:64], bottom[64:128] + bottom[128:]
    tip[1] = -p1_tip
    tip[0] = a_tip
    rows[...] = jnp.concatenate([p1, a], axis=0)
    rows_tip[...] = jnp.concatenate([p1_tip, a_tip], axis=0)
    stores = [
        pltpu.make_async_copy(rows, rows_ref, sem_out.at[0]),
        pltpu.make_async_copy(rows_tip, rows_tip_ref, sem_out.at[1]),
        pltpu.make_async_copy(tip, tip_ref, sem_out.at[2]),
    ]
    for copy in stores:
        copy.start()
    at = lax.broadcasted_iota(jnp.int32, (ROWS, BLOCK), 0) + row * ROWS
    on_diagonal = lax.broadcasted_iota(jnp.int32, (ROWS, BLOCK), 1) == at
    load_x.wait()
    load_weight.wait()
    traced0 = jnp.where(on_diagonal, x[0].astype(F32), 0.0)
    traced0 += z0.astype(F32) * sum_shares(shares) + u * a
    traced1 = jnp.where(on_diagonal, x[1].astype(F32), 0.0) + z1.astype(F32) * p1
    traced = traced0 * weight[0] + traced1 * weight[1]
    tip_traced = u_tip * a_tip * weight[0] + z1_tip.astype(F32) * p1_tip * weight[1]
    slope[...] = jnp.full(slope.shape, jnp.sum(traced) + jnp.sum(tip_traced), F32)
    stores.append(pltpu.make_async_copy(slope, slope_ref, sem_out.at[3]))
    stores[-1].start()
    for copy in stores:
        copy.wait()


def block_kernel(
    got,
    late0,
    late1,
    late2,
    late3,
    start_ref,
    x_ref,
    rows_ref,
    rows_tip_ref,
    diag_ref,
    lower_ref,
    factor1,
    factor0,
    shares,
    start,
    x,
    rows,
    rows_tip,
    diag,
    lower,
    sem_factor1,
    sem_factor0,
    sem_in,
    sem_out,
):
    loads = [
        pltpu.make_async_copy(rows_ref, rows, sem_in.at[0]),
        pltpu.make_async_copy(rows_tip_ref, rows_tip, sem_in.at[1]),
        pltpu.make_async_copy(start_ref, start, sem_in.at[2]),
        pltpu.make_async_copy(x_ref, x, sem_in.at[3]),
        pltpu.make_async_copy(got.at[:, pl.ds(SIDE * EARLY, SHARE)], shares, sem_in.at[4]),
    ]
    loads1 = load_exchanged(got, factor1, sem_factor1, 3)
    loads0 = load_shifted((late0, late1, late2, late3), factor0, sem_factor0)
    for copy in loads[:3] + loads1 + loads[3:] + loads0:
        copy.start()
    for copy in loads[:3]:
        copy.wait()
    p1h, p1l = split(rows[:64])
    ah, al = split(rows[64:])
    p1h_tip, p1l_tip = split(rows_tip[:64])
    ah_tip, al_tip = split(rows_tip[64:])
    for copy in loads1 + loads[3:]:
        copy.wait()
    out = Gathered(factor1).times_factor(
        jnp.concatenate([p1h, p1l, ah, al, start[:, :BLOCK]], axis=0),
        jnp.concatenate([p1h_tip, p1l_tip, ah_tip, al_tip, start[:, BLOCK:]], axis=0),
        0,
    )
    lower[1] = -out[256:]
    sigma1 = x[1].astype(F32) + out[:64] + out[64:128]
    diag[1] = sigma1
    stores = [
        pltpu.make_async_copy(diag.at[1], diag_ref.at[1], sem_out.at[0]),
        pltpu.make_async_copy(lower.at[1], lower_ref.at[1], sem_out.at[1]),
    ]
    for copy in stores:
        copy.start()
    p0h, p0l = split(sum_shares(shares) + out[128:192] + out[192:256])
    for copy in loads0:
        copy.wait()
    out = Gathered(factor0).times_factor(
        jnp.concatenate([p0h, p0l, sigma1.astype(BF)], axis=0),
        jnp.concatenate([-ah_tip, -al_tip, -p1h_tip], axis=0),
        0,
    )
    lower[0] = -out[128:]
    diag[0] = x[0].astype(F32) + out[:64] + out[64:128]
    more = [
        pltpu.make_async_copy(diag.at[0], diag_ref.at[0], sem_out.at[2]),
        pltpu.make_async_copy(lower.at[0], lower_ref.at[0], sem_out.at[3]),
    ]
    for copy in more:
        copy.start()
    for copy in stores + more:
        copy.wait()


def on_device(
    lower_factor,
    arrow_factor,
    block_inverse,
    boundary_sigma,
    boundary_tip,
    tip_inverse,
    slope_weights,
    partitions,
):
    slow = pl.BlockSpec(memory_space=pltpu.HBM)
    params = pltpu.CompilerParams(vmem_limit_bytes=VMEM_BYTES)
    rows, start = pl.pallas_call(
        pack_kernel,
        out_shape=(
            jax.ShapeDtypeStruct((SIDE, SENT, HALF), BF),
            jax.ShapeDtypeStruct((ROWS, BLOCK + HALF), BF),
        ),
        in_specs=[slow] * 5,
        out_specs=(slow,) * 2,
        scratch_shapes=[
            pltpu.VMEM((SENT, HALF), BF),
            pltpu.VMEM((ROWS, BLOCK + HALF), BF),
            pltpu.SemaphoreType.DMA((8,)),
            pltpu.SemaphoreType.DMA((2,)),
            pltpu.SemaphoreType.DMA((SIDE + 1,)),
        ],
        compiler_params=params,
        cost_estimate=cost(4),
    )(lower_factor, arrow_factor, block_inverse, boundary_sigma, boundary_tip)
    got = exchange(rows, line_groups(partitions, 0))
    starts = [lax.ppermute(start, EVERY, state_shift(partitions, k)) for k in range(SIDE)]
    begun = []
    for steps in ((0, 1), (2, 3)):
        count = len(steps)
        begun = [
            pl.pallas_call(
                functools.partial(state_kernel, steps),
                out_shape=jax.ShapeDtypeStruct((SIDE, SIDE * EARLY + OWN, HALF), BF),
                in_specs=[slow] * (count + len(begun)),
                out_specs=slow,
                input_output_aliases={count: 0} if begun else {},
                scratch_shapes=[
                    pltpu.VMEM((count, ROWS, BLOCK + HALF), BF),
                    pltpu.SemaphoreType.DMA((count,)),
                    pltpu.SemaphoreType.DMA((count * SIDE * 3,)),
                ],
                compiler_params=params,
                cost_estimate=cost(8),
            )(*[starts[k] for k in steps], *begun)
        ]
    sent, late = pl.pallas_call(
        panel_kernel,
        out_shape=(
            jax.ShapeDtypeStruct((SIDE, SIDE * EARLY + OWN, HALF), BF),
            jax.ShapeDtypeStruct((SIDE * PART, HALF), BF),
        ),
        in_specs=[slow] * 2,
        out_specs=(slow,) * 2,
        input_output_aliases={1: 0},
        scratch_shapes=[
            pltpu.VMEM((SIDE, SENT, HALF), BF),
            pltpu.VMEM((SIDE, OWN, HALF), BF),
            pltpu.SemaphoreType.DMA((SIDE,)),
            pltpu.SemaphoreType.DMA((16,)),
            pltpu.SemaphoreType.DMA((SIDE,)),
            pltpu.SemaphoreType.DMA((SIDE,)),
        ],
        compiler_params=params,
        cost_estimate=cost(12),
    )(got, *begun)
    lates = [late] + [lax.ppermute(late, EVERY, line_shift(partitions, k)) for k in range(1, SIDE)]
    early = exchange(sent, line_groups(partitions, 1))
    weights = slope_weights[:, :, None]
    outputs = (
        jax.ShapeDtypeStruct((2, ROWS, HALF), F32),
        jax.ShapeDtypeStruct((2 * ROWS, BLOCK), F32),
        jax.ShapeDtypeStruct((2 * ROWS, HALF), F32),
        jax.ShapeDtypeStruct((32, 8, 128), F32),
    )
    tip, rows, rows_tip, slope = pl.pallas_call(
        trace_kernel,
        out_shape=outputs,
        in_specs=[slow] * 5,
        out_specs=(slow,) * 4,
        scratch_shapes=[
            pltpu.VMEM((16, PART, HALF), BF),
            pltpu.VMEM((16, PART, HALF), BF),
            pltpu.VMEM((SIDE, OWN, HALF), BF),
            pltpu.VMEM((2, ROWS, HALF), BF),
            pltpu.VMEM((2, ROWS, BLOCK), BF),
            pltpu.VMEM((HALF, HALF), BF),
            pltpu.VMEM((2, ROWS, 1), F32),
        ]
        + [pltpu.VMEM(leaf.shape, F32) for leaf in outputs]
        + [
            pltpu.SemaphoreType.DMA((16,)),
            pltpu.SemaphoreType.DMA((16,)),
            pltpu.SemaphoreType.DMA((5,)),
            pltpu.SemaphoreType.DMA((4,)),
        ],
        compiler_params=params,
        cost_estimate=cost(20),
    )(early, arrow_factor, block_inverse, tip_inverse, weights)
    total = jnp.sum(exchange(slope, plane_groups(partitions)), axis=0)
    total = jnp.broadcast_to(total[None], (partitions // 2, 8, 128))
    total = jnp.sum(exchange(total, height_groups(partitions)), axis=0)
    diag, lower = pl.pallas_call(
        block_kernel,
        out_shape=(
            jax.ShapeDtypeStruct((2, ROWS, BLOCK), F32),
            jax.ShapeDtypeStruct((2, ROWS, BLOCK), F32),
        ),
        in_specs=[slow] * 9,
        out_specs=(slow,) * 2,
        scratch_shapes=[
            pltpu.VMEM((16, PART, HALF), BF),
            pltpu.VMEM((16, PART, HALF), BF),
            pltpu.VMEM((SIDE, SHARE, HALF), BF),
            pltpu.VMEM((ROWS, BLOCK + HALF), BF),
            pltpu.VMEM((2, ROWS, BLOCK), BF),
            pltpu.VMEM((2 * ROWS, BLOCK), F32),
            pltpu.VMEM((2 * ROWS, HALF), F32),
            pltpu.VMEM((2, ROWS, BLOCK), F32),
            pltpu.VMEM((2, ROWS, BLOCK), F32),
            pltpu.SemaphoreType.DMA((16,)),
            pltpu.SemaphoreType.DMA((16,)),
            pltpu.SemaphoreType.DMA((5,)),
            pltpu.SemaphoreType.DMA((4,)),
        ],
        compiler_params=params,
        cost_estimate=cost(20),
    )(early, *lates, starts[0], block_inverse, rows, rows_tip)
    return diag, lower, tip, total[0, 0]


def solution(mesh):
    partitions = mesh.shape["tm"]
    fine = Mesh(mesh.devices.reshape(partitions, SIDE, SIDE), EVERY)
    rows = P("tm", ("y", "x"), None)

    def program(*args):
        return on_device(*args, partitions=partitions)

    return jax.shard_map(
        program,
        mesh=fine,
        in_specs=(rows, rows, rows, rows, rows, P(), P("tm", ("y", "x"))),
        out_specs=(rows, rows, rows, P()),
        check_vma=False,
    )
```

time: 150 us -> 132 us (0.88)
  blocking collectives: 57.1 us -> 17.7 us
  starting transfers between devices: 30.4 us -> 48.4 us
  waiting for transfers between devices: 30.3 us -> 38.5 us
  local copies, waits for them, and re-layouts: 6.53 us -> 1.91 us
    all_to_all x2 -> x1, blocking collectives: 47 us -> 17.7 us  [exchange(): lax.all_to_all(value, EVERY, 0, 0, tiled=True, axis_index_groups=groups)]
    all_to_all x1 -> x3, starting transfers between devices: 5.51 us -> 20.4 us  [exchange(): lax.all_to_all(value, EVERY, 0, 0, tiled=True, axis_index_groups=groups)]
    all_to_all x1 -> x0, blocking collectives: 10 us -> none  [on_device(): total = jnp.sum(lax.all_to_all(slope, ('y', 'x'), 0, 0, tiled=True), axis=0)]
    ppermute x2 -> x4, waiting for transfers between devices: 0.01 us -> 4.76 us  [on_device(): lax.ppermute(start, EVERY, state_shift(partitions, k))]
    all_to_all x1 -> x3, waiting for transfers between devices: 30.3 us -> 33.7 us  [exchange(): lax.all_to_all(value, EVERY, 0, 0, tiled=True, axis_index_groups=groups)]
    unnamed x22 -> x6, local copies, waits for them, and re-layouts: 3.14 us -> 0.02 us
    pallas_call x3 -> x5, Pallas kernels: 18.5 us -> 21 us  [the longest x1 6.95 us: on_device(): pl.pallas_call(trace_kernel, out_shape=outputs, in_specs=[slow] * 5, out_...]
    squeeze x2 -> x0, local copies, waits for them, and re-layouts: 1.9 us -> none  [the longest x1 0.99 us: on_device(): lower_factor[0]]
  transfers between devices with their start and end apart: 6 -> 10, of which waited for: 1 -> 4; matrix products, arithmetic and copies ran while one was open for 2% -> 1% of each run, Pallas kernels for 12% -> 14%
where the time goes in v3:
time: 132 us
  starting transfers between devices  48.4 us (37%)
  waiting for transfers between devices  38.5 us (29%)
  Pallas kernels  24.4 us (18%)
  blocking collectives  17.7 us (13%)
  local copies, waits for them, and re-layouts  1.91 us (1%)
    all_to_all x3, waiting for transfers between devices, exchange(): lax.all_to_all(value, EVERY, 0, 0, tiled=True, axis_index_groups=groups)  33.7 us
    all_to_all x3, starting transfers between devices, exchange(): lax.all_to_all(value, EVERY, 0, 0, tiled=True, axis_index_groups=groups)  20.4 us
    all_to_all x1, blocking collectives, exchange(): lax.all_to_all(value, EVERY, 0, 0, tiled=True, axis_index_groups=groups)  17.7 us
    ppermute x4, starting transfers between devices, on_device(): lax.ppermute(start, EVERY, state_shift(partitions, k))  15.8 us
    ppermute x3, starting transfers between devices, on_device(): lax.ppermute(late, EVERY, line_shift(partitions, k))  12.2 us
    pallas_call x1, Pallas kernels, on_device(): pl.pallas_call(trace_kernel, out_shape=outputs, in_specs=[slow] * 5, out_...  6.95 us
    pallas_call x1, Pallas kernels, on_device(): pl.pallas_call(block_kernel, out_shape=(jax.ShapeDtypeStruct((2, ROWS, BL...  6.62 us
    ppermute x4, waiting for transfers between devices, on_device(): lax.ppermute(start, EVERY, state_shift(partitions, k))  4.76 us
  transfers between devices with their start and end apart: 10, of which 4 were waited for; matrix products, arithmetic and copies ran while one was open for 1% of the time, Pallas kernels for 14%

profile of v3, /device:TPU:1, one launch (start us, length us, event | category | flops | bytes accessed | tf_op | source)
XLA Modules:
  0.0 131.8 jit_solution(16717510313270223349)
XLA Ops:
  0.6 2.6 %shard_map.102 = (bf16[4,512,512]{2,1,0:T(8,128)(2,1)}, bf16[64,1536]{1,0:T(8,128)(2,1)}) custom-call(bf16[2,64,1024]{2,1,0:T(8,128)(2,1)} %low.1, bf16[2,64,512]{2,1,0:T(8,128)(2,1)} %arrow_ref.1, bf16[2,64,1024]{2,1,0:T(8,128)(2,1)} %x_ref.3, bf16[1,64,1024]{2,1,0:T(8,128)(2,1)} %sigma.1, bf16[1,64,512]{2,1,0:T(8,128)(2,1)} %tip.1), custom_call_target="tpu_custom_call" | custom-call | bytes 4000000 | tf_op jit(solution)/shard_map/pallas_call | solution.py:458
  3.3 5.0 %all-to-all-start = ((bf16[4,512,512]{2,1,0:T(8,128)(2,1)}), bf16[4,512,512]{2,1,0:T(8,128)(2,1)}, u32[]{:S(2)}, u32[]{:S(2)}) async-start(bf16[4,512,512]{2,1,0:T(8,128)(2,1)} %get-tuple-element.14), calls=%async_computation | async-start | bytes 4194304 | tf_op jit(solution)/shard_map/all_to_all | solution.py:80
  8.3 8.2 %collective-permute-start.2 = (bf16[64,1536]{1,0:T(8,128)(2,1)}, bf16[64,1536]{1,0:T(8,128)(2,1)S(1)}, u32[]{:S(2)}, u32[]{:S(2)}) collective-permute-start(bf16[64,1536]{1,0:T(8,128)(2,1)} %get-tuple-element.15), channel_id=1, source_target_pairs={{16,0},{17,1},{18,2},{19,3},{20,4},{21,5},{22,6},{23,7},{24,8},{25... | collective-permute-start | bytes 589832 | tf_op jit(solution)/shard_map/ppermute | solution.py:477
  16.5 2.9 %collective-permute-start.3 = (bf16[64,1536]{1,0:T(8,128)(2,1)}, bf16[64,1536]{1,0:T(8,128)(2,1)}, u32[]{:S(2)}, u32[]{:S(2)}) collective-permute-start(bf16[64,1536]{1,0:T(8,128)(2,1)} %get-tuple-element.15), channel_id=1, source_target_pairs={{16,1},{17,2},{18,3},{19,0},{20,5},{21,6},{22,7},{23,4},{24,9},{25... | collective-permute-start | bytes 589832 | tf_op jit(solution)/shard_map/ppermute | solution.py:477
  19.4 2.8 %collective-permute-start = (bf16[64,1536]{1,0:T(8,128)(2,1)}, bf16[64,1536]{1,0:T(8,128)(2,1)S(1)}, u32[]{:S(2)}, u32[]{:S(2)}) collective-permute-start(bf16[64,1536]{1,0:T(8,128)(2,1)} %get-tuple-element.15), channel_id=1, source_target_pairs={{16,2},{17,3},{18,0},{19,1},{20,6},{21,7},{22,4},{23,5},{24,10},{2... | collective-permute-start | bytes 589832 | tf_op jit(solution)/shard_map/ppermute | solution.py:477
  22.2 1.9 %collective-permute-start.1 = (bf16[64,1536]{1,0:T(8,128)(2,1)}, bf16[64,1536]{1,0:T(8,128)(2,1)}, u32[]{:S(2)}, u32[]{:S(2)}) collective-permute-start(bf16[64,1536]{1,0:T(8,128)(2,1)} %get-tuple-element.15), channel_id=1, source_target_pairs={{16,3},{17,0},{18,1},{19,2},{20,7},{21,4},{22,5},{23,6},{24,11},{2... | collective-permute-start | bytes 589832 | tf_op jit(solution)/shard_map/ppermute | solution.py:477
  24.2 3.9 %collective-permute-done.3.refs_1_ = bf16[64,1536]{1,0:T(8,128)(2,1)} collective-permute-done((bf16[64,1536]{1,0:T(8,128)(2,1)}, bf16[64,1536]{1,0:T(8,128)(2,1)}, u32[]{:S(2)}, u32[]{:S(2)}) %collective-permute-start.3) | collective-permute-done | bytes 196640 | tf_op jit(solution)/shard_map/ppermute | solution.py:477
  28.1 2.4 %shard_map.103.refs_2_ = bf16[4,1696,512]{2,1,0:T(8,128)(2,1)} custom-call(bf16[64,1536]{1,0:T(8,128)(2,1)} %copy-done, bf16[64,1536]{1,0:T(8,128)(2,1)} %collective-permute-done.3.refs_1_), custom_call_target="tpu_custom_call" | custom-call | bytes 8000000 | tf_op jit(solution)/shard_map/pallas_call | solution.py:482
  30.5 0.9 collective-permute-done.1.refs_1_
  31.3 2.3 %shard_map.104.begun = bf16[4,1696,512]{2,1,0:T(8,128)(2,1)} custom-call(bf16[64,1536]{1,0:T(8,128)(2,1)} %copy-done.1, bf16[64,1536]{1,0:T(8,128)(2,1)} %collective-permute-done.1.refs_1_, bf16[4,1696,512]{2,1,0:T(8,128)(2,1)} %shard_map.103.refs_2_), custom_call_target="tpu_custom_call", output_to_operand_aliasing={{}: (2, {})} | custom-call | bytes 8000000 | tf_op jit(solution)/shard_map/pallas_call | solution.py:482
  33.7 3.5 %shard_map.105 = (bf16[4,1696,512]{2,1,0:T(8,128)(2,1)}, bf16[768,512]{1,0:T(8,128)(2,1)}) custom-call(bf16[4,512,512]{2,1,0:T(8,128)(2,1)} %all-to-all-done.got, bf16[4,1696,512]{2,1,0:T(8,128)(2,1)} %shard_map.104.begun), custom_call_target="tpu_custom_call", output_to_operand_aliasing={{0}: (1, {})} | custom-call | bytes 12000000 | tf_op jit(solution)/shard_map/pallas_call | solution.py:497
  37.2 5.8 %all-to-all-start.1 = ((bf16[4,1696,512]{2,1,0:T(8,128)(2,1)}), bf16[4,1696,512]{2,1,0:T(8,128)(2,1)}, u32[]{:S(2)}, u32[]{:S(2)}) async-start(bf16[4,1696,512]{2,1,0:T(8,128)(2,1)} %get-tuple-element.16), calls=%async_computation.1 | async-start | bytes 13893632 | tf_op jit(solution)/shard_map/all_to_all | solution.py:80
  43.0 6.0 %collective-permute-start.4 = (bf16[768,512]{1,0:T(8,128)(2,1)}, bf16[768,512]{1,0:T(8,128)(2,1)}, u32[]{:S(2)}, u32[]{:S(2)}) collective-permute-start(bf16[768,512]{1,0:T(8,128)(2,1)} %get-tuple-element.17.late0), channel_id=1, source_target_pairs={{0,4},{1,5},{2,6},{3,7},{4,8},{5,9},{6,10},{7,11},{8,12},{9,13},{1... | collective-permute-start | bytes 2359304 | tf_op jit(solution)/shard_map/ppermute | solution.py:517
  49.0 1.9 %collective-permute-start.5 = (bf16[768,512]{1,0:T(8,128)(2,1)}, bf16[768,512]{1,0:T(8,128)(2,1)}, u32[]{:S(2)}, u32[]{:S(2)}) collective-permute-start(bf16[768,512]{1,0:T(8,128)(2,1)} %get-tuple-element.17.late0), channel_id=1, source_target_pairs={{0,8},{1,9},{2,10},{3,11},{4,12},{5,13},{6,14},{7,15},{8,0},{9,1},... | collective-permute-start | bytes 2359304 | tf_op jit(solution)/shard_map/ppermute | solution.py:517
  51.0 4.3 %collective-permute-start.6 = (bf16[768,512]{1,0:T(8,128)(2,1)}, bf16[768,512]{1,0:T(8,128)(2,1)}, u32[]{:S(2)}, u32[]{:S(2)}) collective-permute-start(bf16[768,512]{1,0:T(8,128)(2,1)} %get-tuple-element.17.late0), channel_id=1, source_target_pairs={{0,12},{1,13},{2,14},{3,15},{4,0},{5,1},{6,2},{7,3},{8,4},{9,5},{1... | collective-permute-start | bytes 2359304 | tf_op jit(solution)/shard_map/ppermute | solution.py:517
  55.3 0.7 copy.14.weight_ref
  56.0 28.8 %all-to-all-done.1.got = bf16[4,1696,512]{2,1,0:T(8,128)(2,1)} async-done(((bf16[4,1696,512]{2,1,0:T(8,128)(2,1)}), bf16[4,1696,512]{2,1,0:T(8,128)(2,1)}, u32[]{:S(2)}, u32[]{:S(2)}) %all-to-all-start.1) | async-done | bytes 6946848 | tf_op jit(solution)/shard_map/all_to_all | solution.py:80
  84.8 7.0 %shard_map.106 = (f32[2,64,512]{2,1,0:T(8,128)}, f32[128,1024]{1,0:T(8,128)}, f32[128,512]{1,0:T(8,128)}, f32[32,8,128]{2,1,0:T(8,128)}) custom-call(bf16[4,1696,512]{2,1,0:T(8,128)(2,1)} %all-to-all-done.1.got, bf16[2,64,512]{2,1,0:T(8,128)(2,1)} %arrow_ref.1, bf16[2,64,1024]{2,1,0:T(8,128)(2,1)} %x_ref.3, bf16[512,512]{1,0:T(8,128)(2,1)} %q_ref.1, ...), custom_call_target="tpu_custom_call" | custom-call | bytes 20000000 | tf_op jit(solution)/shard_map/pallas_call | solution.py:526
  91.8 17.7 %all_to_all.20 = f32[32,8,128]{2,1,0:T(8,128)S(1)} all-to-all(f32[32,8,128]{2,1,0:T(8,128)} %get-tuple-element.23), channel_id=1, replica_groups={{0,1,2,3,4,5,6,7,8,9,10,11,12,13,14,15,16,17,18,19,20,21,22,23,24,25,26..., dimensions={0} | all-to-all | bytes 262144 | tf_op jit(solution)/shard_map/all_to_all | solution.py:80
  109.5 0.6 broadcast_in_dim.10
  110.2 9.5 %all-to-all-start.3 = ((f32[16,8,128]{2,1,0:T(8,128)}), f32[16,8,128]{2,1,0:T(8,128)S(1)}, u32[]{:S(2)}, u32[]{:S(2)}) async-start(f32[16,8,128]{2,1,0:T(8,128)} %broadcast_in_dim.10), calls=%async_computation.3 | async-start | bytes 131072 | tf_op jit(solution)/shard_map/all_to_all | solution.py:80
  119.7 6.6 %shard_map.107 = (f32[2,64,1024]{2,1,0:T(8,128)}, f32[2,64,1024]{2,1,0:T(8,128)}) custom-call(bf16[4,1696,512]{2,1,0:T(8,128)(2,1)} %all-to-all-done.1.got, bf16[768,512]{1,0:T(8,128)(2,1)} %get-tuple-element.17.late0, bf16[768,512]{1,0:T(8,128)(2,1)} %collective-permute-done.4.late1, bf16[768,512]{1,0:T(8,128)(2,1)} %collective-permute-done.5.late2, ...), custom_call_target="tpu_custom_call" | custom-call | bytes 20000000 | tf_op jit(solution)/shard_map/pallas_call | solution.py:553
  126.4 4.9 %all-to-all-done.3 = f32[16,8,128]{2,1,0:T(8,128)S(1)} async-done(((f32[16,8,128]{2,1,0:T(8,128)}), f32[16,8,128]{2,1,0:T(8,128)S(1)}, u32[]{:S(2)}, u32[]{:S(2)}) %all-to-all-start.3) | async-done | bytes 65568 | tf_op jit(solution)/shard_map/all_to_all | solution.py:80
  131.3 0.5 slice.3
  (14 shorter events, 0.1 us)
Async XLA Ops:
  3.3 30.4 %all-to-all-start = ((bf16[4,512,512]{2,1,0:T(8,128)(2,1)}), bf16[4,512,512]{2,1,0:T(8,128)(2,1)}, u32[]{:S(2)}, u32[]{:S(2)}) async-start(bf16[4,512,512]{2,1,0:T(8,128)(2,1)} %get-tuple-element.14), calls=%async_computation | async-start | bytes 4194304 | tf_op jit(solution)/shard_map/all_to_all | solution.py:80
  8.3 15.8 %collective-permute-start.2 = (bf16[64,1536]{1,0:T(8,128)(2,1)}, bf16[64,1536]{1,0:T(8,128)(2,1)S(1)}, u32[]{:S(2)}, u32[]{:S(2)}) collective-permute-start(bf16[64,1536]{1,0:T(8,128)(2,1)} %get-tuple-element.15), channel_id=1, source_target_pairs={{16,0},{17,1},{18,2},{19,3},{20,4},{21,5},{22,6},{23,7},{24,8},{25... | collective-permute-start | bytes 589832 | tf_op jit(solution)/shard_map/ppermute | solution.py:477
  16.5 11.5 %collective-permute-start.3 = (bf16[64,1536]{1,0:T(8,128)(2,1)}, bf16[64,1536]{1,0:T(8,128)(2,1)}, u32[]{:S(2)}, u32[]{:S(2)}) collective-permute-start(bf16[64,1536]{1,0:T(8,128)(2,1)} %get-tuple-element.15), channel_id=1, source_target_pairs={{16,1},{17,2},{18,3},{19,0},{20,5},{21,6},{22,7},{23,4},{24,9},{25... | collective-permute-start | bytes 589832 | tf_op jit(solution)/shard_map/ppermute | solution.py:477
  19.4 11.1 %collective-permute-start = (bf16[64,1536]{1,0:T(8,128)(2,1)}, bf16[64,1536]{1,0:T(8,128)(2,1)S(1)}, u32[]{:S(2)}, u32[]{:S(2)}) collective-permute-start(bf16[64,1536]{1,0:T(8,128)(2,1)} %get-tuple-element.15), channel_id=1, source_target_pairs={{16,2},{17,3},{18,0},{19,1},{20,6},{21,7},{22,4},{23,5},{24,10},{2... | collective-permute-start | bytes 589832 | tf_op jit(solution)/shard_map/ppermute | solution.py:477
  22.2 9.1 %collective-permute-start.1 = (bf16[64,1536]{1,0:T(8,128)(2,1)}, bf16[64,1536]{1,0:T(8,128)(2,1)}, u32[]{:S(2)}, u32[]{:S(2)}) collective-permute-start(bf16[64,1536]{1,0:T(8,128)(2,1)} %get-tuple-element.15), channel_id=1, source_target_pairs={{16,3},{17,0},{18,1},{19,2},{20,7},{21,4},{22,5},{23,6},{24,11},{2... | collective-permute-start | bytes 589832 | tf_op jit(solution)/shard_map/ppermute | solution.py:477
  24.2 3.9 %copy-start = (bf16[64,1536]{1,0:T(8,128)(2,1)}, bf16[64,1536]{1,0:T(8,128)(2,1)S(1)}, u32[]{:S(2)}) copy-start(bf16[64,1536]{1,0:T(8,128)(2,1)S(1)} %collective-permute-done.2.refs_0_.start_ref) | copy-start | bytes 589828
  30.5 0.9 copy-start.1
  37.2 18.1 %copy-start.2 = (f32[2,64]{1,0:T(2,128)S(1)}, f32[2,64]{1,0:T(2,128)}, u32[]{:S(2)}) copy-start(f32[2,64]{1,0:T(2,128)} %param.13) | copy-start | bytes 1540
  37.2 47.6 %all-to-all-start.1 = ((bf16[4,1696,512]{2,1,0:T(8,128)(2,1)}), bf16[4,1696,512]{2,1,0:T(8,128)(2,1)}, u32[]{:S(2)}, u32[]{:S(2)}) async-start(bf16[4,1696,512]{2,1,0:T(8,128)(2,1)} %get-tuple-element.16), calls=%async_computation.1 | async-start | bytes 13893632 | tf_op jit(solution)/shard_map/all_to_all | solution.py:80
  43.0 76.7 %collective-permute-start.4 = (bf16[768,512]{1,0:T(8,128)(2,1)}, bf16[768,512]{1,0:T(8,128)(2,1)}, u32[]{:S(2)}, u32[]{:S(2)}) collective-permute-start(bf16[768,512]{1,0:T(8,128)(2,1)} %get-tuple-element.17.late0), channel_id=1, source_target_pairs={{0,4},{1,5},{2,6},{3,7},{4,8},{5,9},{6,10},{7,11},{8,12},{9,13},{1... | collective-permute-start | bytes 2359304 | tf_op jit(solution)/shard_map/ppermute | solution.py:517
  49.0 70.7 %collective-permute-start.5 = (bf16[768,512]{1,0:T(8,128)(2,1)}, bf16[768,512]{1,0:T(8,128)(2,1)}, u32[]{:S(2)}, u32[]{:S(2)}) collective-permute-start(bf16[768,512]{1,0:T(8,128)(2,1)} %get-tuple-element.17.late0), channel_id=1, source_target_pairs={{0,8},{1,9},{2,10},{3,11},{4,12},{5,13},{6,14},{7,15},{8,0},{9,1},... | collective-permute-start | bytes 2359304 | tf_op jit(solution)/shard_map/ppermute | solution.py:517
  51.0 68.8 %collective-permute-start.6 = (bf16[768,512]{1,0:T(8,128)(2,1)}, bf16[768,512]{1,0:T(8,128)(2,1)}, u32[]{:S(2)}, u32[]{:S(2)}) collective-permute-start(bf16[768,512]{1,0:T(8,128)(2,1)} %get-tuple-element.17.late0), channel_id=1, source_target_pairs={{0,12},{1,13},{2,14},{3,15},{4,0},{5,1},{6,2},{7,3},{8,4},{9,5},{1... | collective-permute-start | bytes 2359304 | tf_op jit(solution)/shard_map/ppermute | solution.py:517
  110.2 21.1 %all-to-all-start.3 = ((f32[16,8,128]{2,1,0:T(8,128)}), f32[16,8,128]{2,1,0:T(8,128)S(1)}, u32[]{:S(2)}, u32[]{:S(2)}) async-start(f32[16,8,128]{2,1,0:T(8,128)} %broadcast_in_dim.10), calls=%async_computation.3 | async-start | bytes 131072 | tf_op jit(solution)/shard_map/all_to_all | solution.py:80

commit v4 on v3

v4 whole, which is shorter than its diff:
```python
import jax
import jax.numpy as jnp
from jax import lax
from jax.experimental import pallas as pl
from jax.experimental.pallas import tpu as pltpu
from jax.sharding import Mesh, PartitionSpec as P

SIDE = 4
ROWS = 64
HALF = 512
BLOCK = 1024
BF = jnp.bfloat16
F32 = jnp.float32
EVERY = ("tm", "y", "x")

L1, M1, L0, M0, X1 = 0, 2, 3, 5, 6
PART = 3 * ROWS
SENT = 8 * ROWS
SHARE = 2 * ROWS
PANEL = SIDE * PART
MISC = 2 * ROWS + ROWS + 16
WIDE = BLOCK + HALF
LATER = PANEL + SHARE
VMEM_BYTES = 127 * 512 * 1024


def line_groups(partitions, phase):
    groups = []
    for t in range(partitions):
        base = t * SIDE * SIDE
        for i in range(SIDE):
            if (t + phase) % 2 == 0:
                groups.append([base + SIDE * i + x for x in range(SIDE)])
            else:
                groups.append([base + SIDE * y + i for y in range(SIDE)])
    return groups


def plane_groups(partitions):
    plane = 2 * SIDE * SIDE
    return [[z * plane + r for r in range(plane)] for z in range(partitions // 2)]


def height_groups(partitions):
    plane = SIDE * SIDE
    return [
        [t * plane + r for t in range(core, partitions, 2)]
        for core in range(2)
        for r in range(plane)
    ]


def state_shift(partitions, steps):
    pairs = []
    for t in range(partitions - 1):
        for y in range(SIDE):
            for x in range(SIDE):
                to = (y, (x + steps) % SIDE) if t % 2 == 0 else ((y + steps) % SIDE, x)
                source = (t + 1) * SIDE * SIDE + SIDE * y + x
                pairs.append((source, t * SIDE * SIDE + SIDE * to[0] + to[1]))
    return pairs


def line_shift(partitions, steps):
    pairs = []
    for t in range(partitions):
        for y in range(SIDE):
            for x in range(SIDE):
                to = ((y + steps) % SIDE, x) if t % 2 == 0 else (y, (x + steps) % SIDE)
                base = t * SIDE * SIDE
                pairs.append((base + SIDE * y + x, base + SIDE * to[0] + to[1]))
    return pairs


def cost(megabytes):
    return pl.CostEstimate(flops=0, bytes_accessed=megabytes * 1_000_000, transcendentals=0)


def exchange(value, groups):
    return lax.all_to_all(value, EVERY, 0, 0, tiled=True, axis_index_groups=groups)


def dot(left, right):
    return jnp.dot(left, right, preferred_element_type=F32)


def dot_t(left, right):
    return lax.dot_general(left, right, (((1,), (1,)), ((), ())), preferred_element_type=F32)


def split(value):
    high = value.astype(BF)
    return high, (value - high.astype(F32)).astype(BF)


def place():
    core = lax.rem(lax.axis_index("tm"), 2)
    y, x = lax.axis_index("y"), lax.axis_index("x")
    first = jnp.where(core == 0, x, y)
    return core, y * SIDE + x, first


def natural(core, second, first):
    return jnp.where(core == 0, SIDE * second + first, SIDE * first + second)


def columns_t(ref, piece, row, blocks=None):
    half = lax.div(row, 8)
    lane = lax.div(lax.rem(row, 8), 2)
    rows = pl.ds(pl.multiple_of((piece + half) * ROWS, ROWS), ROWS)
    lanes = pl.ds(pl.multiple_of(lane * 128, 128), 128)
    if blocks is None:
        window = ref[:, rows, lanes]
        window = window.reshape(window.shape[0] * ROWS, 128)
    else:
        window = jnp.concatenate([ref[b, rows, lanes] for b in blocks], axis=0)
    want = lax.broadcasted_iota(jnp.int32, (ROWS, 128), 0) + lax.rem(row, 2) * ROWS
    pick = jnp.where(lax.broadcasted_iota(jnp.int32, (ROWS, 128), 1) == want, 1.0, 0.0)
    return dot_t(pick.astype(BF), window).astype(BF)


def pack_kernel(low, arrow, inverse, sigma, tip, out, start, held, own, sem_in, sem_own, sem_out):
    loads = []
    for k, (ref, j, h) in enumerate(
        [(low, 1, 0), (low, 1, 1), (arrow, 1, 0), (low, 0, 0), (low, 0, 1), (arrow, 0, 0)]
        + [(inverse, 1, 0), (inverse, 1, 1)]
    ):
        loads.append(
            pltpu.make_async_copy(
                ref.at[j, :, pl.ds(h * HALF, HALF)],
                held.at[pl.ds(k * ROWS, ROWS)],
                sem_in.at[k],
            )
        )
    loads_own = [
        pltpu.make_async_copy(sigma.at[0], own.at[:, pl.ds(0, BLOCK)], sem_own.at[0]),
        pltpu.make_async_copy(tip.at[0], own.at[:, pl.ds(BLOCK, HALF)], sem_own.at[1]),
    ]
    for copy in loads + loads_own:
        copy.start()
    for copy in loads + loads_own:
        copy.wait()
    stores = [pltpu.make_async_copy(held, out.at[d], sem_out.at[d]) for d in range(SIDE)]
    stores.append(pltpu.make_async_copy(own, start, sem_out.at[SIDE]))
    for copy in stores:
        copy.start()
    for copy in stores:
        copy.wait()


def panel_kernel(
    got,
    arrow,
    weight,
    own0,
    own1,
    own2,
    own3,
    out,
    late0,
    late1,
    late2,
    late3,
    panel,
    state,
    misc,
    share,
    sem_in,
    sem_out,
    sem_late,
    sem_state,
):
    core, _, first = place()
    second = jnp.where(core == 0, lax.axis_index("y"), lax.axis_index("x"))
    loads = [pltpu.make_async_copy(got.at[j], panel.at[j], sem_in.at[j]) for j in range(SIDE)]
    load_arrow = pltpu.make_async_copy(
        arrow.at[0], misc.at[pl.ds(2 * ROWS, ROWS)], sem_in.at[SIDE]
    )
    loads_state = [
        pltpu.make_async_copy(
            own.at[:, pl.ds(h * HALF, HALF)],
            state.at[pl.ds(k * PART + h * ROWS, ROWS)],
            sem_state.at[k * 3 + h],
        )
        for k, own in enumerate((own0, own1, own2, own3))
        for h in range(3)
    ]
    for copy in loads + [load_arrow] + loads_state:
        copy.start()
    stores = []
    for j in range(SIDE):
        loads[j].wait()
        here = [
            pltpu.make_async_copy(
                panel.at[j, pl.ds(0, PART)],
                out.at[d, pl.ds(j * PART, PART)],
                sem_out.at[d * (SIDE + 1) + j],
            )
            for d in range(SIDE)
        ]
        for copy in here:
            copy.start()
        stores += here
    cols = [columns_t(panel, L0, natural(core, d, first)) for d in range(SIDE)]
    cols = jnp.concatenate(cols, axis=0)
    misc[: 2 * ROWS, :] = jnp.concatenate([cols[: 2 * ROWS], cols[2 * ROWS :]], axis=1)
    rest = weight[...]
    parts = []
    for _ in range(3):
        parts.append(rest.astype(BF).astype(F32))
        rest = rest - parts[-1]
    parts = jnp.concatenate(parts + [jnp.zeros((10, ROWS), F32)], axis=0)
    parts = jnp.concatenate([parts, jnp.zeros((16, HALF - ROWS), F32)], axis=1)
    misc[3 * ROWS :, :] = parts.astype(BF)
    load_arrow.wait()
    here = [
        pltpu.make_async_copy(misc, out.at[d, pl.ds(PANEL, MISC)], sem_out.at[d * (SIDE + 1) + SIDE])
        for d in range(SIDE)
    ]
    lates = (late0, late1, late2, late3)
    for k, late in enumerate(lates):
        here += [
            pltpu.make_async_copy(
                panel.at[j, pl.ds(PART, PART)],
                late.at[pl.ds(j * PART, PART)],
                sem_late.at[k * (SIDE + 1) + j],
            )
            for j in range(SIDE)
        ]
    for copy in loads_state:
        copy.wait()
    here += [
        pltpu.make_async_copy(state, late.at[pl.ds(LATER, PANEL)], sem_state.at[12 + k])
        for k, late in enumerate(lates)
    ]
    for copy in here:
        copy.start()
    stores += here
    for h in range(2):
        at = (X1 + h) * ROWS
        part = dot(cols, panel[:, at : at + ROWS, :].reshape(SIDE * ROWS, HALF))
        for d in range(SIDE):
            share[d, h * ROWS : (h + 1) * ROWS, :] = part[d * ROWS : (d + 1) * ROWS].astype(BF)
    here = [
        pltpu.make_async_copy(
            share.at[lax.rem(second + k, SIDE)],
            late.at[pl.ds(PANEL, SHARE)],
            sem_late.at[k * (SIDE + 1) + SIDE],
        )
        for k, late in enumerate(lates)
    ]
    for copy in here:
        copy.start()
    for copy in stores + here:
        copy.wait()


class Gathered:
    def __init__(self, mat):
        self.mat = mat

    def piece(self, k):
        return self.mat[:, k * ROWS : (k + 1) * ROWS, :].reshape(BLOCK, HALF)

    def over_rows(self, left, k):
        return dot(left, self.piece(k))

    def over_columns(self, left, k):
        return dot_t(left, self.piece(k))

    def times_factor(self, left_rows, left_tip):
        both = jnp.concatenate([self.over_rows(left_rows, h) for h in range(2)], axis=1)
        return both + self.over_columns(left_tip, 2)

    def past(self, left):
        u = self.over_columns(left[:, :HALF], 0) + self.over_columns(left[:, HALF:], 1)
        return u, self.over_rows(left, 2)


def load_exchanged(got, mat, sem):
    core, _, _ = place()
    return [
        pltpu.make_async_copy(
            got.at[d, pl.ds(j * PART, PART)],
            mat.at[natural(core, d, j)],
            sem.at[d * SIDE + j],
        )
        for d in range(SIDE)
        for j in range(SIDE)
    ]


def in_order(core, parts):
    even = jnp.concatenate(parts, axis=1)
    odd = [parts[d][:, j * 64 : (j + 1) * 64] for j in range(SIDE) for d in range(SIDE)]
    return jnp.where(core == 0, even, jnp.concatenate(odd, axis=1))


def sum_all(value):
    return jnp.sum(jnp.sum(value, axis=1, keepdims=True))


def trace_kernel(
    got,
    begun,
    panel_ref,
    arrow_ref,
    x_ref,
    q_ref,
    weight_ref,
    slope,
    factor,
    misc,
    state,
    inverse,
    arrow,
    x,
    q,
    sem_factor,
    sem_in,
):
    core, row, first = place()
    second = jnp.where(core == 0, lax.axis_index("y"), lax.axis_index("x"))
    load_misc = pltpu.make_async_copy(got.at[:, pl.ds(PANEL, MISC)], misc, sem_in.at[0])
    load_factor = load_exchanged(got, factor, sem_factor)
    later = [
        pltpu.make_async_copy(begun.at[pl.ds(LATER, PANEL)], state, sem_in.at[1]),
        pltpu.make_async_copy(
            panel_ref.at[:, pl.ds(X1 * ROWS, 2 * ROWS)], inverse, sem_in.at[2]
        ),
        pltpu.make_async_copy(arrow_ref, arrow, sem_in.at[3]),
        pltpu.make_async_copy(q_ref, q, sem_in.at[4]),
        pltpu.make_async_copy(x_ref, x, sem_in.at[5]),
    ]
    for copy in [load_misc] + load_factor + later:
        copy.start()
    load_misc.wait()
    columns = [natural(core, d, first) for d in range(SIDE)]
    mine = [natural(core, second, lax.rem(first + SIDE - k, SIDE)) for k in range(SIDE)]
    parts = []
    for d in range(SIDE):
        held = misc[d, : 2 * ROWS, :]
        parts.append(jnp.concatenate([held[:, :256], held[:, 256:]], axis=0))
    z0 = in_order(core, parts)
    z0_tip = misc[:, 2 * ROWS : 3 * ROWS, :].reshape(256, HALF)
    eye = lax.broadcasted_iota(jnp.int32, (ROWS, ROWS), 0)
    eye = jnp.where(eye == lax.broadcasted_iota(jnp.int32, (ROWS, ROWS), 1), 1.0, 0.0)
    weights = []
    for block in range(2):
        column = []
        for d in range(SIDE):
            held = misc[d, 3 * ROWS :, :].astype(F32)
            held = held[block : block + 1] + held[block + 2 : block + 3] + held[block + 4 : block + 5]
            column.append(jnp.sum(eye * held[:, :ROWS], axis=1, keepdims=True))
        weights.append(jnp.concatenate(column, axis=0))
    for copy in load_factor:
        copy.wait()
    have = Gathered(factor)
    u, u_tip = have.past(z0)
    u_tip = u_tip - z0_tip.astype(F32)
    u_mine = jnp.zeros((256, 256), F32)
    z1_mine = []
    for h in range(2):
        low = jnp.concatenate([factor[b, h * ROWS : (h + 1) * ROWS, :] for b in mine], axis=0)
        u_mine += dot_t(z0[:, h * HALF : (h + 1) * HALF], low)
    z1 = jnp.concatenate([columns_t(factor, 0, c) for c in columns], axis=0)
    z1_mine = jnp.concatenate([columns_t(factor, 0, c, mine) for c in columns], axis=0)
    z1_tip = jnp.concatenate([factor[c, 2 * ROWS :, :] for c in columns], axis=0)
    for copy in later:
        copy.wait()
    rows_in = jnp.concatenate([u.astype(BF), z1], axis=0)
    tip_in = jnp.concatenate([u_tip.astype(BF), z1_tip], axis=0)
    held = state[...].reshape(SIDE, PART, HALF)
    held = [held[:, h * ROWS : (h + 1) * ROWS, :].reshape(256, HALF) for h in range(3)]
    through = dot_t(rows_in[:, :HALF], held[0]) + dot_t(rows_in[:, HALF:], held[1])
    through += 2.0 * dot_t(tip_in, held[2])
    carried = jnp.zeros((256, 256), F32)
    for h in range(2):
        part = inverse[:, h * ROWS : (h + 1) * ROWS, :].reshape(256, HALF)
        carried += dot_t(z0[:, h * HALF : (h + 1) * HALF], part)
    own_parts = parts[0]
    for d in range(1, SIDE):
        own_parts = jnp.where(second == d, parts[d], own_parts)
    traced = (u_mine * through[:256] + own_parts.astype(F32) * carried) * weights[0]
    traced += z1_mine.astype(F32) * through[256:] * weights[1]
    own_tip = dot(z0_own(misc, second, core), Gathered(factor).piece(2))
    own_tip = own_tip - arrow[0].astype(F32)
    both = jnp.concatenate([own_tip.astype(BF), arrow[1]], axis=0)
    tip_traced = both.astype(F32) * dot(both, q[...])
    at = lax.broadcasted_iota(jnp.int32, (ROWS, BLOCK), 0) + row * ROWS
    on_diagonal = lax.broadcasted_iota(jnp.int32, (ROWS, BLOCK), 1) == at
    total = sum_all(traced)
    for block in range(2):
        total += sum_all(tip_traced[block * ROWS : (block + 1) * ROWS] * weight_ref[block])
        own = jnp.where(on_diagonal, x[block].astype(F32), 0.0)
        total += sum_all(own * weight_ref[block])
    slope[...] = jnp.full(slope.shape, total, F32)


def z0_own(misc, second, core):
    rows = pl.ds(pl.multiple_of(lax.rem(second, 2) * ROWS, ROWS), ROWS)
    lanes = pl.ds(pl.multiple_of(lax.div(second, 2) * 256, 256), 256)
    return in_order(core, [misc[d, rows, lanes] for d in range(SIDE)])


def block_kernel(
    got,
    late0,
    late1,
    late2,
    late3,
    arrow_ref,
    x_ref,
    q_ref,
    total_ref,
    diag_ref,
    lower_ref,
    tip_ref,
    factor1,
    factor0,
    state,
    shares,
    misc,
    arrow,
    x,
    q,
    diag,
    lower,
    tip,
    sem_factor1,
    sem_factor0,
    sem_state,
    sem_share,
    sem_in,
    sem_out,
):
    del total_ref
    core, row, first = place()
    second = jnp.where(core == 0, lax.axis_index("y"), lax.axis_index("x"))
    loads1 = [
        pltpu.make_async_copy(got.at[:, pl.ds(PANEL, MISC)], misc, sem_in.at[0]),
        pltpu.make_async_copy(arrow_ref, arrow, sem_in.at[1]),
    ] + load_exchanged(got, factor1, sem_factor1)
    loads_state = [pltpu.make_async_copy(q_ref, q, sem_in.at[2])]
    loads0 = [pltpu.make_async_copy(x_ref, x, sem_in.at[3])]
    for k, late in enumerate((late0, late1, late2, late3)):
        source = lax.rem(second + SIDE - k, SIDE)
        for j in range(SIDE):
            behind = lax.rem(first + SIDE - j, SIDE)
            loads_state.append(
                pltpu.make_async_copy(
                    late.at[pl.ds(LATER + j * PART, PART)],
                    state.at[natural(core, source, behind)],
                    sem_state.at[k * SIDE + j],
                )
            )
            loads0.append(
                pltpu.make_async_copy(
                    late.at[pl.ds(j * PART, PART)],
                    factor0.at[natural(core, source, j)],
                    sem_factor0.at[k * SIDE + j],
                )
            )
        loads0.append(
            pltpu.make_async_copy(late.at[pl.ds(PANEL, SHARE)], shares.at[k], sem_share.at[k])
        )
    for copy in loads1 + loads_state + loads0:
        copy.start()
    for copy in loads1:
        copy.wait()
    have = Gathered(factor1)
    z1 = columns_t(factor1, 0, row)
    z1_tip, z0_tip = arrow[1], arrow[0]
    u, u_tip = have.past(z0_own(misc, second, core))
    u_tip = u_tip - z0_tip.astype(F32)
    uh, ul = split(u)
    uh_tip, ul_tip = split(u_tip)
    rows_in = jnp.concatenate([z1, uh, ul], axis=0)
    tip_in = jnp.concatenate([z1_tip, uh_tip, ul_tip], axis=0)
    for copy in loads_state:
        copy.wait()
    begun = Gathered(state)
    top = begun.times_factor(rows_in, tip_in)
    bottom = begun.over_rows(rows_in, 2) + dot(tip_in, q[...])
    p1, a = top[:64], top[64:128] + top[128:]
    p1_tip, a_tip = bottom[:64], bottom[64:128] + bottom[128:]
    tip[1] = -p1_tip
    tip[0] = a_tip
    stores = [pltpu.make_async_copy(tip, tip_ref, sem_out.at[0])]
    stores[0].start()
    p1h, p1l = split(p1)
    ah, al = split(a)
    p1h_tip, p1l_tip = split(p1_tip)
    ah_tip, al_tip = split(a_tip)
    own = [state[row, h * ROWS : (h + 1) * ROWS, :] for h in range(3)]
    own_rows = jnp.concatenate(own[:2], axis=1)
    out = have.times_factor(
        jnp.concatenate([p1h, p1l, ah, al, own_rows], axis=0),
        jnp.concatenate([p1h_tip, p1l_tip, ah_tip, al_tip, own[2]], axis=0),
    )
    for copy in loads0:
        copy.wait()
    lower[1] = -out[256:]
    sigma1 = x[1].astype(F32) + out[:64] + out[64:128]
    diag[1] = sigma1
    here = [
        pltpu.make_async_copy(diag.at[1], diag_ref.at[1], sem_out.at[1]),
        pltpu.make_async_copy(lower.at[1], lower_ref.at[1], sem_out.at[2]),
    ]
    for copy in here:
        copy.start()
    stores += here
    carried = shares[0].astype(F32)
    for d in range(1, SIDE):
        carried += shares[d].astype(F32)
    carried = jnp.concatenate([carried[:ROWS], carried[ROWS:]], axis=1)
    p0h, p0l = split(carried + out[128:192] + out[192:256])
    out = Gathered(factor0).times_factor(
        jnp.concatenate([p0h, p0l, sigma1.astype(BF)], axis=0),
        jnp.concatenate([-ah_tip, -al_tip, -p1h_tip], axis=0),
    )
    lower[0] = -out[128:]
    diag[0] = x[0].astype(F32) + out[:64] + out[64:128]
    here = [
        pltpu.make_async_copy(diag.at[0], diag_ref.at[0], sem_out.at[3]),
        pltpu.make_async_copy(lower.at[0], lower_ref.at[0], sem_out.at[4]),
    ]
    for copy in here:
        copy.start()
    for copy in stores + here:
        copy.wait()


def on_device(
    lower_factor,
    arrow_factor,
    block_inverse,
    boundary_sigma,
    boundary_tip,
    tip_inverse,
    slope_weights,
    partitions,
):
    slow = pl.BlockSpec(memory_space=pltpu.HBM)
    fast = pl.BlockSpec(memory_space=pltpu.VMEM)
    params = pltpu.CompilerParams(vmem_limit_bytes=VMEM_BYTES)
    rows, start = pl.pallas_call(
        pack_kernel,
        out_shape=(
            jax.ShapeDtypeStruct((SIDE, SENT, HALF), BF),
            jax.ShapeDtypeStruct((ROWS, BLOCK + HALF), BF),
        ),
        in_specs=[slow] * 5,
        out_specs=(slow,) * 2,
        scratch_shapes=[
            pltpu.VMEM((SENT, HALF), BF),
            pltpu.VMEM((ROWS, BLOCK + HALF), BF),
            pltpu.SemaphoreType.DMA((8,)),
            pltpu.SemaphoreType.DMA((2,)),
            pltpu.SemaphoreType.DMA((SIDE + 1,)),
        ],
        compiler_params=params,
        cost_estimate=cost(4),
    )(lower_factor, arrow_factor, block_inverse, boundary_sigma, boundary_tip)
    got = exchange(rows, line_groups(partitions, 0))
    starts = [lax.ppermute(start, EVERY, state_shift(partitions, k)) for k in range(SIDE)]
    sent, *lates = pl.pallas_call(
        panel_kernel,
        out_shape=(
            jax.ShapeDtypeStruct((SIDE, PANEL + MISC, HALF), BF),
        )
        + (jax.ShapeDtypeStruct((LATER + PANEL, HALF), BF),) * SIDE,
        in_specs=[slow, slow, fast] + [slow] * SIDE,
        out_specs=(slow,) * 5,
        scratch_shapes=[
            pltpu.VMEM((SIDE, SENT, HALF), BF),
            pltpu.VMEM((PANEL, HALF), BF),
            pltpu.VMEM((MISC, HALF), BF),
            pltpu.VMEM((SIDE, SHARE, HALF), BF),
            pltpu.SemaphoreType.DMA((SIDE + 1,)),
            pltpu.SemaphoreType.DMA((SIDE * (SIDE + 1),)),
            pltpu.SemaphoreType.DMA((SIDE * (SIDE + 1),)),
            pltpu.SemaphoreType.DMA((16,)),
        ],
        compiler_params=params,
        cost_estimate=cost(12),
    )(got, arrow_factor, slope_weights, *starts)
    early = exchange(sent, line_groups(partitions, 1))
    for k in range(1, SIDE):
        lates[k] = lax.ppermute(lates[k], EVERY, line_shift(partitions, k))
    slope = pl.pallas_call(
        trace_kernel,
        out_shape=jax.ShapeDtypeStruct((32, 8, 128), F32),
        in_specs=[slow] * 6 + [fast],
        out_specs=fast,
        scratch_shapes=[
            pltpu.VMEM((16, PART, HALF), BF),
            pltpu.VMEM((SIDE, MISC, HALF), BF),
            pltpu.VMEM((PANEL, HALF), BF),
            pltpu.VMEM((SIDE, 2 * ROWS, HALF), BF),
            pltpu.VMEM((2, ROWS, HALF), BF),
            pltpu.VMEM((2, ROWS, BLOCK), BF),
            pltpu.VMEM((HALF, HALF), BF),
            pltpu.SemaphoreType.DMA((16,)),
            pltpu.SemaphoreType.DMA((6,)),
        ],
        compiler_params=params,
        cost_estimate=cost(20),
    )(early, lates[0], got, arrow_factor, block_inverse, tip_inverse, slope_weights[:, :, None])
    total = jnp.sum(exchange(slope, plane_groups(partitions)), axis=0)
    in_plane = total
    total = jnp.broadcast_to(total[None], (partitions // 2, 8, 128))
    total = jnp.sum(exchange(total, height_groups(partitions)), axis=0)
    outputs = (
        jax.ShapeDtypeStruct((2, ROWS, BLOCK), F32),
        jax.ShapeDtypeStruct((2, ROWS, BLOCK), F32),
        jax.ShapeDtypeStruct((2, ROWS, HALF), F32),
    )
    diag, lower, tip = pl.pallas_call(
        block_kernel,
        out_shape=outputs,
        in_specs=[slow] * 9,
        out_specs=(slow,) * 3,
        scratch_shapes=[
            pltpu.VMEM((16, PART, HALF), BF),
            pltpu.VMEM((16, PART, HALF), BF),
            pltpu.VMEM((16, PART, HALF), BF),
            pltpu.VMEM((SIDE, SHARE, HALF), BF),
            pltpu.VMEM((SIDE, MISC, HALF), BF),
            pltpu.VMEM((2, ROWS, HALF), BF),
            pltpu.VMEM((2, ROWS, BLOCK), BF),
            pltpu.VMEM((HALF, HALF), BF),
        ]
        + [pltpu.VMEM(leaf.shape, F32) for leaf in outputs]
        + [
            pltpu.SemaphoreType.DMA((16,)),
            pltpu.SemaphoreType.DMA((16,)),
            pltpu.SemaphoreType.DMA((16,)),
            pltpu.SemaphoreType.DMA((SIDE,)),
            pltpu.SemaphoreType.DMA((4,)),
            pltpu.SemaphoreType.DMA((5,)),
        ],
        compiler_params=params,
        cost_estimate=cost(30),
    )(early, *lates, arrow_factor, block_inverse, tip_inverse, in_plane)
    return diag, lower, tip, total[0, 0]


def solution(mesh):
    partitions = mesh.shape["tm"]
    fine = Mesh(mesh.devices.reshape(partitions, SIDE, SIDE), EVERY)
    rows = P("tm", ("y", "x"), None)

    def program(*args):
        return on_device(*args, partitions=partitions)

    return jax.shard_map(
        program,
        mesh=fine,
        in_specs=(rows, rows, rows, rows, rows, P(), P("tm", ("y", "x"))),
        out_specs=(rows, rows, rows, P()),
        check_vma=False,
    )
```

time: 132 us -> 134 us (1.015)
  blocking collectives: 17.7 us -> 35.3 us
  waiting for transfers between devices: 38.5 us -> 23 us
  starting transfers between devices: 48.4 us -> 45.9 us
  Pallas kernels: 24.4 us -> 26.4 us
    all_to_all x1, blocking collectives: 17.7 us -> 35.3 us  [exchange(): lax.all_to_all(value, EVERY, 0, 0, tiled=True, axis_index_groups=groups)]
    all_to_all x3, waiting for transfers between devices: 33.7 us -> 16.2 us  [exchange(): lax.all_to_all(value, EVERY, 0, 0, tiled=True, axis_index_groups=groups)]
    ppermute x4, waiting for transfers between devices: 4.76 us -> 6.86 us  [on_device(): lax.ppermute(start, EVERY, state_shift(partitions, k))]
    pallas_call x5 -> x3, Pallas kernels: 21.8 us -> 23.7 us  [the longest x1 9.8 us: on_device(): pl.pallas_call(block_kernel, out_shape=outputs, in_specs=[slow] * 9, out_...]
    ppermute x3, starting transfers between devices: 12.2 us -> 10.7 us  [on_device(): lates[k] = lax.ppermute(lates[k], EVERY, line_shift(partitions, k))]
  transfers between devices with their start and end apart: 10 -> 10, of which waited for: 4 -> 5; matrix products, arithmetic and copies ran while one was open for 1% -> 1% of each run, Pallas kernels for 14% -> 13%
where the time goes in v4:
time: 134 us; the launch traced here: 133 us
  starting transfers between devices  45.9 us (34%)
  blocking collectives  35.3 us (26%)
  Pallas kernels  26.4 us (20%)
  waiting for transfers between devices  23 us (17%)
  local copies, waits for them, and re-layouts  1.9 us (1%)
    all_to_all x1, blocking collectives, exchange(): lax.all_to_all(value, EVERY, 0, 0, tiled=True, axis_index_groups=groups)  35.3 us
    all_to_all x3, starting transfers between devices, exchange(): lax.all_to_all(value, EVERY, 0, 0, tiled=True, axis_index_groups=groups)  19.4 us
    all_to_all x3, waiting for transfers between devices, exchange(): lax.all_to_all(value, EVERY, 0, 0, tiled=True, axis_index_groups=groups)  16.2 us
    ppermute x4, starting transfers between devices, on_device(): lax.ppermute(start, EVERY, state_shift(partitions, k))  15.9 us
    ppermute x3, starting transfers between devices, on_device(): lates[k] = lax.ppermute(lates[k], EVERY, line_shift(partitions, k))  10.7 us
    pallas_call x1, Pallas kernels, on_device(): pl.pallas_call(block_kernel, out_shape=outputs, in_specs=[slow] * 9, out_...  9.8 us
    pallas_call x1, Pallas kernels, on_device(): pl.pallas_call(trace_kernel, out_shape=jax.ShapeDtypeStruct((32, 8, 128),...  7.41 us
    ppermute x4, waiting for transfers between devices, on_device(): lax.ppermute(start, EVERY, state_shift(partitions, k))  6.86 us
  transfers between devices with their start and end apart: 10, of which 5 were waited for; matrix products, arithmetic and copies ran while one was open for 1% of the time, Pallas kernels for 13%

profile of v4, /device:TPU:1, one launch (start us, length us, event | category | flops | bytes accessed | tf_op | source)
XLA Modules:
  0.0 133.4 jit_solution(14106924571627301813)
XLA Ops:
  0.6 2.6 %shard_map.102 = (bf16[4,512,512]{2,1,0:T(8,128)(2,1)}, bf16[64,1536]{1,0:T(8,128)(2,1)}) custom-call(bf16[2,64,1024]{2,1,0:T(8,128)(2,1)} %low.1, bf16[2,64,512]{2,1,0:T(8,128)(2,1)} %arrow_ref.3, bf16[2,64,1024]{2,1,0:T(8,128)(2,1)} %x_ref.3, bf16[1,64,1024]{2,1,0:T(8,128)(2,1)} %sigma.1, bf16[1,64,512]{2,1,0:T(8,128)(2,1)} %tip.1), custom_call_target="tpu_custom_call" | custom-call | bytes 4000000 | tf_op jit(solution)/shard_map/pallas_call | solution.py:547
  3.3 0.0 copy-start.4
  3.3 5.2 %all-to-all-start = ((bf16[4,512,512]{2,1,0:T(8,128)(2,1)}), bf16[4,512,512]{2,1,0:T(8,128)(2,1)}, u32[]{:S(2)}, u32[]{:S(2)}) async-start(bf16[4,512,512]{2,1,0:T(8,128)(2,1)} %get-tuple-element.14), calls=%async_computation | async-start | bytes 4194304 | tf_op jit(solution)/shard_map/all_to_all | solution.py:80
  8.5 8.3 %collective-permute-start = (bf16[64,1536]{1,0:T(8,128)(2,1)S(1)}, bf16[64,1536]{1,0:T(8,128)(2,1)S(1)}, u32[]{:S(2)}, u32[]{:S(2)}) collective-permute-start(bf16[64,1536]{1,0:T(8,128)(2,1)S(1)} %copy-done.4), channel_id=1, source_target_pairs={{16,0},{17,1},{18,2},{19,3},{20,4},{21,5},{22,6},{23,7},{24,8},{25... | collective-permute-start | bytes 589832 | tf_op jit(solution)/shard_map/ppermute | solution.py:566
  16.7 2.9 %collective-permute-start.1 = (bf16[64,1536]{1,0:T(8,128)(2,1)S(1)}, bf16[64,1536]{1,0:T(8,128)(2,1)S(1)}, u32[]{:S(2)}, u32[]{:S(2)}) collective-permute-start(bf16[64,1536]{1,0:T(8,128)(2,1)S(1)} %copy-done.4), channel_id=1, source_target_pairs={{16,1},{17,2},{18,3},{19,0},{20,5},{21,6},{22,7},{23,4},{24,9},{25... | collective-permute-start | bytes 589832 | tf_op jit(solution)/shard_map/ppermute | solution.py:566
  19.6 2.8 %collective-permute-start.2 = (bf16[64,1536]{1,0:T(8,128)(2,1)S(1)}, bf16[64,1536]{1,0:T(8,128)(2,1)}, u32[]{:S(2)}, u32[]{:S(2)}) collective-permute-start(bf16[64,1536]{1,0:T(8,128)(2,1)S(1)} %copy-done.4), channel_id=1, source_target_pairs={{16,2},{17,3},{18,0},{19,1},{20,6},{21,7},{22,4},{23,5},{24,10},{2... | collective-permute-start | bytes 589832 | tf_op jit(solution)/shard_map/ppermute | solution.py:566
  22.4 1.9 %collective-permute-start.3 = (bf16[64,1536]{1,0:T(8,128)(2,1)S(1)}, bf16[64,1536]{1,0:T(8,128)(2,1)}, u32[]{:S(2)}, u32[]{:S(2)}) collective-permute-start(bf16[64,1536]{1,0:T(8,128)(2,1)S(1)} %copy-done.4), channel_id=1, source_target_pairs={{16,3},{17,0},{18,1},{19,2},{20,7},{21,4},{22,5},{23,6},{24,11},{2... | collective-permute-start | bytes 589832 | tf_op jit(solution)/shard_map/ppermute | solution.py:566
  24.4 3.6 %collective-permute-done.1.own1 = bf16[64,1536]{1,0:T(8,128)(2,1)S(1)} collective-permute-done((bf16[64,1536]{1,0:T(8,128)(2,1)S(1)}, bf16[64,1536]{1,0:T(8,128)(2,1)S(1)}, u32[]{:S(2)}, u32[]{:S(2)}) %collective-permute-start.1) | collective-permute-done | bytes 196640 | tf_op jit(solution)/shard_map/ppermute | solution.py:566
  27.9 2.3 %collective-permute-done.2.own2 = bf16[64,1536]{1,0:T(8,128)(2,1)} collective-permute-done((bf16[64,1536]{1,0:T(8,128)(2,1)S(1)}, bf16[64,1536]{1,0:T(8,128)(2,1)}, u32[]{:S(2)}, u32[]{:S(2)}) %collective-permute-start.2) | collective-permute-done | bytes 196640 | tf_op jit(solution)/shard_map/ppermute | solution.py:566
  30.2 1.0 collective-permute-done.3.own3
  31.2 6.5 %shard_map.103 = (bf16[4,976,512]{2,1,0:T(8,128)(2,1)}, bf16[1664,512]{1,0:T(8,128)(2,1)}, bf16[1664,512]{1,0:T(8,128)(2,1)}, bf16[1664,512]{1,0:T(8,128)(2,1)}, bf16[1664,512]{1,0:T(8,128)(2,1)}) custom-call(bf16[4,512,512]{2,1,0:T(8,128)(2,1)} %all-to-all-done.got.panel_ref, bf16[2,64,512]{2,1,0:T(8,128)(2,1)} %arrow_ref.3, f32[2,64]{1,0:T(2,128)} %weight.1, ...), custom_call_target="tpu_custom_call" | custom-call | bytes 12000000 | tf_op jit(solution)/shard_map/pallas_call | solution.py:567
  37.8 4.8 %all-to-all-start.1 = ((bf16[4,976,512]{2,1,0:T(8,128)(2,1)}), bf16[4,976,512]{2,1,0:T(8,128)(2,1)}, u32[]{:S(2)}, u32[]{:S(2)}) async-start(bf16[4,976,512]{2,1,0:T(8,128)(2,1)} %get-tuple-element.16), calls=%async_computation.1 | async-start | bytes 7995392 | tf_op jit(solution)/shard_map/all_to_all | solution.py:80
  42.6 4.2 %collective-permute-start.4 = (bf16[1664,512]{1,0:T(8,128)(2,1)}, bf16[1664,512]{1,0:T(8,128)(2,1)}, u32[]{:S(2)}, u32[]{:S(2)}) collective-permute-start(bf16[1664,512]{1,0:T(8,128)(2,1)} %get-tuple-element.18), channel_id=1, source_target_pairs={{0,4},{1,5},{2,6},{3,7},{4,8},{5,9},{6,10},{7,11},{8,12},{9,13},{1... | collective-permute-start | bytes 5111816 | tf_op jit(solution)/shard_map/ppermute | solution.py:590
  46.8 3.4 %collective-permute-start.5 = (bf16[1664,512]{1,0:T(8,128)(2,1)}, bf16[1664,512]{1,0:T(8,128)(2,1)}, u32[]{:S(2)}, u32[]{:S(2)}) collective-permute-start(bf16[1664,512]{1,0:T(8,128)(2,1)} %get-tuple-element.19), channel_id=1, source_target_pairs={{0,8},{1,9},{2,10},{3,11},{4,12},{5,13},{6,14},{7,15},{8,0},{9,1},... | collective-permute-start | bytes 5111816 | tf_op jit(solution)/shard_map/ppermute | solution.py:590
  50.2 3.1 %collective-permute-start.6 = (bf16[1664,512]{1,0:T(8,128)(2,1)}, bf16[1664,512]{1,0:T(8,128)(2,1)}, u32[]{:S(2)}, u32[]{:S(2)}) collective-permute-start(bf16[1664,512]{1,0:T(8,128)(2,1)} %get-tuple-element.20), channel_id=1, source_target_pairs={{0,12},{1,13},{2,14},{3,15},{4,0},{5,1},{6,2},{7,3},{8,4},{9,5},{1... | collective-permute-start | bytes 5111816 | tf_op jit(solution)/shard_map/ppermute | solution.py:590
  53.3 0.7 copy.12.weight_ref
  54.1 14.5 %all-to-all-done.1.got = bf16[4,976,512]{2,1,0:T(8,128)(2,1)} async-done(((bf16[4,976,512]{2,1,0:T(8,128)(2,1)}), bf16[4,976,512]{2,1,0:T(8,128)(2,1)}, u32[]{:S(2)}, u32[]{:S(2)}) %all-to-all-start.1) | async-done | bytes 3997728 | tf_op jit(solution)/shard_map/all_to_all | solution.py:80
  68.5 7.4 %shard_map.104 = f32[32,8,128]{2,1,0:T(8,128)} custom-call(bf16[4,976,512]{2,1,0:T(8,128)(2,1)} %all-to-all-done.1.got, bf16[1664,512]{1,0:T(8,128)(2,1)} %get-tuple-element.17.begun.late0, bf16[4,512,512]{2,1,0:T(8,128)(2,1)} %all-to-all-done.got.panel_ref, bf16[2,64,512]{2,1,0:T(8,128)(2,1)} %arrow_ref.3, bf16[2,64,1024]{2,1,0:T(8,128)(2,1)} %x_ref.3, ...), custom_call_target="tpu_custom_call" | custom-call | bytes 20000000 | tf_op jit(solution)/shard_map/pallas_call | solution.py:591
  75.9 35.3 %all_to_all.20 = f32[32,8,128]{2,1,0:T(8,128)S(1)} all-to-all(f32[32,8,128]{2,1,0:T(8,128)} %shard_map.104), channel_id=1, replica_groups={{0,1,2,3,4,5,6,7,8,9,10,11,12,13,14,15,16,17,18,19,20,21,22,23,24,25,26..., dimensions={0} | all-to-all | bytes 262144 | tf_op jit(solution)/shard_map/all_to_all | solution.py:80
  111.3 0.6 broadcast_in_dim.10
  111.9 9.4 %all-to-all-start.3 = ((f32[16,8,128]{2,1,0:T(8,128)}), f32[16,8,128]{2,1,0:T(8,128)S(1)}, u32[]{:S(2)}, u32[]{:S(2)}) async-start(f32[16,8,128]{2,1,0:T(8,128)} %broadcast_in_dim.10), calls=%async_computation.3 | async-start | bytes 131072 | tf_op jit(solution)/shard_map/all_to_all | solution.py:80
  121.4 9.8 %shard_map.105 = (f32[2,64,1024]{2,1,0:T(8,128)}, f32[2,64,1024]{2,1,0:T(8,128)}, f32[2,64,512]{2,1,0:T(8,128)}) custom-call(bf16[4,976,512]{2,1,0:T(8,128)(2,1)} %all-to-all-done.1.got, bf16[1664,512]{1,0:T(8,128)(2,1)} %get-tuple-element.17.begun.late0, bf16[1664,512]{1,0:T(8,128)(2,1)} %collective-permute-done.4.late1, ...), custom_call_target="tpu_custom_call" | custom-call | bytes 30000000 | tf_op jit(solution)/shard_map/pallas_call | solution.py:619
  131.2 1.7 %all-to-all-done.3 = f32[16,8,128]{2,1,0:T(8,128)S(1)} async-done(((f32[16,8,128]{2,1,0:T(8,128)}), f32[16,8,128]{2,1,0:T(8,128)S(1)}, u32[]{:S(2)}, u32[]{:S(2)}) %all-to-all-start.3) | async-done | bytes 65568 | tf_op jit(solution)/shard_map/all_to_all | solution.py:80
  132.9 0.5 slice.3
  (16 shorter events, 0.1 us)
Async XLA Ops:
  3.3 5.2 %copy-start.4 = (bf16[64,1536]{1,0:T(8,128)(2,1)S(1)}, bf16[64,1536]{1,0:T(8,128)(2,1)}, u32[]{:S(2)}) copy-start(bf16[64,1536]{1,0:T(8,128)(2,1)} %get-tuple-element.15) | copy-start | bytes 589828
  3.3 27.9 %all-to-all-start = ((bf16[4,512,512]{2,1,0:T(8,128)(2,1)}), bf16[4,512,512]{2,1,0:T(8,128)(2,1)}, u32[]{:S(2)}, u32[]{:S(2)}) async-start(bf16[4,512,512]{2,1,0:T(8,128)(2,1)} %get-tuple-element.14), calls=%async_computation | async-start | bytes 4194304 | tf_op jit(solution)/shard_map/all_to_all | solution.py:80
  8.5 15.9 %collective-permute-start = (bf16[64,1536]{1,0:T(8,128)(2,1)S(1)}, bf16[64,1536]{1,0:T(8,128)(2,1)S(1)}, u32[]{:S(2)}, u32[]{:S(2)}) collective-permute-start(bf16[64,1536]{1,0:T(8,128)(2,1)S(1)} %copy-done.4), channel_id=1, source_target_pairs={{16,0},{17,1},{18,2},{19,3},{20,4},{21,5},{22,6},{23,7},{24,8},{25... | collective-permute-start | bytes 589832 | tf_op jit(solution)/shard_map/ppermute | solution.py:566
  16.7 11.2 %collective-permute-start.1 = (bf16[64,1536]{1,0:T(8,128)(2,1)S(1)}, bf16[64,1536]{1,0:T(8,128)(2,1)S(1)}, u32[]{:S(2)}, u32[]{:S(2)}) collective-permute-start(bf16[64,1536]{1,0:T(8,128)(2,1)S(1)} %copy-done.4), channel_id=1, source_target_pairs={{16,1},{17,2},{18,3},{19,0},{20,5},{21,6},{22,7},{23,4},{24,9},{25... | collective-permute-start | bytes 589832 | tf_op jit(solution)/shard_map/ppermute | solution.py:566
  19.6 10.6 %collective-permute-start.2 = (bf16[64,1536]{1,0:T(8,128)(2,1)S(1)}, bf16[64,1536]{1,0:T(8,128)(2,1)}, u32[]{:S(2)}, u32[]{:S(2)}) collective-permute-start(bf16[64,1536]{1,0:T(8,128)(2,1)S(1)} %copy-done.4), channel_id=1, source_target_pairs={{16,2},{17,3},{18,0},{19,1},{20,6},{21,7},{22,4},{23,5},{24,10},{2... | collective-permute-start | bytes 589832 | tf_op jit(solution)/shard_map/ppermute | solution.py:566
  22.4 8.8 %collective-permute-start.3 = (bf16[64,1536]{1,0:T(8,128)(2,1)S(1)}, bf16[64,1536]{1,0:T(8,128)(2,1)}, u32[]{:S(2)}, u32[]{:S(2)}) collective-permute-start(bf16[64,1536]{1,0:T(8,128)(2,1)S(1)} %copy-done.4), channel_id=1, source_target_pairs={{16,3},{17,0},{18,1},{19,2},{20,7},{21,4},{22,5},{23,6},{24,11},{2... | collective-permute-start | bytes 589832 | tf_op jit(solution)/shard_map/ppermute | solution.py:566
  24.4 6.9 %copy-start = (bf16[64,1536]{1,0:T(8,128)(2,1)}, bf16[64,1536]{1,0:T(8,128)(2,1)S(1)}, u32[]{:S(2)}) copy-start(bf16[64,1536]{1,0:T(8,128)(2,1)S(1)} %collective-permute-done.own0) | copy-start | bytes 589828
  27.9 3.3 %copy-start.1 = (bf16[64,1536]{1,0:T(8,128)(2,1)}, bf16[64,1536]{1,0:T(8,128)(2,1)S(1)}, u32[]{:S(2)}) copy-start(bf16[64,1536]{1,0:T(8,128)(2,1)S(1)} %collective-permute-done.1.own1) | copy-start | bytes 589828
  37.7 15.6 %copy-start.3 = (f32[2,64]{1,0:T(2,128)S(1)}, f32[2,64]{1,0:T(2,128)}, u32[]{:S(2)}) copy-start(f32[2,64]{1,0:T(2,128)} %weight.1) | copy-start | bytes 1540
  37.8 30.8 %all-to-all-start.1 = ((bf16[4,976,512]{2,1,0:T(8,128)(2,1)}), bf16[4,976,512]{2,1,0:T(8,128)(2,1)}, u32[]{:S(2)}, u32[]{:S(2)}) async-start(bf16[4,976,512]{2,1,0:T(8,128)(2,1)} %get-tuple-element.16), calls=%async_computation.1 | async-start | bytes 7995392 | tf_op jit(solution)/shard_map/all_to_all | solution.py:80
  42.6 78.7 %collective-permute-start.4 = (bf16[1664,512]{1,0:T(8,128)(2,1)}, bf16[1664,512]{1,0:T(8,128)(2,1)}, u32[]{:S(2)}, u32[]{:S(2)}) collective-permute-start(bf16[1664,512]{1,0:T(8,128)(2,1)} %get-tuple-element.18), channel_id=1, source_target_pairs={{0,4},{1,5},{2,6},{3,7},{4,8},{5,9},{6,10},{7,11},{8,12},{9,13},{1... | collective-permute-start | bytes 5111816 | tf_op jit(solution)/shard_map/ppermute | solution.py:590
  46.8 74.5 %collective-permute-start.5 = (bf16[1664,512]{1,0:T(8,128)(2,1)}, bf16[1664,512]{1,0:T(8,128)(2,1)}, u32[]{:S(2)}, u32[]{:S(2)}) collective-permute-start(bf16[1664,512]{1,0:T(8,128)(2,1)} %get-tuple-element.19), channel_id=1, source_target_pairs={{0,8},{1,9},{2,10},{3,11},{4,12},{5,13},{6,14},{7,15},{8,0},{9,1},... | collective-permute-start | bytes 5111816 | tf_op jit(solution)/shard_map/ppermute | solution.py:590
  50.2 71.1 %collective-permute-start.6 = (bf16[1664,512]{1,0:T(8,128)(2,1)}, bf16[1664,512]{1,0:T(8,128)(2,1)}, u32[]{:S(2)}, u32[]{:S(2)}) collective-permute-start(bf16[1664,512]{1,0:T(8,128)(2,1)} %get-tuple-element.20), channel_id=1, source_target_pairs={{0,12},{1,13},{2,14},{3,15},{4,0},{5,1},{6,2},{7,3},{8,4},{9,5},{1... | collective-permute-start | bytes 5111816 | tf_op jit(solution)/shard_map/ppermute | solution.py:590
  111.3 10.1 %copy-start.2 = (f32[8,128]{1,0:T(8,128)}, f32[8,128]{1,0:T(8,128)S(1)}, u32[]{:S(2)}) copy-start(f32[8,128]{1,0:T(8,128)S(1)} %reduce_sum.18.total_ref) | copy-start | bytes 12292
  111.9 21.0 %all-to-all-start.3 = ((f32[16,8,128]{2,1,0:T(8,128)}), f32[16,8,128]{2,1,0:T(8,128)S(1)}, u32[]{:S(2)}, u32[]{:S(2)}) async-start(f32[16,8,128]{2,1,0:T(8,128)} %broadcast_in_dim.10), calls=%async_computation.3 | async-start | bytes 131072 | tf_op jit(solution)/shard_map/all_to_all | solution.py:80

commit v5 on v4

--- a/solution.py
+++ b/solution.py
@@ -149,43 +149,18 @@
 
 
 def panel_kernel(
-    got,
-    arrow,
-    weight,
-    own0,
-    own1,
-    own2,
-    own3,
-    out,
-    late0,
-    late1,
-    late2,
-    late3,
-    panel,
-    state,
-    misc,
-    share,
-    sem_in,
-    sem_out,
-    sem_late,
-    sem_state,
+    got, arrow, weight, own0, own1, own2, own3, out, panel, misc, sem_in, sem_out
 ):
+    del own0, own1, own2, own3
     core, _, first = place()
-    second = jnp.where(core == 0, lax.axis_index("y"), lax.axis_index("x"))
-    loads = [pltpu.make_async_copy(got.at[j], panel.at[j], sem_in.at[j]) for j in range(SIDE)]
+    loads = [
+        pltpu.make_async_copy(got.at[j, pl.ds(0, 2 * PART)], panel.at[j], sem_in.at[j])
+        for j in range(SIDE)
+    ]
     load_arrow = pltpu.make_async_copy(
         arrow.at[0], misc.at[pl.ds(2 * ROWS, ROWS)], sem_in.at[SIDE]
     )
-    loads_state = [
-        pltpu.make_async_copy(
-            own.at[:, pl.ds(h * HALF, HALF)],
-            state.at[pl.ds(k * PART + h * ROWS, ROWS)],
-            sem_state.at[k * 3 + h],
-        )
-        for k, own in enumerate((own0, own1, own2, own3))
-        for h in range(3)
-    ]
-    for copy in loads + [load_arrow] + loads_state:
+    for copy in loads + [load_arrow]:
         copy.start()
     stores = []
     for j in range(SIDE):
@@ -217,27 +192,68 @@
         pltpu.make_async_copy(misc, out.at[d, pl.ds(PANEL, MISC)], sem_out.at[d * (SIDE + 1) + SIDE])
         for d in range(SIDE)
     ]
+    for copy in here:
+        copy.start()
+    for copy in stores + here:
+        copy.wait()
+
+
+def later_kernel(
+    got,
+    own0,
+    own1,
+    own2,
+    own3,
+    late0,
+    late1,
+    late2,
+    late3,
+    panel,
+    state,
+    share,
+    sem_in,
+    sem_out,
+    sem_state,
+):
+    core, _, first = place()
+    second = jnp.where(core == 0, lax.axis_index("y"), lax.axis_index("x"))
     lates = (late0, late1, late2, late3)
+    loads = [
+        pltpu.make_async_copy(got.at[j, pl.ds(PART, SENT - PART)], panel.at[j], sem_in.at[j])
+        for j in range(SIDE)
+    ]
+    loads_state = [
+        pltpu.make_async_copy(
+            own.at[:, pl.ds(h * HALF, HALF)],
+            state.at[pl.ds(k * PART + h * ROWS, ROWS)],
+            sem_state.at[k * 3 + h],
+        )
+        for k, own in enumerate((own0, own1, own2, own3))
+        for h in range(3)
+    ]
+    for copy in loads + loads_state:
+        copy.start()
+    for copy in loads + loads_state:
+        copy.wait()
+    stores = []
     for k, late in enumerate(lates):
-        here += [
+        stores += [
             pltpu.make_async_copy(
-                panel.at[j, pl.ds(PART, PART)],
+                panel.at[j, pl.ds(0, PART)],
                 late.at[pl.ds(j * PART, PART)],
-                sem_late.at[k * (SIDE + 1) + j],
+                sem_out.at[k * (SIDE + 1) + j],
             )
             for j in range(SIDE)
         ]
-    for copy in loads_state:
-        copy.wait()
-    here += [
-        pltpu.make_async_copy(state, late.at[pl.ds(LATER, PANEL)], sem_state.at[12 + k])
-        for k, late in enumerate(lates)
-    ]
-    for copy in here:
-        copy.start()
-    stores += here
+        stores.append(
+            pltpu.make_async_copy(state, late.at[pl.ds(LATER, PANEL)], sem_state.at[12 + k])
+        )
+    for copy in stores:
+        copy.start()
+    cols = [columns_t(panel, 0, natural(core, d, first)) for d in range(SIDE)]
+    cols = jnp.concatenate(cols, axis=0)
     for h in range(2):
-        at = (X1 + h) * ROWS
+        at = PART + h * ROWS
         part = dot(cols, panel[:, at : at + ROWS, :].reshape(SIDE * ROWS, HALF))
         for d in range(SIDE):
             share[d, h * ROWS : (h + 1) * ROWS, :] = part[d * ROWS : (d + 1) * ROWS].astype(BF)
@@ -245,7 +261,7 @@
         pltpu.make_async_copy(
             share.at[lax.rem(second + k, SIDE)],
             late.at[pl.ds(PANEL, SHARE)],
-            sem_late.at[k * (SIDE + 1) + SIDE],
+            sem_out.at[k * (SIDE + 1) + SIDE],
         )
         for k, late in enumerate(lates)
     ]
@@ -412,7 +428,6 @@
     arrow_ref,
     x_ref,
     q_ref,
-    total_ref,
     diag_ref,
     lower_ref,
     tip_ref,
@@ -434,7 +449,6 @@
     sem_in,
     sem_out,
 ):
-    del total_ref
     core, row, first = place()
     second = jnp.where(core == 0, lax.axis_index("y"), lax.axis_index("x"))
     loads1 = [
@@ -564,33 +578,43 @@
     )(lower_factor, arrow_factor, block_inverse, boundary_sigma, boundary_tip)
     got = exchange(rows, line_groups(partitions, 0))
     starts = [lax.ppermute(start, EVERY, state_shift(partitions, k)) for k in range(SIDE)]
-    sent, *lates = pl.pallas_call(
+    sent = pl.pallas_call(
         panel_kernel,
-        out_shape=(
-            jax.ShapeDtypeStruct((SIDE, PANEL + MISC, HALF), BF),
-        )
-        + (jax.ShapeDtypeStruct((LATER + PANEL, HALF), BF),) * SIDE,
+        out_shape=jax.ShapeDtypeStruct((SIDE, PANEL + MISC, HALF), BF),
         in_specs=[slow, slow, fast] + [slow] * SIDE,
-        out_specs=(slow,) * 5,
+        out_specs=slow,
         scratch_shapes=[
-            pltpu.VMEM((SIDE, SENT, HALF), BF),
-            pltpu.VMEM((PANEL, HALF), BF),
+            pltpu.VMEM((SIDE, 2 * PART, HALF), BF),
             pltpu.VMEM((MISC, HALF), BF),
-            pltpu.VMEM((SIDE, SHARE, HALF), BF),
             pltpu.SemaphoreType.DMA((SIDE + 1,)),
             pltpu.SemaphoreType.DMA((SIDE * (SIDE + 1),)),
+        ],
+        compiler_params=params,
+        cost_estimate=cost(12),
+    )(got, arrow_factor, slope_weights, *starts)
+    lates = pl.pallas_call(
+        later_kernel,
+        out_shape=(jax.ShapeDtypeStruct((LATER + PANEL, HALF), BF),) * SIDE,
+        in_specs=[slow] * 5,
+        out_specs=(slow,) * 4,
+        scratch_shapes=[
+            pltpu.VMEM((SIDE, SENT - PART, HALF), BF),
+            pltpu.VMEM((PANEL, HALF), BF),
+            pltpu.VMEM((SIDE, SHARE, HALF), BF),
+            pltpu.SemaphoreType.DMA((SIDE,)),
             pltpu.SemaphoreType.DMA((SIDE * (SIDE + 1),)),
             pltpu.SemaphoreType.DMA((16,)),
         ],
         compiler_params=params,
         cost_estimate=cost(12),
-    )(got, arrow_factor, slope_weights, *starts)
+    )(got, *starts)
+    lates = list(lates)
     early = exchange(sent, line_groups(partitions, 1))
     for k in range(1, SIDE):
         lates[k] = lax.ppermute(lates[k], EVERY, line_shift(partitions, k))
     slope = pl.pallas_call(
         trace_kernel,
-        out_shape=jax.ShapeDtypeStruct((32, 8, 128), F32),
+        out_shape=jax.ShapeDtypeStruct((partitions // 2, 8, 128), F32),
         in_specs=[slow] * 6 + [fast],
         out_specs=fast,
         scratch_shapes=[
@@ -607,10 +631,9 @@
         compiler_params=params,
         cost_estimate=cost(20),
     )(early, lates[0], got, arrow_factor, block_inverse, tip_inverse, slope_weights[:, :, None])
-    total = jnp.sum(exchange(slope, plane_groups(partitions)), axis=0)
-    in_plane = total
-    total = jnp.broadcast_to(total[None], (partitions // 2, 8, 128))
-    total = jnp.sum(exchange(total, height_groups(partitions)), axis=0)
+    total = jnp.sum(exchange(slope, height_groups(partitions)), axis=0)
+    total = jnp.broadcast_to(total[None], (2 * SIDE * SIDE, 8, 128))
+    total = jnp.sum(exchange(total, plane_groups(partitions)), axis=0)
     outputs = (
         jax.ShapeDtypeStruct((2, ROWS, BLOCK), F32),
         jax.ShapeDtypeStruct((2, ROWS, BLOCK), F32),
@@ -619,7 +642,7 @@
     diag, lower, tip = pl.pallas_call(
         block_kernel,
         out_shape=outputs,
-        in_specs=[slow] * 9,
+        in_specs=[slow] * 8,
         out_specs=(slow,) * 3,
         scratch_shapes=[
             pltpu.VMEM((16, PART, HALF), BF),
@@ -642,7 +665,7 @@
         ],
         compiler_params=params,
         cost_estimate=cost(30),
-    )(early, *lates, arrow_factor, block_inverse, tip_inverse, in_plane)
+    )(early, *lates, arrow_factor, block_inverse, tip_inverse)
     return diag, lower, tip, total[0, 0]
 
 

time: 134 us -> 117 us (0.87)
  blocking collectives: 35.3 us -> 24 us
  waiting for transfers between devices: 23 us -> 15.7 us
  Pallas kernels: 26.4 us -> 28.4 us
    all_to_all x1, blocking collectives: 35.3 us -> 24 us  [exchange(): lax.all_to_all(value, EVERY, 0, 0, tiled=True, axis_index_groups=groups)]
    all_to_all x3, waiting for transfers between devices: 16.2 us -> 9.66 us  [exchange(): lax.all_to_all(value, EVERY, 0, 0, tiled=True, axis_index_groups=groups)]
    pallas_call x3 -> x4, Pallas kernels: 23.7 us -> 25.8 us  [the longest x1 9.79 us: on_device(): pl.pallas_call(block_kernel, out_shape=outputs, in_specs=[slow] * 8, out_...]
    all_to_all x3, starting transfers between devices: 19.4 us -> 17.8 us  [exchange(): lax.all_to_all(value, EVERY, 0, 0, tiled=True, axis_index_groups=groups)]
  transfers between devices with their start and end apart: 10 -> 10, of which waited for: 5 -> 3; matrix products, arithmetic and copies ran while one was open for 1% -> 1% of each run, Pallas kernels for 13% -> 19%
where the time goes in v5:
time: 117 us; the launch traced here: 116 us
  starting transfers between devices  45.3 us (39%)
  Pallas kernels  28.4 us (24%)
  blocking collectives  24 us (21%)
  waiting for transfers between devices  15.7 us (13%)
  local copies, waits for them, and re-layouts  1.93 us (2%)
    all_to_all x1, blocking collectives, exchange(): lax.all_to_all(value, EVERY, 0, 0, tiled=True, axis_index_groups=groups)  24 us
    all_to_all x3, starting transfers between devices, exchange(): lax.all_to_all(value, EVERY, 0, 0, tiled=True, axis_index_groups=groups)  17.8 us
    ppermute x4, starting transfers between devices, on_device(): lax.ppermute(start, EVERY, state_shift(partitions, k))  16.8 us
    ppermute x3, starting transfers between devices, on_device(): lates[k] = lax.ppermute(lates[k], EVERY, line_shift(partitions, k))  10.7 us
    pallas_call x1, Pallas kernels, on_device(): pl.pallas_call(block_kernel, out_shape=outputs, in_specs=[slow] * 8, out_...  9.79 us
    all_to_all x3, waiting for transfers between devices, exchange(): lax.all_to_all(value, EVERY, 0, 0, tiled=True, axis_index_groups=groups)  9.66 us
    pallas_call x1, Pallas kernels, on_device(): pl.pallas_call(trace_kernel, out_shape=jax.ShapeDtypeStruct((partitions /...  7.38 us
    ppermute x4, waiting for transfers between devices, on_device(): lax.ppermute(start, EVERY, state_shift(partitions, k))  6.04 us
  transfers between devices with their start and end apart: 10, of which 3 were waited for; matrix products, arithmetic and copies ran while one was open for 1% of the time, Pallas kernels for 19%

profile of v5, /device:TPU:1, one launch (start us, length us, event | category | flops | bytes accessed | tf_op | source)
XLA Modules:
  0.0 116.2 jit_solution(12947893724103092315)
XLA Ops:
  0.6 2.6 %shard_map.102 = (bf16[4,512,512]{2,1,0:T(8,128)(2,1)}, bf16[64,1536]{1,0:T(8,128)(2,1)}) custom-call(bf16[2,64,1024]{2,1,0:T(8,128)(2,1)} %low.1, bf16[2,64,512]{2,1,0:T(8,128)(2,1)} %arrow_ref.3, bf16[2,64,1024]{2,1,0:T(8,128)(2,1)} %x_ref.3, bf16[1,64,1024]{2,1,0:T(8,128)(2,1)} %sigma.1, bf16[1,64,512]{2,1,0:T(8,128)(2,1)} %tip.1), custom_call_target="tpu_custom_call" | custom-call | bytes 4000000 | tf_op jit(solution)/shard_map/pallas_call | solution.py:561
  3.3 5.2 %all-to-all-start = ((bf16[4,512,512]{2,1,0:T(8,128)(2,1)}), bf16[4,512,512]{2,1,0:T(8,128)(2,1)}, u32[]{:S(2)}, u32[]{:S(2)}) async-start(bf16[4,512,512]{2,1,0:T(8,128)(2,1)} %get-tuple-element.13), calls=%async_computation | async-start | bytes 4194304 | tf_op jit(solution)/shard_map/all_to_all | solution.py:80
  8.5 11.1 %collective-permute-start.3 = (bf16[64,1536]{1,0:T(8,128)(2,1)S(1)}, bf16[64,1536]{1,0:T(8,128)(2,1)S(1)}, u32[]{:S(2)}, u32[]{:S(2)}) collective-permute-start(bf16[64,1536]{1,0:T(8,128)(2,1)S(1)} %copy-done.3), channel_id=1, source_target_pairs={{16,3},{17,0},{18,1},{19,2},{20,7},{21,4},{22,5},{23,6},{24,11},{2... | collective-permute-start | bytes 589832 | tf_op jit(solution)/shard_map/ppermute | solution.py:580
  19.5 1.9 %collective-permute-start.2 = (bf16[64,1536]{1,0:T(8,128)(2,1)S(1)}, bf16[64,1536]{1,0:T(8,128)(2,1)S(1)}, u32[]{:S(2)}, u32[]{:S(2)}) collective-permute-start(bf16[64,1536]{1,0:T(8,128)(2,1)S(1)} %copy-done.3), channel_id=1, source_target_pairs={{16,2},{17,3},{18,0},{19,1},{20,6},{21,7},{22,4},{23,5},{24,10},{2... | collective-permute-start | bytes 589832 | tf_op jit(solution)/shard_map/ppermute | solution.py:580
  21.4 1.9 %collective-permute-start.1 = (bf16[64,1536]{1,0:T(8,128)(2,1)S(1)}, bf16[64,1536]{1,0:T(8,128)(2,1)}, u32[]{:S(2)}, u32[]{:S(2)}) collective-permute-start(bf16[64,1536]{1,0:T(8,128)(2,1)S(1)} %copy-done.3), channel_id=1, source_target_pairs={{16,1},{17,2},{18,3},{19,0},{20,5},{21,6},{22,7},{23,4},{24,9},{25... | collective-permute-start | bytes 589832 | tf_op jit(solution)/shard_map/ppermute | solution.py:580
  23.4 1.9 %collective-permute-start = (bf16[64,1536]{1,0:T(8,128)(2,1)S(1)}, bf16[64,1536]{1,0:T(8,128)(2,1)}, u32[]{:S(2)}, u32[]{:S(2)}) collective-permute-start(bf16[64,1536]{1,0:T(8,128)(2,1)S(1)} %copy-done.3), channel_id=1, source_target_pairs={{16,0},{17,1},{18,2},{19,3},{20,4},{21,5},{22,6},{23,7},{24,8},{25... | collective-permute-start | bytes 589832 | tf_op jit(solution)/shard_map/ppermute | solution.py:580
  25.3 0.0 copy-start
  25.3 4.0 %collective-permute-done.2.own2 = bf16[64,1536]{1,0:T(8,128)(2,1)S(1)} collective-permute-done((bf16[64,1536]{1,0:T(8,128)(2,1)S(1)}, bf16[64,1536]{1,0:T(8,128)(2,1)S(1)}, u32[]{:S(2)}, u32[]{:S(2)}) %collective-permute-start.2) | collective-permute-done | bytes 196640 | tf_op jit(solution)/shard_map/ppermute | solution.py:580
  29.4 2.0 %collective-permute-done.1.own1 = bf16[64,1536]{1,0:T(8,128)(2,1)} collective-permute-done((bf16[64,1536]{1,0:T(8,128)(2,1)S(1)}, bf16[64,1536]{1,0:T(8,128)(2,1)}, u32[]{:S(2)}, u32[]{:S(2)}) %collective-permute-start.1) | collective-permute-done | bytes 196640 | tf_op jit(solution)/shard_map/ppermute | solution.py:580
  31.4 3.8 %shard_map.103 = bf16[4,976,512]{2,1,0:T(8,128)(2,1)} custom-call(bf16[4,512,512]{2,1,0:T(8,128)(2,1)} %all-to-all-done.got.panel_ref, bf16[2,64,512]{2,1,0:T(8,128)(2,1)} %arrow_ref.3, f32[2,64]{1,0:T(2,128)} %weight.1, bf16[64,1536]{1,0:T(8,128)(2,1)} %collective-permute-done.own0, bf16[64,1536]{1,0:T(8,128)(2,1)} %collective-permute-done.1.own1, ...), custom_call_target="tpu_custom_call" | custom-call | bytes 12000000 | tf_op jit(solution)/shard_map/pallas_call | solution.py:581
  35.2 4.8 %all-to-all-start.1 = ((bf16[4,976,512]{2,1,0:T(8,128)(2,1)}), bf16[4,976,512]{2,1,0:T(8,128)(2,1)}, u32[]{:S(2)}, u32[]{:S(2)}) async-start(bf16[4,976,512]{2,1,0:T(8,128)(2,1)} %shard_map.103), calls=%async_computation.1 | async-start | bytes 7995392 | tf_op jit(solution)/shard_map/all_to_all | solution.py:80
  40.0 0.0 copy-start.2
  40.0 4.8 %shard_map.104 = (bf16[1664,512]{1,0:T(8,128)(2,1)}, bf16[1664,512]{1,0:T(8,128)(2,1)}, bf16[1664,512]{1,0:T(8,128)(2,1)}, bf16[1664,512]{1,0:T(8,128)(2,1)}) custom-call(bf16[4,512,512]{2,1,0:T(8,128)(2,1)} %all-to-all-done.got.panel_ref, bf16[64,1536]{1,0:T(8,128)(2,1)} %collective-permute-done.own0, bf16[64,1536]{1,0:T(8,128)(2,1)} %collective-permute-done.1.own1, ...), custom_call_target="tpu_custom_call" | custom-call | bytes 12000000 | tf_op jit(solution)/shard_map/pallas_call | solution.py:595
  44.8 3.4 %collective-permute-start.4 = (bf16[1664,512]{1,0:T(8,128)(2,1)}, bf16[1664,512]{1,0:T(8,128)(2,1)}, u32[]{:S(2)}, u32[]{:S(2)}) collective-permute-start(bf16[1664,512]{1,0:T(8,128)(2,1)} %get-tuple-element.16), channel_id=1, source_target_pairs={{0,4},{1,5},{2,6},{3,7},{4,8},{5,9},{6,10},{7,11},{8,12},{9,13},{1... | collective-permute-start | bytes 5111816 | tf_op jit(solution)/shard_map/ppermute | solution.py:614
  48.3 4.2 %collective-permute-start.5 = (bf16[1664,512]{1,0:T(8,128)(2,1)}, bf16[1664,512]{1,0:T(8,128)(2,1)}, u32[]{:S(2)}, u32[]{:S(2)}) collective-permute-start(bf16[1664,512]{1,0:T(8,128)(2,1)} %get-tuple-element.17), channel_id=1, source_target_pairs={{0,8},{1,9},{2,10},{3,11},{4,12},{5,13},{6,14},{7,15},{8,0},{9,1},... | collective-permute-start | bytes 5111816 | tf_op jit(solution)/shard_map/ppermute | solution.py:614
  52.5 3.1 %collective-permute-start.6 = (bf16[1664,512]{1,0:T(8,128)(2,1)}, bf16[1664,512]{1,0:T(8,128)(2,1)}, u32[]{:S(2)}, u32[]{:S(2)}) collective-permute-start(bf16[1664,512]{1,0:T(8,128)(2,1)} %get-tuple-element.18), channel_id=1, source_target_pairs={{0,12},{1,13},{2,14},{3,15},{4,0},{5,1},{6,2},{7,3},{8,4},{9,5},{1... | collective-permute-start | bytes 5111816 | tf_op jit(solution)/shard_map/ppermute | solution.py:614
  55.6 0.7 copy.12.weight_ref
  56.3 9.7 %all-to-all-done.1.got = bf16[4,976,512]{2,1,0:T(8,128)(2,1)} async-done(((bf16[4,976,512]{2,1,0:T(8,128)(2,1)}), bf16[4,976,512]{2,1,0:T(8,128)(2,1)}, u32[]{:S(2)}, u32[]{:S(2)}) %all-to-all-start.1) | async-done | bytes 3997728 | tf_op jit(solution)/shard_map/all_to_all | solution.py:80
  66.0 7.4 %shard_map.106 = f32[16,8,128]{2,1,0:T(8,128)} custom-call(bf16[4,976,512]{2,1,0:T(8,128)(2,1)} %all-to-all-done.1.got, bf16[1664,512]{1,0:T(8,128)(2,1)} %get-tuple-element.15.late0.begun, bf16[4,512,512]{2,1,0:T(8,128)(2,1)} %all-to-all-done.got.panel_ref, bf16[2,64,512]{2,1,0:T(8,128)(2,1)} %arrow_ref.3, bf16[2,64,1024]{2,1,0:T(8,128)(2,1)} %x_ref.3, ...), custom_call_target="tpu_custom_call" | custom-call | bytes 20000000 | tf_op jit(solution)/shard_map/pallas_call | solution.py:615
  73.3 24.0 %all_to_all.20 = f32[16,8,128]{2,1,0:T(8,128)S(1)} all-to-all(f32[16,8,128]{2,1,0:T(8,128)} %shard_map.106), channel_id=1, replica_groups={{0,32,64,96,128,160,192,224,256,288,320,352,384,416,448,480},{1,33,65,9..., dimensions={0} | all-to-all | bytes 131072 | tf_op jit(solution)/shard_map/all_to_all | solution.py:80
  97.3 0.7 broadcast_in_dim.10
  98.0 7.8 %all-to-all-start.3 = ((f32[32,8,128]{2,1,0:T(8,128)}), f32[32,8,128]{2,1,0:T(8,128)S(1)}, u32[]{:S(2)}, u32[]{:S(2)}) async-start(f32[32,8,128]{2,1,0:T(8,128)} %broadcast_in_dim.10), calls=%async_computation.3 | async-start | bytes 262144 | tf_op jit(solution)/shard_map/all_to_all | solution.py:80
  105.8 9.8 %shard_map.105 = (f32[2,64,1024]{2,1,0:T(8,128)}, f32[2,64,1024]{2,1,0:T(8,128)}, f32[2,64,512]{2,1,0:T(8,128)}) custom-call(bf16[4,976,512]{2,1,0:T(8,128)(2,1)} %all-to-all-done.1.got, bf16[1664,512]{1,0:T(8,128)(2,1)} %get-tuple-element.15.late0.begun, bf16[1664,512]{1,0:T(8,128)(2,1)} %collective-permute-done.4.late1, ...), custom_call_target="tpu_custom_call" | custom-call | bytes 30000000 | tf_op jit(solution)/shard_map/pallas_call | solution.py:642
  115.7 0.5 slice.3
  (15 shorter events, 0.1 us)
Async XLA Ops:
  3.3 5.2 %copy-start.3 = (bf16[64,1536]{1,0:T(8,128)(2,1)S(1)}, bf16[64,1536]{1,0:T(8,128)(2,1)}, u32[]{:S(2)}) copy-start(bf16[64,1536]{1,0:T(8,128)(2,1)} %get-tuple-element.14) | copy-start | bytes 589828
  3.3 28.1 %all-to-all-start = ((bf16[4,512,512]{2,1,0:T(8,128)(2,1)}), bf16[4,512,512]{2,1,0:T(8,128)(2,1)}, u32[]{:S(2)}, u32[]{:S(2)}) async-start(bf16[4,512,512]{2,1,0:T(8,128)(2,1)} %get-tuple-element.13), calls=%async_computation | async-start | bytes 4194304 | tf_op jit(solution)/shard_map/all_to_all | solution.py:80
  8.5 16.9 %collective-permute-start.3 = (bf16[64,1536]{1,0:T(8,128)(2,1)S(1)}, bf16[64,1536]{1,0:T(8,128)(2,1)S(1)}, u32[]{:S(2)}, u32[]{:S(2)}) collective-permute-start(bf16[64,1536]{1,0:T(8,128)(2,1)S(1)} %copy-done.3), channel_id=1, source_target_pairs={{16,3},{17,0},{18,1},{19,2},{20,7},{21,4},{22,5},{23,6},{24,11},{2... | collective-permute-start | bytes 589832 | tf_op jit(solution)/shard_map/ppermute | solution.py:580
  19.5 9.9 %collective-permute-start.2 = (bf16[64,1536]{1,0:T(8,128)(2,1)S(1)}, bf16[64,1536]{1,0:T(8,128)(2,1)S(1)}, u32[]{:S(2)}, u32[]{:S(2)}) collective-permute-start(bf16[64,1536]{1,0:T(8,128)(2,1)S(1)} %copy-done.3), channel_id=1, source_target_pairs={{16,2},{17,3},{18,0},{19,1},{20,6},{21,7},{22,4},{23,5},{24,10},{2... | collective-permute-start | bytes 589832 | tf_op jit(solution)/shard_map/ppermute | solution.py:580
  21.4 9.9 %collective-permute-start.1 = (bf16[64,1536]{1,0:T(8,128)(2,1)S(1)}, bf16[64,1536]{1,0:T(8,128)(2,1)}, u32[]{:S(2)}, u32[]{:S(2)}) collective-permute-start(bf16[64,1536]{1,0:T(8,128)(2,1)S(1)} %copy-done.3), channel_id=1, source_target_pairs={{16,1},{17,2},{18,3},{19,0},{20,5},{21,6},{22,7},{23,4},{24,9},{25... | collective-permute-start | bytes 589832 | tf_op jit(solution)/shard_map/ppermute | solution.py:580
  23.4 8.0 %collective-permute-start = (bf16[64,1536]{1,0:T(8,128)(2,1)S(1)}, bf16[64,1536]{1,0:T(8,128)(2,1)}, u32[]{:S(2)}, u32[]{:S(2)}) collective-permute-start(bf16[64,1536]{1,0:T(8,128)(2,1)S(1)} %copy-done.3), channel_id=1, source_target_pairs={{16,0},{17,1},{18,2},{19,3},{20,4},{21,5},{22,6},{23,7},{24,8},{25... | collective-permute-start | bytes 589832 | tf_op jit(solution)/shard_map/ppermute | solution.py:580
  25.3 6.1 %copy-start = (bf16[64,1536]{1,0:T(8,128)(2,1)}, bf16[64,1536]{1,0:T(8,128)(2,1)S(1)}, u32[]{:S(2)}) copy-start(bf16[64,1536]{1,0:T(8,128)(2,1)S(1)} %collective-permute-done.3.own3) | copy-start | bytes 589828
  29.4 2.0 %copy-start.1 = (bf16[64,1536]{1,0:T(8,128)(2,1)}, bf16[64,1536]{1,0:T(8,128)(2,1)S(1)}, u32[]{:S(2)}) copy-start(bf16[64,1536]{1,0:T(8,128)(2,1)S(1)} %collective-permute-done.2.own2) | copy-start | bytes 589828
  35.2 30.8 %all-to-all-start.1 = ((bf16[4,976,512]{2,1,0:T(8,128)(2,1)}), bf16[4,976,512]{2,1,0:T(8,128)(2,1)}, u32[]{:S(2)}, u32[]{:S(2)}) async-start(bf16[4,976,512]{2,1,0:T(8,128)(2,1)} %shard_map.103), calls=%async_computation.1 | async-start | bytes 7995392 | tf_op jit(solution)/shard_map/all_to_all | solution.py:80
  40.0 15.5 %copy-start.2 = (f32[2,64]{1,0:T(2,128)S(1)}, f32[2,64]{1,0:T(2,128)}, u32[]{:S(2)}) copy-start(f32[2,64]{1,0:T(2,128)} %weight.1) | copy-start | bytes 1540
  44.8 61.0 %collective-permute-start.4 = (bf16[1664,512]{1,0:T(8,128)(2,1)}, bf16[1664,512]{1,0:T(8,128)(2,1)}, u32[]{:S(2)}, u32[]{:S(2)}) collective-permute-start(bf16[1664,512]{1,0:T(8,128)(2,1)} %get-tuple-element.16), channel_id=1, source_target_pairs={{0,4},{1,5},{2,6},{3,7},{4,8},{5,9},{6,10},{7,11},{8,12},{9,13},{1... | collective-permute-start | bytes 5111816 | tf_op jit(solution)/shard_map/ppermute | solution.py:614
  48.3 57.5 %collective-permute-start.5 = (bf16[1664,512]{1,0:T(8,128)(2,1)}, bf16[1664,512]{1,0:T(8,128)(2,1)}, u32[]{:S(2)}, u32[]{:S(2)}) collective-permute-start(bf16[1664,512]{1,0:T(8,128)(2,1)} %get-tuple-element.17), channel_id=1, source_target_pairs={{0,8},{1,9},{2,10},{3,11},{4,12},{5,13},{6,14},{7,15},{8,0},{9,1},... | collective-permute-start | bytes 5111816 | tf_op jit(solution)/shard_map/ppermute | solution.py:614
  52.5 53.4 %collective-permute-start.6 = (bf16[1664,512]{1,0:T(8,128)(2,1)}, bf16[1664,512]{1,0:T(8,128)(2,1)}, u32[]{:S(2)}, u32[]{:S(2)}) collective-permute-start(bf16[1664,512]{1,0:T(8,128)(2,1)} %get-tuple-element.18), channel_id=1, source_target_pairs={{0,12},{1,13},{2,14},{3,15},{4,0},{5,1},{6,2},{7,3},{8,4},{9,5},{1... | collective-permute-start | bytes 5111816 | tf_op jit(solution)/shard_map/ppermute | solution.py:614
  98.0 17.6 %all-to-all-start.3 = ((f32[32,8,128]{2,1,0:T(8,128)}), f32[32,8,128]{2,1,0:T(8,128)S(1)}, u32[]{:S(2)}, u32[]{:S(2)}) async-start(f32[32,8,128]{2,1,0:T(8,128)} %broadcast_in_dim.10), calls=%async_computation.3 | async-start | bytes 262144 | tf_op jit(solution)/shard_map/all_to_all | solution.py:80

commit v6 on v5

--- a/solution.py
+++ b/solution.py
@@ -138,12 +138,22 @@
     ]
     for copy in loads + loads_own:
         copy.start()
-    for copy in loads + loads_own:
-        copy.wait()
-    stores = [pltpu.make_async_copy(held, out.at[d], sem_out.at[d]) for d in range(SIDE)]
-    stores.append(pltpu.make_async_copy(own, start, sem_out.at[SIDE]))
-    for copy in stores:
-        copy.start()
+    stores = []
+    for h in range(2):
+        for copy in loads[4 * h : 4 * h + 4]:
+            copy.wait()
+        rows = pl.ds(h * SENT // 2, SENT // 2)
+        here = [
+            pltpu.make_async_copy(held.at[rows], out.at[d, rows], sem_out.at[d * 2 + h])
+            for d in range(SIDE)
+        ]
+        for copy in here:
+            copy.start()
+        stores += here
+    for copy in loads_own:
+        copy.wait()
+    stores.append(pltpu.make_async_copy(own, start, sem_out.at[2 * SIDE]))
+    stores[-1].start()
     for copy in stores:
         copy.wait()
 
@@ -154,7 +164,7 @@
     del own0, own1, own2, own3
     core, _, first = place()
     loads = [
-        pltpu.make_async_copy(got.at[j, pl.ds(0, 2 * PART)], panel.at[j], sem_in.at[j])
+        pltpu.make_async_copy(got.at[j, pl.ds(0, 5 * ROWS)], panel.at[j], sem_in.at[j])
         for j in range(SIDE)
     ]
     load_arrow = pltpu.make_async_copy(
@@ -204,10 +214,11 @@
     own1,
     own2,
     own3,
-    late0,
-    late1,
-    late2,
-    late3,
+    begun0,
+    begun1,
+    begun2,
+    begun3,
+    late,
     panel,
     state,
     share,
@@ -217,7 +228,7 @@
 ):
     core, _, first = place()
     second = jnp.where(core == 0, lax.axis_index("y"), lax.axis_index("x"))
-    lates = (late0, late1, late2, late3)
+    all_begun = (begun0, begun1, begun2, begun3)
     loads = [
         pltpu.make_async_copy(got.at[j, pl.ds(PART, SENT - PART)], panel.at[j], sem_in.at[j])
         for j in range(SIDE)
@@ -235,19 +246,19 @@
         copy.start()
     for copy in loads + loads_state:
         copy.wait()
-    stores = []
-    for k, late in enumerate(lates):
+    stores = [
+        pltpu.make_async_copy(state, begun.at[pl.ds(0, PANEL)], sem_state.at[12 + k])
+        for k, begun in enumerate(all_begun)
+    ]
+    for k, (ref, at) in enumerate(((late, 0), (begun2, LATER))):
         stores += [
             pltpu.make_async_copy(
                 panel.at[j, pl.ds(0, PART)],
-                late.at[pl.ds(j * PART, PART)],
-                sem_out.at[k * (SIDE + 1) + j],
+                ref.at[pl.ds(at + j * PART, PART)],
+                sem_out.at[k * SIDE + j],
             )
             for j in range(SIDE)
         ]
-        stores.append(
-            pltpu.make_async_copy(state, late.at[pl.ds(LATER, PANEL)], sem_state.at[12 + k])
-        )
     for copy in stores:
         copy.start()
     cols = [columns_t(panel, 0, natural(core, d, first)) for d in range(SIDE)]
@@ -260,10 +271,10 @@
     here = [
         pltpu.make_async_copy(
             share.at[lax.rem(second + k, SIDE)],
-            late.at[pl.ds(PANEL, SHARE)],
-            sem_out.at[k * (SIDE + 1) + SIDE],
+            begun.at[pl.ds(PANEL, SHARE)],
+            sem_out.at[2 * SIDE + k],
         )
-        for k, late in enumerate(lates)
+        for k, begun in enumerate(all_begun)
     ]
     for copy in here:
         copy.start()
@@ -340,7 +351,7 @@
     load_misc = pltpu.make_async_copy(got.at[:, pl.ds(PANEL, MISC)], misc, sem_in.at[0])
     load_factor = load_exchanged(got, factor, sem_factor)
     later = [
-        pltpu.make_async_copy(begun.at[pl.ds(LATER, PANEL)], state, sem_in.at[1]),
+        pltpu.make_async_copy(begun.at[pl.ds(0, PANEL)], state, sem_in.at[1]),
         pltpu.make_async_copy(
             panel_ref.at[:, pl.ds(X1 * ROWS, 2 * ROWS)], inverse, sem_in.at[2]
         ),
@@ -399,8 +410,9 @@
         own_parts = jnp.where(second == d, parts[d], own_parts)
     traced = (u_mine * through[:256] + own_parts.astype(F32) * carried) * weights[0]
     traced += z1_mine.astype(F32) * through[256:] * weights[1]
-    own_tip = dot(z0_own(misc, second, core), Gathered(factor).piece(2))
-    own_tip = own_tip - arrow[0].astype(F32)
+    own_tip = u_tip[:ROWS]
+    for d in range(1, SIDE):
+        own_tip = jnp.where(second == d, u_tip[d * ROWS : (d + 1) * ROWS], own_tip)
     both = jnp.concatenate([own_tip.astype(BF), arrow[1]], axis=0)
     tip_traced = both.astype(F32) * dot(both, q[...])
     at = lax.broadcasted_iota(jnp.int32, (ROWS, BLOCK), 0) + row * ROWS
@@ -419,125 +431,221 @@
     return in_order(core, [misc[d, rows, lanes] for d in range(SIDE)])
 
 
-def block_kernel(
+def sum_kernel(parts, after, out):
+    del after
+    out[...] = jnp.broadcast_to(jnp.sum(parts[...], axis=0)[None], out.shape)
+
+
+def own_kernel(
     got,
-    late0,
-    late1,
-    late2,
-    late3,
+    begun,
     arrow_ref,
+    lower_ref,
+    rows_ref,
+    rows_tip_ref,
+    factor,
+    misc,
+    own,
+    arrow,
+    lower,
+    rows,
+    rows_tip,
+    sem_factor,
+    sem_in,
+    sem_out,
+):
+    core, row, _ = place()
+    second = jnp.where(core == 0, lax.axis_index("y"), lax.axis_index("x"))
+    loads = [
+        pltpu.make_async_copy(got.at[:, pl.ds(PANEL, MISC)], misc, sem_in.at[0]),
+        pltpu.make_async_copy(arrow_ref, arrow, sem_in.at[1]),
+        pltpu.make_async_copy(begun.at[pl.ds(0, PART)], own, sem_in.at[2]),
+    ] + load_exchanged(got, factor, sem_factor)
+    for copy in loads:
+        copy.start()
+    for copy in loads:
+        copy.wait()
+    have = Gathered(factor)
+    u, u_tip = have.past(z0_own(misc, second, core))
+    uh, ul = split(u)
+    uh_tip, ul_tip = split(u_tip - arrow[0].astype(F32))
+    rows[...] = jnp.concatenate([columns_t(factor, 0, row), uh, ul], axis=0)
+    rows_tip[...] = jnp.concatenate([arrow[1], uh_tip, ul_tip], axis=0)
+    stores = [
+        pltpu.make_async_copy(rows, rows_ref, sem_out.at[0]),
+        pltpu.make_async_copy(rows_tip, rows_tip_ref, sem_out.at[1]),
+    ]
+    for copy in stores:
+        copy.start()
+    own_rows = jnp.concatenate([own[:ROWS], own[ROWS : 2 * ROWS]], axis=1)
+    lower[...] = -have.times_factor(own_rows, own[2 * ROWS :])
+    stores.append(pltpu.make_async_copy(lower, lower_ref, sem_out.at[2]))
+    stores[-1].start()
+    for copy in stores:
+        copy.wait()
+
+
+def first_kernel(
+    got,
+    begun0,
+    begun1,
+    begun2,
+    begun3,
     x_ref,
     q_ref,
+    own_ref,
+    own_tip_ref,
     diag_ref,
-    lower_ref,
     tip_ref,
-    factor1,
-    factor0,
+    rows_ref,
+    rows_tip_ref,
+    factor,
     state,
     shares,
-    misc,
-    arrow,
     x,
     q,
+    own,
+    own_tip,
     diag,
-    lower,
     tip,
-    sem_factor1,
-    sem_factor0,
+    rows,
+    rows_tip,
+    sem_factor,
     sem_state,
     sem_share,
     sem_in,
     sem_out,
 ):
-    core, row, first = place()
+    core, _, first = place()
     second = jnp.where(core == 0, lax.axis_index("y"), lax.axis_index("x"))
-    loads1 = [
-        pltpu.make_async_copy(got.at[:, pl.ds(PANEL, MISC)], misc, sem_in.at[0]),
-        pltpu.make_async_copy(arrow_ref, arrow, sem_in.at[1]),
-    ] + load_exchanged(got, factor1, sem_factor1)
-    loads_state = [pltpu.make_async_copy(q_ref, q, sem_in.at[2])]
-    loads0 = [pltpu.make_async_copy(x_ref, x, sem_in.at[3])]
-    for k, late in enumerate((late0, late1, late2, late3)):
+    loads_state = [
+        pltpu.make_async_copy(own_ref, own, sem_in.at[0]),
+        pltpu.make_async_copy(own_tip_ref, own_tip, sem_in.at[1]),
+        pltpu.make_async_copy(q_ref, q, sem_in.at[2]),
+    ]
+    loads = load_exchanged(got, factor, sem_factor)
+    loads.append(pltpu.make_async_copy(x_ref.at[1], x, sem_in.at[3]))
+    for k, begun in enumerate((begun0, begun1, begun2, begun3)):
+        loads.append(
+            pltpu.make_async_copy(begun.at[pl.ds(PANEL, SHARE)], shares.at[k], sem_share.at[k])
+        )
         source = lax.rem(second + SIDE - k, SIDE)
         for j in range(SIDE):
             behind = lax.rem(first + SIDE - j, SIDE)
             loads_state.append(
                 pltpu.make_async_copy(
-                    late.at[pl.ds(LATER + j * PART, PART)],
+                    begun.at[pl.ds(j * PART, PART)],
                     state.at[natural(core, source, behind)],
                     sem_state.at[k * SIDE + j],
                 )
             )
-            loads0.append(
-                pltpu.make_async_copy(
-                    late.at[pl.ds(j * PART, PART)],
-                    factor0.at[natural(core, source, j)],
-                    sem_factor0.at[k * SIDE + j],
-                )
-            )
-        loads0.append(
-            pltpu.make_async_copy(late.at[pl.ds(PANEL, SHARE)], shares.at[k], sem_share.at[k])
-        )
-    for copy in loads1 + loads_state + loads0:
-        copy.start()
-    for copy in loads1:
-        copy.wait()
-    have = Gathered(factor1)
-    z1 = columns_t(factor1, 0, row)
-    z1_tip, z0_tip = arrow[1], arrow[0]
-    u, u_tip = have.past(z0_own(misc, second, core))
-    u_tip = u_tip - z0_tip.astype(F32)
-    uh, ul = split(u)
-    uh_tip, ul_tip = split(u_tip)
-    rows_in = jnp.concatenate([z1, uh, ul], axis=0)
-    tip_in = jnp.concatenate([z1_tip, uh_tip, ul_tip], axis=0)
+    for copy in loads_state + loads:
+        copy.start()
     for copy in loads_state:
         copy.wait()
     begun = Gathered(state)
-    top = begun.times_factor(rows_in, tip_in)
-    bottom = begun.over_rows(rows_in, 2) + dot(tip_in, q[...])
+    top = begun.times_factor(own[...], own_tip[...])
+    bottom = begun.over_rows(own[...], 2) + dot(own_tip[...], q[...])
     p1, a = top[:64], top[64:128] + top[128:]
     p1_tip, a_tip = bottom[:64], bottom[64:128] + bottom[128:]
     tip[1] = -p1_tip
     tip[0] = a_tip
-    stores = [pltpu.make_async_copy(tip, tip_ref, sem_out.at[0])]
-    stores[0].start()
     p1h, p1l = split(p1)
     ah, al = split(a)
     p1h_tip, p1l_tip = split(p1_tip)
     ah_tip, al_tip = split(a_tip)
-    own = [state[row, h * ROWS : (h + 1) * ROWS, :] for h in range(3)]
-    own_rows = jnp.concatenate(own[:2], axis=1)
-    out = have.times_factor(
-        jnp.concatenate([p1h, p1l, ah, al, own_rows], axis=0),
-        jnp.concatenate([p1h_tip, p1l_tip, ah_tip, al_tip, own[2]], axis=0),
+    rows_tip[...] = jnp.concatenate([-ah_tip, -al_tip, -p1h_tip], axis=0)
+    stores = [
+        pltpu.make_async_copy(tip, tip_ref, sem_out.at[0]),
+        pltpu.make_async_copy(rows_tip, rows_tip_ref, sem_out.at[1]),
+    ]
+    for copy in stores:
+        copy.start()
+    for copy in loads:
+        copy.wait()
+    out = Gathered(factor).times_factor(
+        jnp.concatenate([p1h, p1l, ah, al], axis=0),
+        jnp.concatenate([p1h_tip, p1l_tip, ah_tip, al_tip], axis=0),
     )
-    for copy in loads0:
-        copy.wait()
-    lower[1] = -out[256:]
-    sigma1 = x[1].astype(F32) + out[:64] + out[64:128]
-    diag[1] = sigma1
-    here = [
-        pltpu.make_async_copy(diag.at[1], diag_ref.at[1], sem_out.at[1]),
-        pltpu.make_async_copy(lower.at[1], lower_ref.at[1], sem_out.at[2]),
-    ]
-    for copy in here:
-        copy.start()
-    stores += here
+    sigma1 = x[...].astype(F32) + out[:64] + out[64:128]
+    diag[...] = sigma1
     carried = shares[0].astype(F32)
     for d in range(1, SIDE):
         carried += shares[d].astype(F32)
     carried = jnp.concatenate([carried[:ROWS], carried[ROWS:]], axis=1)
-    p0h, p0l = split(carried + out[128:192] + out[192:256])
-    out = Gathered(factor0).times_factor(
-        jnp.concatenate([p0h, p0l, sigma1.astype(BF)], axis=0),
-        jnp.concatenate([-ah_tip, -al_tip, -p1h_tip], axis=0),
-    )
+    p0h, p0l = split(carried + out[128:192] + out[192:])
+    rows[...] = jnp.concatenate([p0h, p0l, sigma1.astype(BF)], axis=0)
+    here = [
+        pltpu.make_async_copy(diag, diag_ref, sem_out.at[2]),
+        pltpu.make_async_copy(rows, rows_ref, sem_out.at[3]),
+    ]
+    for copy in here:
+        copy.start()
+    for copy in stores + here:
+        copy.wait()
+
+
+def last_kernel(
+    late0,
+    late1,
+    late2,
+    late3,
+    x_ref,
+    diag1_ref,
+    lower1_ref,
+    rows_ref,
+    rows_tip_ref,
+    diag_ref,
+    lower_ref,
+    factor,
+    x,
+    diag,
+    lower,
+    rows,
+    rows_tip,
+    sem_factor,
+    sem_in,
+    sem_out,
+):
+    core, _, first = place()
+    second = jnp.where(core == 0, lax.axis_index("y"), lax.axis_index("x"))
+    loads = [
+        pltpu.make_async_copy(diag1_ref, diag.at[1], sem_in.at[0]),
+        pltpu.make_async_copy(rows_ref, rows, sem_in.at[1]),
+        pltpu.make_async_copy(rows_tip_ref, rows_tip, sem_in.at[2]),
+        pltpu.make_async_copy(x_ref.at[0], x, sem_in.at[3]),
+    ]
+    load_lower = pltpu.make_async_copy(lower1_ref, lower.at[1], sem_in.at[4])
+    loads0 = []
+    for k, (late, at) in enumerate(((late0, 0), (late1, 0), (late2, LATER), (late3, 0))):
+        source = lax.rem(second + SIDE - k, SIDE)
+        loads0 += [
+            pltpu.make_async_copy(
+                late.at[pl.ds(at + j * PART, PART)],
+                factor.at[natural(core, source, j)],
+                sem_factor.at[k * SIDE + j],
+            )
+            for j in range(SIDE)
+        ]
+    for copy in loads + loads0 + [load_lower]:
+        copy.start()
+    for copy in loads:
+        copy.wait()
+    load_lower.wait()
+    stores = [
+        pltpu.make_async_copy(diag.at[1], diag_ref.at[1], sem_out.at[0]),
+        pltpu.make_async_copy(lower.at[1], lower_ref.at[1], sem_out.at[1]),
+    ]
+    for copy in stores:
+        copy.start()
+    for copy in loads0:
+        copy.wait()
+    out = Gathered(factor).times_factor(rows[...], rows_tip[...])
     lower[0] = -out[128:]
-    diag[0] = x[0].astype(F32) + out[:64] + out[64:128]
+    diag[0] = x[...].astype(F32) + out[:64] + out[64:128]
     here = [
-        pltpu.make_async_copy(diag.at[0], diag_ref.at[0], sem_out.at[3]),
-        pltpu.make_async_copy(lower.at[0], lower_ref.at[0], sem_out.at[4]),
+        pltpu.make_async_copy(diag.at[0], diag_ref.at[0], sem_out.at[2]),
+        pltpu.make_async_copy(lower.at[0], lower_ref.at[0], sem_out.at[3]),
     ]
     for copy in here:
         copy.start()
@@ -571,7 +679,7 @@
             pltpu.VMEM((ROWS, BLOCK + HALF), BF),
             pltpu.SemaphoreType.DMA((8,)),
             pltpu.SemaphoreType.DMA((2,)),
-            pltpu.SemaphoreType.DMA((SIDE + 1,)),
+            pltpu.SemaphoreType.DMA((2 * SIDE + 1,)),
         ],
         compiler_params=params,
         cost_estimate=cost(4),
@@ -584,7 +692,7 @@
         in_specs=[slow, slow, fast] + [slow] * SIDE,
         out_specs=slow,
         scratch_shapes=[
-            pltpu.VMEM((SIDE, 2 * PART, HALF), BF),
+            pltpu.VMEM((SIDE, 5 * ROWS, HALF), BF),
             pltpu.VMEM((MISC, HALF), BF),
             pltpu.SemaphoreType.DMA((SIDE + 1,)),
             pltpu.SemaphoreType.DMA((SIDE * (SIDE + 1),)),
@@ -592,26 +700,29 @@
         compiler_params=params,
         cost_estimate=cost(12),
     )(got, arrow_factor, slope_weights, *starts)
-    lates = pl.pallas_call(
+    short = jax.ShapeDtypeStruct((LATER, HALF), BF)
+    long = jax.ShapeDtypeStruct((LATER + PANEL, HALF), BF)
+    *begun, late = pl.pallas_call(
         later_kernel,
-        out_shape=(jax.ShapeDtypeStruct((LATER + PANEL, HALF), BF),) * SIDE,
+        out_shape=(short, short, long, short, jax.ShapeDtypeStruct((PANEL, HALF), BF)),
         in_specs=[slow] * 5,
-        out_specs=(slow,) * 4,
+        out_specs=(slow,) * 5,
         scratch_shapes=[
             pltpu.VMEM((SIDE, SENT - PART, HALF), BF),
             pltpu.VMEM((PANEL, HALF), BF),
             pltpu.VMEM((SIDE, SHARE, HALF), BF),
             pltpu.SemaphoreType.DMA((SIDE,)),
-            pltpu.SemaphoreType.DMA((SIDE * (SIDE + 1),)),
+            pltpu.SemaphoreType.DMA((3 * SIDE,)),
             pltpu.SemaphoreType.DMA((16,)),
         ],
         compiler_params=params,
         cost_estimate=cost(12),
     )(got, *starts)
-    lates = list(lates)
     early = exchange(sent, line_groups(partitions, 1))
-    for k in range(1, SIDE):
-        lates[k] = lax.ppermute(lates[k], EVERY, line_shift(partitions, k))
+    shifts = [line_shift(partitions, k) for k in range(SIDE)]
+    begun[1:] = [lax.ppermute(begun[k], EVERY, shifts[k]) for k in range(1, SIDE)]
+    lates = [lax.ppermute(late, EVERY, shifts[k]) for k in (1, 3)]
+    lates = [late, lates[0], begun[2], lates[1]]
     slope = pl.pallas_call(
         trace_kernel,
         out_shape=jax.ShapeDtypeStruct((partitions // 2, 8, 128), F32),
@@ -630,42 +741,96 @@
         ],
         compiler_params=params,
         cost_estimate=cost(20),
-    )(early, lates[0], got, arrow_factor, block_inverse, tip_inverse, slope_weights[:, :, None])
-    total = jnp.sum(exchange(slope, height_groups(partitions)), axis=0)
-    total = jnp.broadcast_to(total[None], (2 * SIDE * SIDE, 8, 128))
+    )(early, begun[0], got, arrow_factor, block_inverse, tip_inverse, slope_weights[:, :, None])
+    total = exchange(slope, height_groups(partitions))
+    outputs = (
+        jax.ShapeDtypeStruct((ROWS, BLOCK), F32),
+        jax.ShapeDtypeStruct((3 * ROWS, BLOCK), BF),
+        jax.ShapeDtypeStruct((3 * ROWS, HALF), BF),
+    )
+    lower1, own, own_tip = pl.pallas_call(
+        own_kernel,
+        out_shape=outputs,
+        in_specs=[slow] * 3,
+        out_specs=(slow,) * 3,
+        scratch_shapes=[
+            pltpu.VMEM((16, PART, HALF), BF),
+            pltpu.VMEM((SIDE, MISC, HALF), BF),
+            pltpu.VMEM((PART, HALF), BF),
+            pltpu.VMEM((2, ROWS, HALF), BF),
+        ]
+        + [pltpu.VMEM(leaf.shape, leaf.dtype) for leaf in outputs]
+        + [
+            pltpu.SemaphoreType.DMA((16,)),
+            pltpu.SemaphoreType.DMA((3,)),
+            pltpu.SemaphoreType.DMA((3,)),
+        ],
+        compiler_params=params,
+        cost_estimate=cost(15),
+    )(early, begun[0], arrow_factor)
+    outputs = (
+        jax.ShapeDtypeStruct((ROWS, BLOCK), F32),
+        jax.ShapeDtypeStruct((2, ROWS, HALF), F32),
+        jax.ShapeDtypeStruct((3 * ROWS, BLOCK), BF),
+        jax.ShapeDtypeStruct((3 * ROWS, HALF), BF),
+    )
+    diag1, tip, rows, rows_tip = pl.pallas_call(
+        first_kernel,
+        out_shape=outputs,
+        in_specs=[slow] * 9,
+        out_specs=(slow,) * 4,
+        scratch_shapes=[
+            pltpu.VMEM((16, PART, HALF), BF),
+            pltpu.VMEM((16, PART, HALF), BF),
+            pltpu.VMEM((SIDE, SHARE, HALF), BF),
+            pltpu.VMEM((ROWS, BLOCK), BF),
+            pltpu.VMEM((HALF, HALF), BF),
+            pltpu.VMEM((3 * ROWS, BLOCK), BF),
+            pltpu.VMEM((3 * ROWS, HALF), BF),
+        ]
+        + [pltpu.VMEM(leaf.shape, leaf.dtype) for leaf in outputs]
+        + [
+            pltpu.SemaphoreType.DMA((16,)),
+            pltpu.SemaphoreType.DMA((16,)),
+            pltpu.SemaphoreType.DMA((SIDE,)),
+            pltpu.SemaphoreType.DMA((4,)),
+            pltpu.SemaphoreType.DMA((4,)),
+        ],
+        compiler_params=params,
+        cost_estimate=cost(25),
+    )(early, *begun, block_inverse, tip_inverse, own, own_tip)
+    total = pl.pallas_call(
+        sum_kernel,
+        out_shape=jax.ShapeDtypeStruct((2 * SIDE * SIDE, 8, 128), F32),
+        in_specs=[fast, slow],
+        out_specs=fast,
+        compiler_params=params,
+        cost_estimate=cost(1),
+    )(total, rows_tip)
     total = jnp.sum(exchange(total, plane_groups(partitions)), axis=0)
     outputs = (
         jax.ShapeDtypeStruct((2, ROWS, BLOCK), F32),
         jax.ShapeDtypeStruct((2, ROWS, BLOCK), F32),
-        jax.ShapeDtypeStruct((2, ROWS, HALF), F32),
     )
-    diag, lower, tip = pl.pallas_call(
-        block_kernel,
+    diag, lower = pl.pallas_call(
+        last_kernel,
         out_shape=outputs,
-        in_specs=[slow] * 8,
-        out_specs=(slow,) * 3,
+        in_specs=[slow] * 9,
+        out_specs=(slow,) * 2,
         scratch_shapes=[
             pltpu.VMEM((16, PART, HALF), BF),
-            pltpu.VMEM((16, PART, HALF), BF),
-            pltpu.VMEM((16, PART, HALF), BF),
-            pltpu.VMEM((SIDE, SHARE, HALF), BF),
-            pltpu.VMEM((SIDE, MISC, HALF), BF),
-            pltpu.VMEM((2, ROWS, HALF), BF),
-            pltpu.VMEM((2, ROWS, BLOCK), BF),
-            pltpu.VMEM((HALF, HALF), BF),
-        ]
-        + [pltpu.VMEM(leaf.shape, F32) for leaf in outputs]
-        + [
+            pltpu.VMEM((ROWS, BLOCK), BF),
+            pltpu.VMEM((2, ROWS, BLOCK), F32),
+            pltpu.VMEM((2, ROWS, BLOCK), F32),
+            pltpu.VMEM((3 * ROWS, BLOCK), BF),
+            pltpu.VMEM((3 * ROWS, HALF), BF),
             pltpu.SemaphoreType.DMA((16,)),
-            pltpu.SemaphoreType.DMA((16,)),
-            pltpu.SemaphoreType.DMA((16,)),
-            pltpu.SemaphoreType.DMA((SIDE,)),
+            pltpu.SemaphoreType.DMA((5,)),
             pltpu.SemaphoreType.DMA((4,)),
-            pltpu.SemaphoreType.DMA((5,)),
         ],
         compiler_params=params,
-        cost_estimate=cost(30),
-    )(early, *lates, arrow_factor, block_inverse, tip_inverse)
+        cost_estimate=cost(15),
+    )(*lates, block_inverse, diag1, lower1, rows, rows_tip)
     return diag, lower, tip, total[0, 0]
 
 

time: 117 us -> 133 us (1.14)
  starting transfers between devices: 45.3 us -> 80.3 us
  blocking collectives: 24 us -> 0 us
  Pallas kernels: 28.4 us -> 34.9 us
  waiting for transfers between devices: 15.7 us -> 13.6 us
    all_to_all x3 -> x4, starting transfers between devices: 17.8 us -> 46.9 us  [exchange(): lax.all_to_all(value, EVERY, 0, 0, tiled=True, axis_index_groups=groups)]
    all_to_all x1 -> x0, blocking collectives: 24 us -> none  [exchange(): lax.all_to_all(value, EVERY, 0, 0, tiled=True, axis_index_groups=groups)]
    pallas_call x2 -> x5, Pallas kernels: 14.6 us -> 21.6 us  [the longest x1 6.72 us: on_device(): pl.pallas_call(first_kernel, out_shape=outputs, in_specs=[slow] * 9, out_...]
    ppermute x3 -> x5, starting transfers between devices: 10.7 us -> 16.6 us  [the longest x3 11.3 us: on_device(): lax.ppermute(begun[k], EVERY, shifts[k])]
    all_to_all x3 -> x4, waiting for transfers between devices: 9.66 us -> 7.6 us  [exchange(): lax.all_to_all(value, EVERY, 0, 0, tiled=True, axis_index_groups=groups)]
  transfers between devices with their start and end apart: 10 -> 13, of which waited for: 3 -> 4; matrix products, arithmetic and copies ran while one was open for 1% -> 1% of each run, Pallas kernels for 19% -> 22%
where the time goes in v6:
time: 133 us; the launch traced here: 132 us
  starting transfers between devices  80.3 us (60%)
  Pallas kernels  34.9 us (26%)
  waiting for transfers between devices  13.6 us (10%)
  local copies, waits for them, and re-layouts  1.9 us (1%)
    all_to_all x4, starting transfers between devices, exchange(): lax.all_to_all(value, EVERY, 0, 0, tiled=True, axis_index_groups=groups)  46.9 us
    ppermute x4, starting transfers between devices, on_device(): lax.ppermute(start, EVERY, state_shift(partitions, k))  16.8 us
    ppermute x3, starting transfers between devices, on_device(): lax.ppermute(begun[k], EVERY, shifts[k])  11.3 us
    all_to_all x4, waiting for transfers between devices, exchange(): lax.all_to_all(value, EVERY, 0, 0, tiled=True, axis_index_groups=groups)  7.6 us
    pallas_call x1, Pallas kernels, on_device(): pl.pallas_call(trace_kernel, out_shape=jax.ShapeDtypeStruct((partitions /...  7.1 us
    pallas_call x1, Pallas kernels, on_device(): pl.pallas_call(first_kernel, out_shape=outputs, in_specs=[slow] * 9, out_...  6.72 us
    ppermute x4, waiting for transfers between devices, on_device(): lax.ppermute(start, EVERY, state_shift(partitions, k))  6.04 us
    ppermute x2, starting transfers between devices, on_device(): lates = [lax.ppermute(late, EVERY, shifts[k]) for k in (1, 3)]  5.28 us
  transfers between devices with their start and end apart: 13, of which 4 were waited for; matrix products, arithmetic and copies ran while one was open for 1% of the time, Pallas kernels for 22%

profile of v6, /device:TPU:1, one launch (start us, length us, event | category | flops | bytes accessed | tf_op | source)
XLA Modules:
  0.0 131.7 jit_solution(15056160243292903466)
XLA Ops:
  0.6 2.5 %shard_map.102 = (bf16[4,512,512]{2,1,0:T(8,128)(2,1)}, bf16[64,1536]{1,0:T(8,128)(2,1)}) custom-call(bf16[2,64,1024]{2,1,0:T(8,128)(2,1)} %low.1, bf16[2,64,512]{2,1,0:T(8,128)(2,1)} %arrow_ref.3, bf16[2,64,1024]{2,1,0:T(8,128)(2,1)} %x_ref.5, bf16[1,64,1024]{2,1,0:T(8,128)(2,1)} %sigma.1, bf16[1,64,512]{2,1,0:T(8,128)(2,1)} %tip.1), custom_call_target="tpu_custom_call" | custom-call | bytes 4000000 | tf_op jit(solution)/shard_map/pallas_call | solution.py:669
  3.1 5.2 %all-to-all-start = ((bf16[4,512,512]{2,1,0:T(8,128)(2,1)}), bf16[4,512,512]{2,1,0:T(8,128)(2,1)}, u32[]{:S(2)}, u32[]{:S(2)}) async-start(bf16[4,512,512]{2,1,0:T(8,128)(2,1)} %get-tuple-element.20), calls=%async_computation | async-start | bytes 4194304 | tf_op jit(solution)/shard_map/all_to_all | solution.py:80
  8.3 11.1 %collective-permute-start.3 = (bf16[64,1536]{1,0:T(8,128)(2,1)S(1)}, bf16[64,1536]{1,0:T(8,128)(2,1)S(1)}, u32[]{:S(2)}, u32[]{:S(2)}) collective-permute-start(bf16[64,1536]{1,0:T(8,128)(2,1)S(1)} %copy-done.4), channel_id=1, source_target_pairs={{16,3},{17,0},{18,1},{19,2},{20,7},{21,4},{22,5},{23,6},{24,11},{2... | collective-permute-start | bytes 589832 | tf_op jit(solution)/shard_map/ppermute | solution.py:688
  19.3 1.9 %collective-permute-start.2 = (bf16[64,1536]{1,0:T(8,128)(2,1)S(1)}, bf16[64,1536]{1,0:T(8,128)(2,1)S(1)}, u32[]{:S(2)}, u32[]{:S(2)}) collective-permute-start(bf16[64,1536]{1,0:T(8,128)(2,1)S(1)} %copy-done.4), channel_id=1, source_target_pairs={{16,2},{17,3},{18,0},{19,1},{20,6},{21,7},{22,4},{23,5},{24,10},{2... | collective-permute-start | bytes 589832 | tf_op jit(solution)/shard_map/ppermute | solution.py:688
  21.3 1.9 %collective-permute-start.1 = (bf16[64,1536]{1,0:T(8,128)(2,1)S(1)}, bf16[64,1536]{1,0:T(8,128)(2,1)}, u32[]{:S(2)}, u32[]{:S(2)}) collective-permute-start(bf16[64,1536]{1,0:T(8,128)(2,1)S(1)} %copy-done.4), channel_id=1, source_target_pairs={{16,1},{17,2},{18,3},{19,0},{20,5},{21,6},{22,7},{23,4},{24,9},{25... | collective-permute-start | bytes 589832 | tf_op jit(solution)/shard_map/ppermute | solution.py:688
  23.2 1.9 %collective-permute-start = (bf16[64,1536]{1,0:T(8,128)(2,1)S(1)}, bf16[64,1536]{1,0:T(8,128)(2,1)}, u32[]{:S(2)}, u32[]{:S(2)}) collective-permute-start(bf16[64,1536]{1,0:T(8,128)(2,1)S(1)} %copy-done.4), channel_id=1, source_target_pairs={{16,0},{17,1},{18,2},{19,3},{20,4},{21,5},{22,6},{23,7},{24,8},{25... | collective-permute-start | bytes 589832 | tf_op jit(solution)/shard_map/ppermute | solution.py:688
  25.2 4.0 %collective-permute-done.2.own2 = bf16[64,1536]{1,0:T(8,128)(2,1)S(1)} collective-permute-done((bf16[64,1536]{1,0:T(8,128)(2,1)S(1)}, bf16[64,1536]{1,0:T(8,128)(2,1)S(1)}, u32[]{:S(2)}, u32[]{:S(2)}) %collective-permute-start.2) | collective-permute-done | bytes 196640 | tf_op jit(solution)/shard_map/ppermute | solution.py:688
  29.2 2.0 %collective-permute-done.1.own1 = bf16[64,1536]{1,0:T(8,128)(2,1)} collective-permute-done((bf16[64,1536]{1,0:T(8,128)(2,1)S(1)}, bf16[64,1536]{1,0:T(8,128)(2,1)}, u32[]{:S(2)}, u32[]{:S(2)}) %collective-permute-start.1) | collective-permute-done | bytes 196640 | tf_op jit(solution)/shard_map/ppermute | solution.py:688
  31.2 3.8 %shard_map.104 = bf16[4,976,512]{2,1,0:T(8,128)(2,1)} custom-call(bf16[4,512,512]{2,1,0:T(8,128)(2,1)} %all-to-all-done.got.panel_ref, bf16[2,64,512]{2,1,0:T(8,128)(2,1)} %arrow_ref.3, f32[2,64]{1,0:T(2,128)} %weight.1, bf16[64,1536]{1,0:T(8,128)(2,1)} %collective-permute-done.own0, bf16[64,1536]{1,0:T(8,128)(2,1)} %collective-permute-done.1.own1, ...), custom_call_target="tpu_custom_call" | custom-call | bytes 12000000 | tf_op jit(solution)/shard_map/pallas_call | solution.py:689
  35.0 4.8 %all-to-all-start.1 = ((bf16[4,976,512]{2,1,0:T(8,128)(2,1)}), bf16[4,976,512]{2,1,0:T(8,128)(2,1)}, u32[]{:S(2)}, u32[]{:S(2)}) async-start(bf16[4,976,512]{2,1,0:T(8,128)(2,1)} %shard_map.104), calls=%async_computation.1 | async-start | bytes 7995392 | tf_op jit(solution)/shard_map/all_to_all | solution.py:80
  39.9 4.2 %shard_map.103 = (bf16[896,512]{1,0:T(8,128)(2,1)}, bf16[896,512]{1,0:T(8,128)(2,1)}, bf16[1664,512]{1,0:T(8,128)(2,1)}, bf16[896,512]{1,0:T(8,128)(2,1)}, bf16[768,512]{1,0:T(8,128)(2,1)}) custom-call(bf16[4,512,512]{2,1,0:T(8,128)(2,1)} %all-to-all-done.got.panel_ref, bf16[64,1536]{1,0:T(8,128)(2,1)} %collective-permute-done.own0, ...), custom_call_target="tpu_custom_call" | custom-call | bytes 12000000 | tf_op jit(solution)/shard_map/pallas_call | solution.py:705
  44.1 4.8 %collective-permute-start.5 = (bf16[1664,512]{1,0:T(8,128)(2,1)}, bf16[1664,512]{1,0:T(8,128)(2,1)}, u32[]{:S(2)}, u32[]{:S(2)}) collective-permute-start(bf16[1664,512]{1,0:T(8,128)(2,1)} %get-tuple-element.23), channel_id=1, source_target_pairs={{0,8},{1,9},{2,10},{3,11},{4,12},{5,13},{6,14},{7,15},{8,0},{9,1},... | collective-permute-start | bytes 5111816 | tf_op jit(solution)/shard_map/ppermute | solution.py:723
  48.9 2.2 %collective-permute-start.7 = (bf16[896,512]{1,0:T(8,128)(2,1)}, bf16[896,512]{1,0:T(8,128)(2,1)}, u32[]{:S(2)}, u32[]{:S(2)}) collective-permute-start(bf16[896,512]{1,0:T(8,128)(2,1)} %get-tuple-element.25), channel_id=1, source_target_pairs={{0,4},{1,5},{2,6},{3,7},{4,8},{5,9},{6,10},{7,11},{8,12},{9,13},{1... | collective-permute-start | bytes 2752520 | tf_op jit(solution)/shard_map/ppermute | solution.py:723
  51.1 4.3 %collective-permute-start.8 = (bf16[896,512]{1,0:T(8,128)(2,1)}, bf16[896,512]{1,0:T(8,128)(2,1)}, u32[]{:S(2)}, u32[]{:S(2)}) collective-permute-start(bf16[896,512]{1,0:T(8,128)(2,1)} %get-tuple-element.26), channel_id=1, source_target_pairs={{0,12},{1,13},{2,14},{3,15},{4,0},{5,1},{6,2},{7,3},{8,4},{9,5},{1... | collective-permute-start | bytes 2752520 | tf_op jit(solution)/shard_map/ppermute | solution.py:723
  55.4 1.9 %collective-permute-start.6 = (bf16[768,512]{1,0:T(8,128)(2,1)}, bf16[768,512]{1,0:T(8,128)(2,1)}, u32[]{:S(2)}, u32[]{:S(2)}) collective-permute-start(bf16[768,512]{1,0:T(8,128)(2,1)} %get-tuple-element.22.late0), channel_id=1, source_target_pairs={{0,12},{1,13},{2,14},{3,15},{4,0},{5,1},{6,2},{7,3},{8,4},{9,5},{1... | collective-permute-start | bytes 2359304 | tf_op jit(solution)/shard_map/ppermute | solution.py:724
  57.4 3.4 %collective-permute-start.4 = (bf16[768,512]{1,0:T(8,128)(2,1)}, bf16[768,512]{1,0:T(8,128)(2,1)}, u32[]{:S(2)}, u32[]{:S(2)}) collective-permute-start(bf16[768,512]{1,0:T(8,128)(2,1)} %get-tuple-element.22.late0), channel_id=1, source_target_pairs={{0,4},{1,5},{2,6},{3,7},{4,8},{5,9},{6,10},{7,11},{8,12},{9,13},{1... | collective-permute-start | bytes 2359304 | tf_op jit(solution)/shard_map/ppermute | solution.py:724
  61.5 4.3 %all-to-all-done.1.got = bf16[4,976,512]{2,1,0:T(8,128)(2,1)} async-done(((bf16[4,976,512]{2,1,0:T(8,128)(2,1)}), bf16[4,976,512]{2,1,0:T(8,128)(2,1)}, u32[]{:S(2)}, u32[]{:S(2)}) %all-to-all-start.1) | async-done | bytes 3997728 | tf_op jit(solution)/shard_map/all_to_all | solution.py:80
  65.8 7.1 %shard_map.108 = f32[16,8,128]{2,1,0:T(8,128)} custom-call(bf16[4,976,512]{2,1,0:T(8,128)(2,1)} %all-to-all-done.1.got, bf16[896,512]{1,0:T(8,128)(2,1)} %get-tuple-element.24.begun.begun0, bf16[4,512,512]{2,1,0:T(8,128)(2,1)} %all-to-all-done.got.panel_ref, bf16[2,64,512]{2,1,0:T(8,128)(2,1)} %arrow_ref.3, bf16[2,64,1024]{2,1,0:T(8,128)(2,1)} %x_ref.5, ...), custom_call_target="tpu_custom_call" | custom-call | bytes 20000000 | tf_op jit(solution)/shard_map/pallas_call | solution.py:726
  72.9 28.4 %all-to-all-start.2 = ((f32[16,8,128]{2,1,0:T(8,128)}), f32[16,8,128]{2,1,0:T(8,128)S(1)}, u32[]{:S(2)}, u32[]{:S(2)}) async-start(f32[16,8,128]{2,1,0:T(8,128)} %shard_map.108), calls=%async_computation.2 | async-start | bytes 131072 | tf_op jit(solution)/shard_map/all_to_all | solution.py:80
  101.3 4.9 %shard_map.105 = (f32[64,1024]{1,0:T(8,128)}, bf16[192,1024]{1,0:T(8,128)(2,1)}, bf16[192,512]{1,0:T(8,128)(2,1)}) custom-call(bf16[4,976,512]{2,1,0:T(8,128)(2,1)} %all-to-all-done.1.got, bf16[896,512]{1,0:T(8,128)(2,1)} %get-tuple-element.24.begun.begun0, bf16[2,64,512]{2,1,0:T(8,128)(2,1)} %arrow_ref.3), custom_call_target="tpu_custom_call" | custom-call | bytes 15000000 | tf_op jit(solution)/shard_map/pallas_call | solution.py:751
  106.3 6.7 %shard_map.106 = (f32[64,1024]{1,0:T(8,128)}, f32[2,64,512]{2,1,0:T(8,128)}, bf16[192,1024]{1,0:T(8,128)(2,1)}, bf16[192,512]{1,0:T(8,128)(2,1)}) custom-call(bf16[4,976,512]{2,1,0:T(8,128)(2,1)} %all-to-all-done.1.got, bf16[896,512]{1,0:T(8,128)(2,1)} %get-tuple-element.24.begun.begun0, bf16[896,512]{1,0:T(8,128)(2,1)} %collective-permute-done.7.begun1, ...), custom_call_target="tpu_custom_call" | custom-call | bytes 25000000 | tf_op jit(solution)/shard_map/pallas_call | solution.py:777
  115.2 8.4 %all-to-all-start.3 = ((f32[32,8,128]{2,1,0:T(8,128)}), f32[32,8,128]{2,1,0:T(8,128)S(1)}, u32[]{:S(2)}, u32[]{:S(2)}) async-start(f32[32,8,128]{2,1,0:T(8,128)} %shard_map.109), calls=%async_computation.3 | async-start | bytes 262144 | tf_op jit(solution)/shard_map/all_to_all | solution.py:80
  123.6 4.2 %shard_map.107 = (f32[2,64,1024]{2,1,0:T(8,128)}, f32[2,64,1024]{2,1,0:T(8,128)}) custom-call(bf16[768,512]{1,0:T(8,128)(2,1)} %get-tuple-element.22.late0, bf16[768,512]{1,0:T(8,128)(2,1)} %collective-permute-done.4.late1, bf16[1664,512]{1,0:T(8,128)(2,1)} %collective-permute-done.5.begun2.late2, bf16[768,512]{1,0:T(8,128)(2,1)} %collective-permute-done.6.late3, ...), custom_call_target="tpu_custom_call" | custom-call | bytes 15000000 | tf_op jit(solution)/shard_map/pallas_call | solution.py:815
  127.9 3.3 %all-to-all-done.3 = f32[32,8,128]{2,1,0:T(8,128)S(1)} async-done(((f32[32,8,128]{2,1,0:T(8,128)}), f32[32,8,128]{2,1,0:T(8,128)S(1)}, u32[]{:S(2)}, u32[]{:S(2)}) %all-to-all-start.3) | async-done | bytes 131104 | tf_op jit(solution)/shard_map/all_to_all | solution.py:80
  (23 shorter events, 3.5 us)
Async XLA Ops:
  3.1 5.2 %copy-start.4 = (bf16[64,1536]{1,0:T(8,128)(2,1)S(1)}, bf16[64,1536]{1,0:T(8,128)(2,1)}, u32[]{:S(2)}) copy-start(bf16[64,1536]{1,0:T(8,128)(2,1)} %get-tuple-element.21) | copy-start | bytes 589828
  3.1 28.1 %all-to-all-start = ((bf16[4,512,512]{2,1,0:T(8,128)(2,1)}), bf16[4,512,512]{2,1,0:T(8,128)(2,1)}, u32[]{:S(2)}, u32[]{:S(2)}) async-start(bf16[4,512,512]{2,1,0:T(8,128)(2,1)} %get-tuple-element.20), calls=%async_computation | async-start | bytes 4194304 | tf_op jit(solution)/shard_map/all_to_all | solution.py:80
  8.3 16.9 %collective-permute-start.3 = (bf16[64,1536]{1,0:T(8,128)(2,1)S(1)}, bf16[64,1536]{1,0:T(8,128)(2,1)S(1)}, u32[]{:S(2)}, u32[]{:S(2)}) collective-permute-start(bf16[64,1536]{1,0:T(8,128)(2,1)S(1)} %copy-done.4), channel_id=1, source_target_pairs={{16,3},{17,0},{18,1},{19,2},{20,7},{21,4},{22,5},{23,6},{24,11},{2... | collective-permute-start | bytes 589832 | tf_op jit(solution)/shard_map/ppermute | solution.py:688
  19.3 9.9 %collective-permute-start.2 = (bf16[64,1536]{1,0:T(8,128)(2,1)S(1)}, bf16[64,1536]{1,0:T(8,128)(2,1)S(1)}, u32[]{:S(2)}, u32[]{:S(2)}) collective-permute-start(bf16[64,1536]{1,0:T(8,128)(2,1)S(1)} %copy-done.4), channel_id=1, source_target_pairs={{16,2},{17,3},{18,0},{19,1},{20,6},{21,7},{22,4},{23,5},{24,10},{2... | collective-permute-start | bytes 589832 | tf_op jit(solution)/shard_map/ppermute | solution.py:688
  21.3 9.9 %collective-permute-start.1 = (bf16[64,1536]{1,0:T(8,128)(2,1)S(1)}, bf16[64,1536]{1,0:T(8,128)(2,1)}, u32[]{:S(2)}, u32[]{:S(2)}) collective-permute-start(bf16[64,1536]{1,0:T(8,128)(2,1)S(1)} %copy-done.4), channel_id=1, source_target_pairs={{16,1},{17,2},{18,3},{19,0},{20,5},{21,6},{22,7},{23,4},{24,9},{25... | collective-permute-start | bytes 589832 | tf_op jit(solution)/shard_map/ppermute | solution.py:688
  23.2 8.0 %collective-permute-start = (bf16[64,1536]{1,0:T(8,128)(2,1)S(1)}, bf16[64,1536]{1,0:T(8,128)(2,1)}, u32[]{:S(2)}, u32[]{:S(2)}) collective-permute-start(bf16[64,1536]{1,0:T(8,128)(2,1)S(1)} %copy-done.4), channel_id=1, source_target_pairs={{16,0},{17,1},{18,2},{19,3},{20,4},{21,5},{22,6},{23,7},{24,8},{25... | collective-permute-start | bytes 589832 | tf_op jit(solution)/shard_map/ppermute | solution.py:688
  25.1 6.1 %copy-start = (bf16[64,1536]{1,0:T(8,128)(2,1)}, bf16[64,1536]{1,0:T(8,128)(2,1)S(1)}, u32[]{:S(2)}) copy-start(bf16[64,1536]{1,0:T(8,128)(2,1)S(1)} %collective-permute-done.3.own3) | copy-start | bytes 589828
  29.2 2.0 %copy-start.1 = (bf16[64,1536]{1,0:T(8,128)(2,1)}, bf16[64,1536]{1,0:T(8,128)(2,1)S(1)}, u32[]{:S(2)}) copy-start(bf16[64,1536]{1,0:T(8,128)(2,1)S(1)} %collective-permute-done.2.own2) | copy-start | bytes 589828
  35.0 30.8 %all-to-all-start.1 = ((bf16[4,976,512]{2,1,0:T(8,128)(2,1)}), bf16[4,976,512]{2,1,0:T(8,128)(2,1)}, u32[]{:S(2)}, u32[]{:S(2)}) async-start(bf16[4,976,512]{2,1,0:T(8,128)(2,1)} %shard_map.104), calls=%async_computation.1 | async-start | bytes 7995392 | tf_op jit(solution)/shard_map/all_to_all | solution.py:80
  39.9 20.9 %copy-start.3 = (f32[2,64]{1,0:T(2,128)S(1)}, f32[2,64]{1,0:T(2,128)}, u32[]{:S(2)}) copy-start(f32[2,64]{1,0:T(2,128)} %weight.1) | copy-start | bytes 1540
  44.1 62.2 %collective-permute-start.5 = (bf16[1664,512]{1,0:T(8,128)(2,1)}, bf16[1664,512]{1,0:T(8,128)(2,1)}, u32[]{:S(2)}, u32[]{:S(2)}) collective-permute-start(bf16[1664,512]{1,0:T(8,128)(2,1)} %get-tuple-element.23), channel_id=1, source_target_pairs={{0,8},{1,9},{2,10},{3,11},{4,12},{5,13},{6,14},{7,15},{8,0},{9,1},... | collective-permute-start | bytes 5111816 | tf_op jit(solution)/shard_map/ppermute | solution.py:723
  48.9 57.3 %collective-permute-start.7 = (bf16[896,512]{1,0:T(8,128)(2,1)}, bf16[896,512]{1,0:T(8,128)(2,1)}, u32[]{:S(2)}, u32[]{:S(2)}) collective-permute-start(bf16[896,512]{1,0:T(8,128)(2,1)} %get-tuple-element.25), channel_id=1, source_target_pairs={{0,4},{1,5},{2,6},{3,7},{4,8},{5,9},{6,10},{7,11},{8,12},{9,13},{1... | collective-permute-start | bytes 2752520 | tf_op jit(solution)/shard_map/ppermute | solution.py:723
  51.1 55.1 %collective-permute-start.8 = (bf16[896,512]{1,0:T(8,128)(2,1)}, bf16[896,512]{1,0:T(8,128)(2,1)}, u32[]{:S(2)}, u32[]{:S(2)}) collective-permute-start(bf16[896,512]{1,0:T(8,128)(2,1)} %get-tuple-element.26), channel_id=1, source_target_pairs={{0,12},{1,13},{2,14},{3,15},{4,0},{5,1},{6,2},{7,3},{8,4},{9,5},{1... | collective-permute-start | bytes 2752520 | tf_op jit(solution)/shard_map/ppermute | solution.py:723
  55.4 68.2 %collective-permute-start.6 = (bf16[768,512]{1,0:T(8,128)(2,1)}, bf16[768,512]{1,0:T(8,128)(2,1)}, u32[]{:S(2)}, u32[]{:S(2)}) collective-permute-start(bf16[768,512]{1,0:T(8,128)(2,1)} %get-tuple-element.22.late0), channel_id=1, source_target_pairs={{0,12},{1,13},{2,14},{3,15},{4,0},{5,1},{6,2},{7,3},{8,4},{9,5},{1... | collective-permute-start | bytes 2359304 | tf_op jit(solution)/shard_map/ppermute | solution.py:724
  57.4 66.3 %collective-permute-start.4 = (bf16[768,512]{1,0:T(8,128)(2,1)}, bf16[768,512]{1,0:T(8,128)(2,1)}, u32[]{:S(2)}, u32[]{:S(2)}) collective-permute-start(bf16[768,512]{1,0:T(8,128)(2,1)} %get-tuple-element.22.late0), channel_id=1, source_target_pairs={{0,4},{1,5},{2,6},{3,7},{4,8},{5,9},{6,10},{7,11},{8,12},{9,13},{1... | collective-permute-start | bytes 2359304 | tf_op jit(solution)/shard_map/ppermute | solution.py:724
  72.9 40.1 %all-to-all-start.2 = ((f32[16,8,128]{2,1,0:T(8,128)}), f32[16,8,128]{2,1,0:T(8,128)S(1)}, u32[]{:S(2)}, u32[]{:S(2)}) async-start(f32[16,8,128]{2,1,0:T(8,128)} %shard_map.108), calls=%async_computation.2 | async-start | bytes 131072 | tf_op jit(solution)/shard_map/all_to_all | solution.py:80
  113.0 0.6 copy-start.2
  115.2 16.0 %all-to-all-start.3 = ((f32[32,8,128]{2,1,0:T(8,128)}), f32[32,8,128]{2,1,0:T(8,128)S(1)}, u32[]{:S(2)}, u32[]{:S(2)}) async-start(f32[32,8,128]{2,1,0:T(8,128)} %shard_map.109), calls=%async_computation.3 | async-start | bytes 262144 | tf_op jit(solution)/shard_map/all_to_all | solution.py:80

commit v7 on v5

--- a/solution.py
+++ b/solution.py
@@ -138,12 +138,22 @@
     ]
     for copy in loads + loads_own:
         copy.start()
-    for copy in loads + loads_own:
-        copy.wait()
-    stores = [pltpu.make_async_copy(held, out.at[d], sem_out.at[d]) for d in range(SIDE)]
-    stores.append(pltpu.make_async_copy(own, start, sem_out.at[SIDE]))
-    for copy in stores:
-        copy.start()
+    stores = []
+    for h in range(2):
+        for copy in loads[4 * h : 4 * h + 4]:
+            copy.wait()
+        rows = pl.ds(h * SENT // 2, SENT // 2)
+        here = [
+            pltpu.make_async_copy(held.at[rows], out.at[d, rows], sem_out.at[d * 2 + h])
+            for d in range(SIDE)
+        ]
+        for copy in here:
+            copy.start()
+        stores += here
+    for copy in loads_own:
+        copy.wait()
+    stores.append(pltpu.make_async_copy(own, start, sem_out.at[2 * SIDE]))
+    stores[-1].start()
     for copy in stores:
         copy.wait()
 
@@ -154,7 +164,7 @@
     del own0, own1, own2, own3
     core, _, first = place()
     loads = [
-        pltpu.make_async_copy(got.at[j, pl.ds(0, 2 * PART)], panel.at[j], sem_in.at[j])
+        pltpu.make_async_copy(got.at[j, pl.ds(0, 5 * ROWS)], panel.at[j], sem_in.at[j])
         for j in range(SIDE)
     ]
     load_arrow = pltpu.make_async_copy(
@@ -399,8 +409,9 @@
         own_parts = jnp.where(second == d, parts[d], own_parts)
     traced = (u_mine * through[:256] + own_parts.astype(F32) * carried) * weights[0]
     traced += z1_mine.astype(F32) * through[256:] * weights[1]
-    own_tip = dot(z0_own(misc, second, core), Gathered(factor).piece(2))
-    own_tip = own_tip - arrow[0].astype(F32)
+    own_tip = u_tip[:ROWS]
+    for d in range(1, SIDE):
+        own_tip = jnp.where(second == d, u_tip[d * ROWS : (d + 1) * ROWS], own_tip)
     both = jnp.concatenate([own_tip.astype(BF), arrow[1]], axis=0)
     tip_traced = both.astype(F32) * dot(both, q[...])
     at = lax.broadcasted_iota(jnp.int32, (ROWS, BLOCK), 0) + row * ROWS
@@ -571,7 +582,7 @@
             pltpu.VMEM((ROWS, BLOCK + HALF), BF),
             pltpu.SemaphoreType.DMA((8,)),
             pltpu.SemaphoreType.DMA((2,)),
-            pltpu.SemaphoreType.DMA((SIDE + 1,)),
+            pltpu.SemaphoreType.DMA((2 * SIDE + 1,)),
         ],
         compiler_params=params,
         cost_estimate=cost(4),
@@ -584,7 +595,7 @@
         in_specs=[slow, slow, fast] + [slow] * SIDE,
         out_specs=slow,
         scratch_shapes=[
-            pltpu.VMEM((SIDE, 2 * PART, HALF), BF),
+            pltpu.VMEM((SIDE, 5 * ROWS, HALF), BF),
             pltpu.VMEM((MISC, HALF), BF),
             pltpu.SemaphoreType.DMA((SIDE + 1,)),
             pltpu.SemaphoreType.DMA((SIDE * (SIDE + 1),)),

time: 117 us -> 116 us (level)
  no operation moved by 1% of the time
where the time goes in v7:
time: 116 us
  starting transfers between devices  45.3 us (39%)
  Pallas kernels  27.9 us (24%)
  blocking collectives  24 us (21%)
  waiting for transfers between devices  15.7 us (14%)
  local copies, waits for them, and re-layouts  1.93 us (2%)
    all_to_all x1, blocking collectives, exchange(): lax.all_to_all(value, EVERY, 0, 0, tiled=True, axis_index_groups=groups)  24 us
    all_to_all x3, starting transfers between devices, exchange(): lax.all_to_all(value, EVERY, 0, 0, tiled=True, axis_index_groups=groups)  17.8 us
    ppermute x4, starting transfers between devices, on_device(): lax.ppermute(start, EVERY, state_shift(partitions, k))  16.8 us
    ppermute x3, starting transfers between devices, on_device(): lates[k] = lax.ppermute(lates[k], EVERY, line_shift(partitions, k))  10.7 us
    pallas_call x1, Pallas kernels, on_device(): pl.pallas_call(block_kernel, out_shape=outputs, in_specs=[slow] * 8, out_...  9.79 us
    all_to_all x3, waiting for transfers between devices, exchange(): lax.all_to_all(value, EVERY, 0, 0, tiled=True, axis_index_groups=groups)  9.66 us
    pallas_call x1, Pallas kernels, on_device(): pl.pallas_call(trace_kernel, out_shape=jax.ShapeDtypeStruct((partitions /...  7.1 us
    ppermute x4, waiting for transfers between devices, on_device(): lax.ppermute(start, EVERY, state_shift(partitions, k))  6.04 us
  transfers between devices with their start and end apart: 10, of which 3 were waited for; matrix products, arithmetic and copies ran while one was open for 1% of the time, Pallas kernels for 19%

profile of v7, /device:TPU:1, one launch (start us, length us, event | category | flops | bytes accessed | tf_op | source)
XLA Modules:
  0.0 115.7 jit_solution(18159473519975923807)
XLA Ops:
  0.6 2.5 %shard_map.102 = (bf16[4,512,512]{2,1,0:T(8,128)(2,1)}, bf16[64,1536]{1,0:T(8,128)(2,1)}) custom-call(bf16[2,64,1024]{2,1,0:T(8,128)(2,1)} %low.1, bf16[2,64,512]{2,1,0:T(8,128)(2,1)} %arrow_ref.3, bf16[2,64,1024]{2,1,0:T(8,128)(2,1)} %x_ref.3, bf16[1,64,1024]{2,1,0:T(8,128)(2,1)} %sigma.1, bf16[1,64,512]{2,1,0:T(8,128)(2,1)} %tip.1), custom_call_target="tpu_custom_call" | custom-call | bytes 4000000 | tf_op jit(solution)/shard_map/pallas_call | solution.py:572
  3.1 0.0 copy-start.3
  3.1 5.2 %all-to-all-start = ((bf16[4,512,512]{2,1,0:T(8,128)(2,1)}), bf16[4,512,512]{2,1,0:T(8,128)(2,1)}, u32[]{:S(2)}, u32[]{:S(2)}) async-start(bf16[4,512,512]{2,1,0:T(8,128)(2,1)} %get-tuple-element.13), calls=%async_computation | async-start | bytes 4194304 | tf_op jit(solution)/shard_map/all_to_all | solution.py:80
  8.3 11.1 %collective-permute-start.3 = (bf16[64,1536]{1,0:T(8,128)(2,1)S(1)}, bf16[64,1536]{1,0:T(8,128)(2,1)S(1)}, u32[]{:S(2)}, u32[]{:S(2)}) collective-permute-start(bf16[64,1536]{1,0:T(8,128)(2,1)S(1)} %copy-done.3), channel_id=1, source_target_pairs={{16,3},{17,0},{18,1},{19,2},{20,7},{21,4},{22,5},{23,6},{24,11},{2... | collective-permute-start | bytes 589832 | tf_op jit(solution)/shard_map/ppermute | solution.py:591
  19.3 1.9 %collective-permute-start.2 = (bf16[64,1536]{1,0:T(8,128)(2,1)S(1)}, bf16[64,1536]{1,0:T(8,128)(2,1)S(1)}, u32[]{:S(2)}, u32[]{:S(2)}) collective-permute-start(bf16[64,1536]{1,0:T(8,128)(2,1)S(1)} %copy-done.3), channel_id=1, source_target_pairs={{16,2},{17,3},{18,0},{19,1},{20,6},{21,7},{22,4},{23,5},{24,10},{2... | collective-permute-start | bytes 589832 | tf_op jit(solution)/shard_map/ppermute | solution.py:591
  21.3 1.9 %collective-permute-start.1 = (bf16[64,1536]{1,0:T(8,128)(2,1)S(1)}, bf16[64,1536]{1,0:T(8,128)(2,1)}, u32[]{:S(2)}, u32[]{:S(2)}) collective-permute-start(bf16[64,1536]{1,0:T(8,128)(2,1)S(1)} %copy-done.3), channel_id=1, source_target_pairs={{16,1},{17,2},{18,3},{19,0},{20,5},{21,6},{22,7},{23,4},{24,9},{25... | collective-permute-start | bytes 589832 | tf_op jit(solution)/shard_map/ppermute | solution.py:591
  23.2 1.9 %collective-permute-start = (bf16[64,1536]{1,0:T(8,128)(2,1)S(1)}, bf16[64,1536]{1,0:T(8,128)(2,1)}, u32[]{:S(2)}, u32[]{:S(2)}) collective-permute-start(bf16[64,1536]{1,0:T(8,128)(2,1)S(1)} %copy-done.3), channel_id=1, source_target_pairs={{16,0},{17,1},{18,2},{19,3},{20,4},{21,5},{22,6},{23,7},{24,8},{25... | collective-permute-start | bytes 589832 | tf_op jit(solution)/shard_map/ppermute | solution.py:591
  25.1 0.0 copy-start
  25.2 4.0 %collective-permute-done.2.own2 = bf16[64,1536]{1,0:T(8,128)(2,1)S(1)} collective-permute-done((bf16[64,1536]{1,0:T(8,128)(2,1)S(1)}, bf16[64,1536]{1,0:T(8,128)(2,1)S(1)}, u32[]{:S(2)}, u32[]{:S(2)}) %collective-permute-start.2) | collective-permute-done | bytes 196640 | tf_op jit(solution)/shard_map/ppermute | solution.py:591
  29.2 2.0 %collective-permute-done.1.own1 = bf16[64,1536]{1,0:T(8,128)(2,1)} collective-permute-done((bf16[64,1536]{1,0:T(8,128)(2,1)S(1)}, bf16[64,1536]{1,0:T(8,128)(2,1)}, u32[]{:S(2)}, u32[]{:S(2)}) %collective-permute-start.1) | collective-permute-done | bytes 196640 | tf_op jit(solution)/shard_map/ppermute | solution.py:591
  31.2 3.8 %shard_map.103 = bf16[4,976,512]{2,1,0:T(8,128)(2,1)} custom-call(bf16[4,512,512]{2,1,0:T(8,128)(2,1)} %all-to-all-done.got.panel_ref, bf16[2,64,512]{2,1,0:T(8,128)(2,1)} %arrow_ref.3, f32[2,64]{1,0:T(2,128)} %weight.1, bf16[64,1536]{1,0:T(8,128)(2,1)} %collective-permute-done.own0, bf16[64,1536]{1,0:T(8,128)(2,1)} %collective-permute-done.1.own1, ...), custom_call_target="tpu_custom_call" | custom-call | bytes 12000000 | tf_op jit(solution)/shard_map/pallas_call | solution.py:592
  35.0 4.8 %all-to-all-start.1 = ((bf16[4,976,512]{2,1,0:T(8,128)(2,1)}), bf16[4,976,512]{2,1,0:T(8,128)(2,1)}, u32[]{:S(2)}, u32[]{:S(2)}) async-start(bf16[4,976,512]{2,1,0:T(8,128)(2,1)} %shard_map.103), calls=%async_computation.1 | async-start | bytes 7995392 | tf_op jit(solution)/shard_map/all_to_all | solution.py:80
  39.8 4.8 %shard_map.104 = (bf16[1664,512]{1,0:T(8,128)(2,1)}, bf16[1664,512]{1,0:T(8,128)(2,1)}, bf16[1664,512]{1,0:T(8,128)(2,1)}, bf16[1664,512]{1,0:T(8,128)(2,1)}) custom-call(bf16[4,512,512]{2,1,0:T(8,128)(2,1)} %all-to-all-done.got.panel_ref, bf16[64,1536]{1,0:T(8,128)(2,1)} %collective-permute-done.own0, bf16[64,1536]{1,0:T(8,128)(2,1)} %collective-permute-done.1.own1, ...), custom_call_target="tpu_custom_call" | custom-call | bytes 12000000 | tf_op jit(solution)/shard_map/pallas_call | solution.py:606
  44.6 3.4 %collective-permute-start.4 = (bf16[1664,512]{1,0:T(8,128)(2,1)}, bf16[1664,512]{1,0:T(8,128)(2,1)}, u32[]{:S(2)}, u32[]{:S(2)}) collective-permute-start(bf16[1664,512]{1,0:T(8,128)(2,1)} %get-tuple-element.16), channel_id=1, source_target_pairs={{0,4},{1,5},{2,6},{3,7},{4,8},{5,9},{6,10},{7,11},{8,12},{9,13},{1... | collective-permute-start | bytes 5111816 | tf_op jit(solution)/shard_map/ppermute | solution.py:625
  48.1 4.2 %collective-permute-start.5 = (bf16[1664,512]{1,0:T(8,128)(2,1)}, bf16[1664,512]{1,0:T(8,128)(2,1)}, u32[]{:S(2)}, u32[]{:S(2)}) collective-permute-start(bf16[1664,512]{1,0:T(8,128)(2,1)} %get-tuple-element.17), channel_id=1, source_target_pairs={{0,8},{1,9},{2,10},{3,11},{4,12},{5,13},{6,14},{7,15},{8,0},{9,1},... | collective-permute-start | bytes 5111816 | tf_op jit(solution)/shard_map/ppermute | solution.py:625
  52.3 3.1 %collective-permute-start.6 = (bf16[1664,512]{1,0:T(8,128)(2,1)}, bf16[1664,512]{1,0:T(8,128)(2,1)}, u32[]{:S(2)}, u32[]{:S(2)}) collective-permute-start(bf16[1664,512]{1,0:T(8,128)(2,1)} %get-tuple-element.18), channel_id=1, source_target_pairs={{0,12},{1,13},{2,14},{3,15},{4,0},{5,1},{6,2},{7,3},{8,4},{9,5},{1... | collective-permute-start | bytes 5111816 | tf_op jit(solution)/shard_map/ppermute | solution.py:625
  55.4 0.7 copy.12.weight_ref
  56.1 9.7 %all-to-all-done.1.got = bf16[4,976,512]{2,1,0:T(8,128)(2,1)} async-done(((bf16[4,976,512]{2,1,0:T(8,128)(2,1)}), bf16[4,976,512]{2,1,0:T(8,128)(2,1)}, u32[]{:S(2)}, u32[]{:S(2)}) %all-to-all-start.1) | async-done | bytes 3997728 | tf_op jit(solution)/shard_map/all_to_all | solution.py:80
  65.8 7.1 %shard_map.106 = f32[16,8,128]{2,1,0:T(8,128)} custom-call(bf16[4,976,512]{2,1,0:T(8,128)(2,1)} %all-to-all-done.1.got, bf16[1664,512]{1,0:T(8,128)(2,1)} %get-tuple-element.15.late0.begun, bf16[4,512,512]{2,1,0:T(8,128)(2,1)} %all-to-all-done.got.panel_ref, bf16[2,64,512]{2,1,0:T(8,128)(2,1)} %arrow_ref.3, bf16[2,64,1024]{2,1,0:T(8,128)(2,1)} %x_ref.3, ...), custom_call_target="tpu_custom_call" | custom-call | bytes 20000000 | tf_op jit(solution)/shard_map/pallas_call | solution.py:626
  72.9 24.0 %all_to_all.20 = f32[16,8,128]{2,1,0:T(8,128)S(1)} all-to-all(f32[16,8,128]{2,1,0:T(8,128)} %shard_map.106), channel_id=1, replica_groups={{0,32,64,96,128,160,192,224,256,288,320,352,384,416,448,480},{1,33,65,9..., dimensions={0} | all-to-all | bytes 131072 | tf_op jit(solution)/shard_map/all_to_all | solution.py:80
  96.9 0.7 broadcast_in_dim.10
  97.5 7.8 %all-to-all-start.3 = ((f32[32,8,128]{2,1,0:T(8,128)}), f32[32,8,128]{2,1,0:T(8,128)S(1)}, u32[]{:S(2)}, u32[]{:S(2)}) async-start(f32[32,8,128]{2,1,0:T(8,128)} %broadcast_in_dim.10), calls=%async_computation.3 | async-start | bytes 262144 | tf_op jit(solution)/shard_map/all_to_all | solution.py:80
  105.3 9.8 %shard_map.105 = (f32[2,64,1024]{2,1,0:T(8,128)}, f32[2,64,1024]{2,1,0:T(8,128)}, f32[2,64,512]{2,1,0:T(8,128)}) custom-call(bf16[4,976,512]{2,1,0:T(8,128)(2,1)} %all-to-all-done.1.got, bf16[1664,512]{1,0:T(8,128)(2,1)} %get-tuple-element.15.late0.begun, bf16[1664,512]{1,0:T(8,128)(2,1)} %collective-permute-done.4.late1, ...), custom_call_target="tpu_custom_call" | custom-call | bytes 30000000 | tf_op jit(solution)/shard_map/pallas_call | solution.py:653
  115.2 0.5 slice.3
  (15 shorter events, 0.1 us)
Async XLA Ops:
  3.1 5.2 %copy-start.3 = (bf16[64,1536]{1,0:T(8,128)(2,1)S(1)}, bf16[64,1536]{1,0:T(8,128)(2,1)}, u32[]{:S(2)}) copy-start(bf16[64,1536]{1,0:T(8,128)(2,1)} %get-tuple-element.14) | copy-start | bytes 589828
  3.1 28.1 %all-to-all-start = ((bf16[4,512,512]{2,1,0:T(8,128)(2,1)}), bf16[4,512,512]{2,1,0:T(8,128)(2,1)}, u32[]{:S(2)}, u32[]{:S(2)}) async-start(bf16[4,512,512]{2,1,0:T(8,128)(2,1)} %get-tuple-element.13), calls=%async_computation | async-start | bytes 4194304 | tf_op jit(solution)/shard_map/all_to_all | solution.py:80
  8.3 16.9 %collective-permute-start.3 = (bf16[64,1536]{1,0:T(8,128)(2,1)S(1)}, bf16[64,1536]{1,0:T(8,128)(2,1)S(1)}, u32[]{:S(2)}, u32[]{:S(2)}) collective-permute-start(bf16[64,1536]{1,0:T(8,128)(2,1)S(1)} %copy-done.3), channel_id=1, source_target_pairs={{16,3},{17,0},{18,1},{19,2},{20,7},{21,4},{22,5},{23,6},{24,11},{2... | collective-permute-start | bytes 589832 | tf_op jit(solution)/shard_map/ppermute | solution.py:591
  19.3 9.9 %collective-permute-start.2 = (bf16[64,1536]{1,0:T(8,128)(2,1)S(1)}, bf16[64,1536]{1,0:T(8,128)(2,1)S(1)}, u32[]{:S(2)}, u32[]{:S(2)}) collective-permute-start(bf16[64,1536]{1,0:T(8,128)(2,1)S(1)} %copy-done.3), channel_id=1, source_target_pairs={{16,2},{17,3},{18,0},{19,1},{20,6},{21,7},{22,4},{23,5},{24,10},{2... | collective-permute-start | bytes 589832 | tf_op jit(solution)/shard_map/ppermute | solution.py:591
  21.3 9.9 %collective-permute-start.1 = (bf16[64,1536]{1,0:T(8,128)(2,1)S(1)}, bf16[64,1536]{1,0:T(8,128)(2,1)}, u32[]{:S(2)}, u32[]{:S(2)}) collective-permute-start(bf16[64,1536]{1,0:T(8,128)(2,1)S(1)} %copy-done.3), channel_id=1, source_target_pairs={{16,1},{17,2},{18,3},{19,0},{20,5},{21,6},{22,7},{23,4},{24,9},{25... | collective-permute-start | bytes 589832 | tf_op jit(solution)/shard_map/ppermute | solution.py:591
  23.2 8.0 %collective-permute-start = (bf16[64,1536]{1,0:T(8,128)(2,1)S(1)}, bf16[64,1536]{1,0:T(8,128)(2,1)}, u32[]{:S(2)}, u32[]{:S(2)}) collective-permute-start(bf16[64,1536]{1,0:T(8,128)(2,1)S(1)} %copy-done.3), channel_id=1, source_target_pairs={{16,0},{17,1},{18,2},{19,3},{20,4},{21,5},{22,6},{23,7},{24,8},{25... | collective-permute-start | bytes 589832 | tf_op jit(solution)/shard_map/ppermute | solution.py:591
  25.1 6.1 %copy-start = (bf16[64,1536]{1,0:T(8,128)(2,1)}, bf16[64,1536]{1,0:T(8,128)(2,1)S(1)}, u32[]{:S(2)}) copy-start(bf16[64,1536]{1,0:T(8,128)(2,1)S(1)} %collective-permute-done.3.own3) | copy-start | bytes 589828
  29.2 2.0 %copy-start.1 = (bf16[64,1536]{1,0:T(8,128)(2,1)}, bf16[64,1536]{1,0:T(8,128)(2,1)S(1)}, u32[]{:S(2)}) copy-start(bf16[64,1536]{1,0:T(8,128)(2,1)S(1)} %collective-permute-done.2.own2) | copy-start | bytes 589828
  35.0 30.8 %all-to-all-start.1 = ((bf16[4,976,512]{2,1,0:T(8,128)(2,1)}), bf16[4,976,512]{2,1,0:T(8,128)(2,1)}, u32[]{:S(2)}, u32[]{:S(2)}) async-start(bf16[4,976,512]{2,1,0:T(8,128)(2,1)} %shard_map.103), calls=%async_computation.1 | async-start | bytes 7995392 | tf_op jit(solution)/shard_map/all_to_all | solution.py:80
  39.8 15.5 %copy-start.2 = (f32[2,64]{1,0:T(2,128)S(1)}, f32[2,64]{1,0:T(2,128)}, u32[]{:S(2)}) copy-start(f32[2,64]{1,0:T(2,128)} %weight.1) | copy-start | bytes 1540
  44.6 60.7 %collective-permute-start.4 = (bf16[1664,512]{1,0:T(8,128)(2,1)}, bf16[1664,512]{1,0:T(8,128)(2,1)}, u32[]{:S(2)}, u32[]{:S(2)}) collective-permute-start(bf16[1664,512]{1,0:T(8,128)(2,1)} %get-tuple-element.16), channel_id=1, source_target_pairs={{0,4},{1,5},{2,6},{3,7},{4,8},{5,9},{6,10},{7,11},{8,12},{9,13},{1... | collective-permute-start | bytes 5111816 | tf_op jit(solution)/shard_map/ppermute | solution.py:625
  48.1 57.3 %collective-permute-start.5 = (bf16[1664,512]{1,0:T(8,128)(2,1)}, bf16[1664,512]{1,0:T(8,128)(2,1)}, u32[]{:S(2)}, u32[]{:S(2)}) collective-permute-start(bf16[1664,512]{1,0:T(8,128)(2,1)} %get-tuple-element.17), channel_id=1, source_target_pairs={{0,8},{1,9},{2,10},{3,11},{4,12},{5,13},{6,14},{7,15},{8,0},{9,1},... | collective-permute-start | bytes 5111816 | tf_op jit(solution)/shard_map/ppermute | solution.py:625
  52.3 53.1 %collective-permute-start.6 = (bf16[1664,512]{1,0:T(8,128)(2,1)}, bf16[1664,512]{1,0:T(8,128)(2,1)}, u32[]{:S(2)}, u32[]{:S(2)}) collective-permute-start(bf16[1664,512]{1,0:T(8,128)(2,1)} %get-tuple-element.18), channel_id=1, source_target_pairs={{0,12},{1,13},{2,14},{3,15},{4,0},{5,1},{6,2},{7,3},{8,4},{9,5},{1... | collective-permute-start | bytes 5111816 | tf_op jit(solution)/shard_map/ppermute | solution.py:625
  97.5 17.6 %all-to-all-start.3 = ((f32[32,8,128]{2,1,0:T(8,128)}), f32[32,8,128]{2,1,0:T(8,128)S(1)}, u32[]{:S(2)}, u32[]{:S(2)}) async-start(f32[32,8,128]{2,1,0:T(8,128)} %broadcast_in_dim.10), calls=%async_computation.3 | async-start | bytes 262144 | tf_op jit(solution)/shard_map/all_to_all | solution.py:80

commit v8 on v7

--- a/solution.py
+++ b/solution.py
@@ -347,6 +347,7 @@
 ):
     core, row, first = place()
     second = jnp.where(core == 0, lax.axis_index("y"), lax.axis_index("x"))
+    near = pl.ds(pl.multiple_of(lax.div(row, 2) * 128, 128), 128)
     load_misc = pltpu.make_async_copy(got.at[:, pl.ds(PANEL, MISC)], misc, sem_in.at[0])
     load_factor = load_exchanged(got, factor, sem_factor)
     later = [
@@ -356,7 +357,7 @@
         ),
         pltpu.make_async_copy(arrow_ref, arrow, sem_in.at[3]),
         pltpu.make_async_copy(q_ref, q, sem_in.at[4]),
-        pltpu.make_async_copy(x_ref, x, sem_in.at[5]),
+        pltpu.make_async_copy(x_ref.at[:, :, near], x, sem_in.at[5]),
     ]
     for copy in [load_misc] + load_factor + later:
         copy.start()
@@ -382,8 +383,9 @@
     for copy in load_factor:
         copy.wait()
     have = Gathered(factor)
-    u, u_tip = have.past(z0)
-    u_tip = u_tip - z0_tip.astype(F32)
+    whole = jnp.concatenate([have.piece(0), have.piece(1)], axis=1)
+    u = dot_t(z0, whole)
+    u_tip = have.over_rows(z0, 2) - z0_tip.astype(F32)
     u_mine = jnp.zeros((256, 256), F32)
     z1_mine = []
     for h in range(2):
@@ -414,8 +416,8 @@
         own_tip = jnp.where(second == d, u_tip[d * ROWS : (d + 1) * ROWS], own_tip)
     both = jnp.concatenate([own_tip.astype(BF), arrow[1]], axis=0)
     tip_traced = both.astype(F32) * dot(both, q[...])
-    at = lax.broadcasted_iota(jnp.int32, (ROWS, BLOCK), 0) + row * ROWS
-    on_diagonal = lax.broadcasted_iota(jnp.int32, (ROWS, BLOCK), 1) == at
+    at = lax.broadcasted_iota(jnp.int32, (ROWS, 128), 0) + lax.rem(row, 2) * ROWS
+    on_diagonal = lax.broadcasted_iota(jnp.int32, (ROWS, 128), 1) == at
     total = sum_all(traced)
     for block in range(2):
         total += sum_all(tip_traced[block * ROWS : (block + 1) * ROWS] * weight_ref[block])
@@ -634,7 +636,7 @@
             pltpu.VMEM((PANEL, HALF), BF),
             pltpu.VMEM((SIDE, 2 * ROWS, HALF), BF),
             pltpu.VMEM((2, ROWS, HALF), BF),
-            pltpu.VMEM((2, ROWS, BLOCK), BF),
+            pltpu.VMEM((2, ROWS, 128), BF),
             pltpu.VMEM((HALF, HALF), BF),
             pltpu.SemaphoreType.DMA((16,)),
             pltpu.SemaphoreType.DMA((6,)),

time: 116 us -> 116 us (level)
  no operation moved by 1% of the time
where the time goes in v8:
time: 116 us
  starting transfers between devices  45.3 us (39%)
  Pallas kernels  27.8 us (24%)
  blocking collectives  24 us (21%)
  waiting for transfers between devices  15.7 us (14%)
  local copies, waits for them, and re-layouts  1.93 us (2%)
    all_to_all x1, blocking collectives, exchange(): lax.all_to_all(value, EVERY, 0, 0, tiled=True, axis_index_groups=groups)  24 us
    all_to_all x3, starting transfers between devices, exchange(): lax.all_to_all(value, EVERY, 0, 0, tiled=True, axis_index_groups=groups)  17.8 us
    ppermute x4, starting transfers between devices, on_device(): lax.ppermute(start, EVERY, state_shift(partitions, k))  16.8 us
    ppermute x3, starting transfers between devices, on_device(): lates[k] = lax.ppermute(lates[k], EVERY, line_shift(partitions, k))  10.7 us
    pallas_call x1, Pallas kernels, on_device(): pl.pallas_call(block_kernel, out_shape=outputs, in_specs=[slow] * 8, out_...  9.79 us
    all_to_all x3, waiting for transfers between devices, exchange(): lax.all_to_all(value, EVERY, 0, 0, tiled=True, axis_index_groups=groups)  9.66 us
    pallas_call x1, Pallas kernels, on_device(): pl.pallas_call(trace_kernel, out_shape=jax.ShapeDtypeStruct((partitions /...  7.02 us
    ppermute x4, waiting for transfers between devices, on_device(): lax.ppermute(start, EVERY, state_shift(partitions, k))  6.04 us
  transfers between devices with their start and end apart: 10, of which 3 were waited for; matrix products, arithmetic and copies ran while one was open for 1% of the time, Pallas kernels for 19%

profile of v8, /device:TPU:1, one launch (start us, length us, event | category | flops | bytes accessed | tf_op | source)
XLA Modules:
  0.0 115.6 jit_solution(2353797065974255462)
XLA Ops:
  0.6 2.5 %shard_map.102 = (bf16[4,512,512]{2,1,0:T(8,128)(2,1)}, bf16[64,1536]{1,0:T(8,128)(2,1)}) custom-call(bf16[2,64,1024]{2,1,0:T(8,128)(2,1)} %low.1, bf16[2,64,512]{2,1,0:T(8,128)(2,1)} %arrow_ref.3, bf16[2,64,1024]{2,1,0:T(8,128)(2,1)} %x_ref.3, bf16[1,64,1024]{2,1,0:T(8,128)(2,1)} %sigma.1, bf16[1,64,512]{2,1,0:T(8,128)(2,1)} %tip.1), custom_call_target="tpu_custom_call" | custom-call | bytes 4000000 | tf_op jit(solution)/shard_map/pallas_call | solution.py:574
  3.1 5.2 %all-to-all-start = ((bf16[4,512,512]{2,1,0:T(8,128)(2,1)}), bf16[4,512,512]{2,1,0:T(8,128)(2,1)}, u32[]{:S(2)}, u32[]{:S(2)}) async-start(bf16[4,512,512]{2,1,0:T(8,128)(2,1)} %get-tuple-element.13), calls=%async_computation | async-start | bytes 4194304 | tf_op jit(solution)/shard_map/all_to_all | solution.py:80
  8.3 11.1 %collective-permute-start.3 = (bf16[64,1536]{1,0:T(8,128)(2,1)S(1)}, bf16[64,1536]{1,0:T(8,128)(2,1)S(1)}, u32[]{:S(2)}, u32[]{:S(2)}) collective-permute-start(bf16[64,1536]{1,0:T(8,128)(2,1)S(1)} %copy-done.3), channel_id=1, source_target_pairs={{16,3},{17,0},{18,1},{19,2},{20,7},{21,4},{22,5},{23,6},{24,11},{2... | collective-permute-start | bytes 589832 | tf_op jit(solution)/shard_map/ppermute | solution.py:593
  19.3 1.9 %collective-permute-start.2 = (bf16[64,1536]{1,0:T(8,128)(2,1)S(1)}, bf16[64,1536]{1,0:T(8,128)(2,1)S(1)}, u32[]{:S(2)}, u32[]{:S(2)}) collective-permute-start(bf16[64,1536]{1,0:T(8,128)(2,1)S(1)} %copy-done.3), channel_id=1, source_target_pairs={{16,2},{17,3},{18,0},{19,1},{20,6},{21,7},{22,4},{23,5},{24,10},{2... | collective-permute-start | bytes 589832 | tf_op jit(solution)/shard_map/ppermute | solution.py:593
  21.3 1.9 %collective-permute-start.1 = (bf16[64,1536]{1,0:T(8,128)(2,1)S(1)}, bf16[64,1536]{1,0:T(8,128)(2,1)}, u32[]{:S(2)}, u32[]{:S(2)}) collective-permute-start(bf16[64,1536]{1,0:T(8,128)(2,1)S(1)} %copy-done.3), channel_id=1, source_target_pairs={{16,1},{17,2},{18,3},{19,0},{20,5},{21,6},{22,7},{23,4},{24,9},{25... | collective-permute-start | bytes 589832 | tf_op jit(solution)/shard_map/ppermute | solution.py:593
  23.2 1.9 %collective-permute-start = (bf16[64,1536]{1,0:T(8,128)(2,1)S(1)}, bf16[64,1536]{1,0:T(8,128)(2,1)}, u32[]{:S(2)}, u32[]{:S(2)}) collective-permute-start(bf16[64,1536]{1,0:T(8,128)(2,1)S(1)} %copy-done.3), channel_id=1, source_target_pairs={{16,0},{17,1},{18,2},{19,3},{20,4},{21,5},{22,6},{23,7},{24,8},{25... | collective-permute-start | bytes 589832 | tf_op jit(solution)/shard_map/ppermute | solution.py:593
  25.1 0.0 copy-start
  25.2 4.0 %collective-permute-done.2.own2 = bf16[64,1536]{1,0:T(8,128)(2,1)S(1)} collective-permute-done((bf16[64,1536]{1,0:T(8,128)(2,1)S(1)}, bf16[64,1536]{1,0:T(8,128)(2,1)S(1)}, u32[]{:S(2)}, u32[]{:S(2)}) %collective-permute-start.2) | collective-permute-done | bytes 196640 | tf_op jit(solution)/shard_map/ppermute | solution.py:593
  29.2 2.0 %collective-permute-done.1.own1 = bf16[64,1536]{1,0:T(8,128)(2,1)} collective-permute-done((bf16[64,1536]{1,0:T(8,128)(2,1)S(1)}, bf16[64,1536]{1,0:T(8,128)(2,1)}, u32[]{:S(2)}, u32[]{:S(2)}) %collective-permute-start.1) | collective-permute-done | bytes 196640 | tf_op jit(solution)/shard_map/ppermute | solution.py:593
  31.2 3.8 %shard_map.103 = bf16[4,976,512]{2,1,0:T(8,128)(2,1)} custom-call(bf16[4,512,512]{2,1,0:T(8,128)(2,1)} %all-to-all-done.got.panel_ref, bf16[2,64,512]{2,1,0:T(8,128)(2,1)} %arrow_ref.3, f32[2,64]{1,0:T(2,128)} %weight.1, bf16[64,1536]{1,0:T(8,128)(2,1)} %collective-permute-done.own0, bf16[64,1536]{1,0:T(8,128)(2,1)} %collective-permute-done.1.own1, ...), custom_call_target="tpu_custom_call" | custom-call | bytes 12000000 | tf_op jit(solution)/shard_map/pallas_call | solution.py:594
  35.0 4.8 %all-to-all-start.1 = ((bf16[4,976,512]{2,1,0:T(8,128)(2,1)}), bf16[4,976,512]{2,1,0:T(8,128)(2,1)}, u32[]{:S(2)}, u32[]{:S(2)}) async-start(bf16[4,976,512]{2,1,0:T(8,128)(2,1)} %shard_map.103), calls=%async_computation.1 | async-start | bytes 7995392 | tf_op jit(solution)/shard_map/all_to_all | solution.py:80
  39.8 0.0 copy-start.2
  39.8 4.8 %shard_map.104 = (bf16[1664,512]{1,0:T(8,128)(2,1)}, bf16[1664,512]{1,0:T(8,128)(2,1)}, bf16[1664,512]{1,0:T(8,128)(2,1)}, bf16[1664,512]{1,0:T(8,128)(2,1)}) custom-call(bf16[4,512,512]{2,1,0:T(8,128)(2,1)} %all-to-all-done.got.panel_ref, bf16[64,1536]{1,0:T(8,128)(2,1)} %collective-permute-done.own0, bf16[64,1536]{1,0:T(8,128)(2,1)} %collective-permute-done.1.own1, ...), custom_call_target="tpu_custom_call" | custom-call | bytes 12000000 | tf_op jit(solution)/shard_map/pallas_call | solution.py:608
  44.6 3.4 %collective-permute-start.4 = (bf16[1664,512]{1,0:T(8,128)(2,1)}, bf16[1664,512]{1,0:T(8,128)(2,1)}, u32[]{:S(2)}, u32[]{:S(2)}) collective-permute-start(bf16[1664,512]{1,0:T(8,128)(2,1)} %get-tuple-element.16), channel_id=1, source_target_pairs={{0,4},{1,5},{2,6},{3,7},{4,8},{5,9},{6,10},{7,11},{8,12},{9,13},{1... | collective-permute-start | bytes 5111816 | tf_op jit(solution)/shard_map/ppermute | solution.py:627
  48.1 4.2 %collective-permute-start.5 = (bf16[1664,512]{1,0:T(8,128)(2,1)}, bf16[1664,512]{1,0:T(8,128)(2,1)}, u32[]{:S(2)}, u32[]{:S(2)}) collective-permute-start(bf16[1664,512]{1,0:T(8,128)(2,1)} %get-tuple-element.17), channel_id=1, source_target_pairs={{0,8},{1,9},{2,10},{3,11},{4,12},{5,13},{6,14},{7,15},{8,0},{9,1},... | collective-permute-start | bytes 5111816 | tf_op jit(solution)/shard_map/ppermute | solution.py:627
  52.3 3.1 %collective-permute-start.6 = (bf16[1664,512]{1,0:T(8,128)(2,1)}, bf16[1664,512]{1,0:T(8,128)(2,1)}, u32[]{:S(2)}, u32[]{:S(2)}) collective-permute-start(bf16[1664,512]{1,0:T(8,128)(2,1)} %get-tuple-element.18), channel_id=1, source_target_pairs={{0,12},{1,13},{2,14},{3,15},{4,0},{5,1},{6,2},{7,3},{8,4},{9,5},{1... | collective-permute-start | bytes 5111816 | tf_op jit(solution)/shard_map/ppermute | solution.py:627
  55.4 0.7 copy.12.weight_ref
  56.1 9.7 %all-to-all-done.1.got = bf16[4,976,512]{2,1,0:T(8,128)(2,1)} async-done(((bf16[4,976,512]{2,1,0:T(8,128)(2,1)}), bf16[4,976,512]{2,1,0:T(8,128)(2,1)}, u32[]{:S(2)}, u32[]{:S(2)}) %all-to-all-start.1) | async-done | bytes 3997728 | tf_op jit(solution)/shard_map/all_to_all | solution.py:80
  65.8 7.0 %shard_map.106 = f32[16,8,128]{2,1,0:T(8,128)} custom-call(bf16[4,976,512]{2,1,0:T(8,128)(2,1)} %all-to-all-done.1.got, bf16[1664,512]{1,0:T(8,128)(2,1)} %get-tuple-element.15.late0.begun, bf16[4,512,512]{2,1,0:T(8,128)(2,1)} %all-to-all-done.got.panel_ref, bf16[2,64,512]{2,1,0:T(8,128)(2,1)} %arrow_ref.3, bf16[2,64,1024]{2,1,0:T(8,128)(2,1)} %x_ref.3, ...), custom_call_target="tpu_custom_call" | custom-call | bytes 20000000 | tf_op jit(solution)/shard_map/pallas_call | solution.py:628
  72.8 24.0 %all_to_all.20 = f32[16,8,128]{2,1,0:T(8,128)S(1)} all-to-all(f32[16,8,128]{2,1,0:T(8,128)} %shard_map.106), channel_id=1, replica_groups={{0,32,64,96,128,160,192,224,256,288,320,352,384,416,448,480},{1,33,65,9..., dimensions={0} | all-to-all | bytes 131072 | tf_op jit(solution)/shard_map/all_to_all | solution.py:80
  96.8 0.7 broadcast_in_dim.10
  97.4 7.8 %all-to-all-start.3 = ((f32[32,8,128]{2,1,0:T(8,128)}), f32[32,8,128]{2,1,0:T(8,128)S(1)}, u32[]{:S(2)}, u32[]{:S(2)}) async-start(f32[32,8,128]{2,1,0:T(8,128)} %broadcast_in_dim.10), calls=%async_computation.3 | async-start | bytes 262144 | tf_op jit(solution)/shard_map/all_to_all | solution.py:80
  105.3 9.8 %shard_map.105 = (f32[2,64,1024]{2,1,0:T(8,128)}, f32[2,64,1024]{2,1,0:T(8,128)}, f32[2,64,512]{2,1,0:T(8,128)}) custom-call(bf16[4,976,512]{2,1,0:T(8,128)(2,1)} %all-to-all-done.1.got, bf16[1664,512]{1,0:T(8,128)(2,1)} %get-tuple-element.15.late0.begun, bf16[1664,512]{1,0:T(8,128)(2,1)} %collective-permute-done.4.late1, ...), custom_call_target="tpu_custom_call" | custom-call | bytes 30000000 | tf_op jit(solution)/shard_map/pallas_call | solution.py:655
  115.1 0.5 slice.3
  (15 shorter events, 0.1 us)
Async XLA Ops:
  3.1 5.2 %copy-start.3 = (bf16[64,1536]{1,0:T(8,128)(2,1)S(1)}, bf16[64,1536]{1,0:T(8,128)(2,1)}, u32[]{:S(2)}) copy-start(bf16[64,1536]{1,0:T(8,128)(2,1)} %get-tuple-element.14) | copy-start | bytes 589828
  3.1 28.1 %all-to-all-start = ((bf16[4,512,512]{2,1,0:T(8,128)(2,1)}), bf16[4,512,512]{2,1,0:T(8,128)(2,1)}, u32[]{:S(2)}, u32[]{:S(2)}) async-start(bf16[4,512,512]{2,1,0:T(8,128)(2,1)} %get-tuple-element.13), calls=%async_computation | async-start | bytes 4194304 | tf_op jit(solution)/shard_map/all_to_all | solution.py:80
  8.3 16.9 %collective-permute-start.3 = (bf16[64,1536]{1,0:T(8,128)(2,1)S(1)}, bf16[64,1536]{1,0:T(8,128)(2,1)S(1)}, u32[]{:S(2)}, u32[]{:S(2)}) collective-permute-start(bf16[64,1536]{1,0:T(8,128)(2,1)S(1)} %copy-done.3), channel_id=1, source_target_pairs={{16,3},{17,0},{18,1},{19,2},{20,7},{21,4},{22,5},{23,6},{24,11},{2... | collective-permute-start | bytes 589832 | tf_op jit(solution)/shard_map/ppermute | solution.py:593
  19.3 9.9 %collective-permute-start.2 = (bf16[64,1536]{1,0:T(8,128)(2,1)S(1)}, bf16[64,1536]{1,0:T(8,128)(2,1)S(1)}, u32[]{:S(2)}, u32[]{:S(2)}) collective-permute-start(bf16[64,1536]{1,0:T(8,128)(2,1)S(1)} %copy-done.3), channel_id=1, source_target_pairs={{16,2},{17,3},{18,0},{19,1},{20,6},{21,7},{22,4},{23,5},{24,10},{2... | collective-permute-start | bytes 589832 | tf_op jit(solution)/shard_map/ppermute | solution.py:593
  21.3 9.9 %collective-permute-start.1 = (bf16[64,1536]{1,0:T(8,128)(2,1)S(1)}, bf16[64,1536]{1,0:T(8,128)(2,1)}, u32[]{:S(2)}, u32[]{:S(2)}) collective-permute-start(bf16[64,1536]{1,0:T(8,128)(2,1)S(1)} %copy-done.3), channel_id=1, source_target_pairs={{16,1},{17,2},{18,3},{19,0},{20,5},{21,6},{22,7},{23,4},{24,9},{25... | collective-permute-start | bytes 589832 | tf_op jit(solution)/shard_map/ppermute | solution.py:593
  23.2 8.0 %collective-permute-start = (bf16[64,1536]{1,0:T(8,128)(2,1)S(1)}, bf16[64,1536]{1,0:T(8,128)(2,1)}, u32[]{:S(2)}, u32[]{:S(2)}) collective-permute-start(bf16[64,1536]{1,0:T(8,128)(2,1)S(1)} %copy-done.3), channel_id=1, source_target_pairs={{16,0},{17,1},{18,2},{19,3},{20,4},{21,5},{22,6},{23,7},{24,8},{25... | collective-permute-start | bytes 589832 | tf_op jit(solution)/shard_map/ppermute | solution.py:593
  25.1 6.1 %copy-start = (bf16[64,1536]{1,0:T(8,128)(2,1)}, bf16[64,1536]{1,0:T(8,128)(2,1)S(1)}, u32[]{:S(2)}) copy-start(bf16[64,1536]{1,0:T(8,128)(2,1)S(1)} %collective-permute-done.3.own3) | copy-start | bytes 589828
  29.2 2.0 %copy-start.1 = (bf16[64,1536]{1,0:T(8,128)(2,1)}, bf16[64,1536]{1,0:T(8,128)(2,1)S(1)}, u32[]{:S(2)}) copy-start(bf16[64,1536]{1,0:T(8,128)(2,1)S(1)} %collective-permute-done.2.own2) | copy-start | bytes 589828
  35.0 30.8 %all-to-all-start.1 = ((bf16[4,976,512]{2,1,0:T(8,128)(2,1)}), bf16[4,976,512]{2,1,0:T(8,128)(2,1)}, u32[]{:S(2)}, u32[]{:S(2)}) async-start(bf16[4,976,512]{2,1,0:T(8,128)(2,1)} %shard_map.103), calls=%async_computation.1 | async-start | bytes 7995392 | tf_op jit(solution)/shard_map/all_to_all | solution.py:80
  39.8 15.5 %copy-start.2 = (f32[2,64]{1,0:T(2,128)S(1)}, f32[2,64]{1,0:T(2,128)}, u32[]{:S(2)}) copy-start(f32[2,64]{1,0:T(2,128)} %weight.1) | copy-start | bytes 1540
  44.6 60.6 %collective-permute-start.4 = (bf16[1664,512]{1,0:T(8,128)(2,1)}, bf16[1664,512]{1,0:T(8,128)(2,1)}, u32[]{:S(2)}, u32[]{:S(2)}) collective-permute-start(bf16[1664,512]{1,0:T(8,128)(2,1)} %get-tuple-element.16), channel_id=1, source_target_pairs={{0,4},{1,5},{2,6},{3,7},{4,8},{5,9},{6,10},{7,11},{8,12},{9,13},{1... | collective-permute-start | bytes 5111816 | tf_op jit(solution)/shard_map/ppermute | solution.py:627
  48.1 57.2 %collective-permute-start.5 = (bf16[1664,512]{1,0:T(8,128)(2,1)}, bf16[1664,512]{1,0:T(8,128)(2,1)}, u32[]{:S(2)}, u32[]{:S(2)}) collective-permute-start(bf16[1664,512]{1,0:T(8,128)(2,1)} %get-tuple-element.17), channel_id=1, source_target_pairs={{0,8},{1,9},{2,10},{3,11},{4,12},{5,13},{6,14},{7,15},{8,0},{9,1},... | collective-permute-start | bytes 5111816 | tf_op jit(solution)/shard_map/ppermute | solution.py:627
  52.3 53.0 %collective-permute-start.6 = (bf16[1664,512]{1,0:T(8,128)(2,1)}, bf16[1664,512]{1,0:T(8,128)(2,1)}, u32[]{:S(2)}, u32[]{:S(2)}) collective-permute-start(bf16[1664,512]{1,0:T(8,128)(2,1)} %get-tuple-element.18), channel_id=1, source_target_pairs={{0,12},{1,13},{2,14},{3,15},{4,0},{5,1},{6,2},{7,3},{8,4},{9,5},{1... | collective-permute-start | bytes 5111816 | tf_op jit(solution)/shard_map/ppermute | solution.py:627
  97.4 17.6 %all-to-all-start.3 = ((f32[32,8,128]{2,1,0:T(8,128)}), f32[32,8,128]{2,1,0:T(8,128)S(1)}, u32[]{:S(2)}, u32[]{:S(2)}) async-start(f32[32,8,128]{2,1,0:T(8,128)} %broadcast_in_dim.10), calls=%async_computation.3 | async-start | bytes 262144 | tf_op jit(solution)/shard_map/all_to_all | solution.py:80
